TPU v7x, 32 devices: a whole 2x2x4 slice. The times are simulated.
32 devices in a mesh: section: 4 (over y, x), dp: 4 (over z), tensor: 2 (over core).
Axes of the slice: x: 2, y: 2, z: 4, core: 2. Of those that a mesh axis runs over, the one named last changes fastest.
Arguments:
- inputs: bfloat16 [4, 4096, 1024], P('section', 'dp'), may hold values from -6 to 6
- lengths: int32 [4, 4], P('dp'), may hold values from 1 to 512, 1024 in all within a row
- gain_attn: float32 [4, 1024], P('section'), may hold values from 0.25 to 1.75
- w_query: bfloat16 [4, 1024, 1024], P('section', None, 'tensor'), may hold values from -0.1875 to 0.1875
- w_key: bfloat16 [4, 1024, 1024], P('section', None, 'tensor'), may hold values from -0.1875 to 0.1875
- w_value: bfloat16 [4, 1024, 1024], P('section', None, 'tensor'), may hold values from -0.1875 to 0.1875
- w_out: bfloat16 [4, 1024, 1024], P('section', 'tensor'), may hold values from -1.5 to 1.5
- gain_ffn: float32 [4, 1024], P('section'), may hold values from 0.25 to 1.75
- w_gate: bfloat16 [4, 1024, 2816], P('section', None, 'tensor'), may hold values from -0.1875 to 0.1875
- w_up: bfloat16 [4, 1024, 2816], P('section', None, 'tensor'), may hold values from -0.1875 to 0.1875
- w_down: bfloat16 [4, 2816, 1024], P('section', 'tensor'), may hold values from -0.15625 to 0.15625
- cotangent: bfloat16 [4, 4096, 1024], P('section', 'dp'), may hold values from -6 to 6
Outputs:
- result: bfloat16 [4, 4096, 1024], P('section', 'dp')
- grad_input: float32 [4, 4096, 1024], P('section', 'dp')
- grad_gain_attn: float32 [4, 1024], P('section')
- grad_w_query: float32 [4, 1024, 1024], P('section', None, 'tensor')
- grad_w_key: float32 [4, 1024, 1024], P('section', None, 'tensor')
- grad_w_value: float32 [4, 1024, 1024], P('section', None, 'tensor')
- grad_w_out: float32 [4, 1024, 1024], P('section', 'tensor')
- grad_gain_ffn: float32 [4, 1024], P('section')
- grad_w_gate: float32 [4, 1024, 2816], P('section', None, 'tensor')
- grad_w_up: float32 [4, 1024, 2816], P('section', None, 'tensor')
- grad_w_down: float32 [4, 2816, 1024], P('section', 'tensor')
Inputs may be any that keep to these rules, and one draw needn't show every extreme that they name: Each row gives the lengths of the 4 sequences of one data group, in order; they sum to 1024, and the longest of every row has exactly 512 tokens.
All inputs are finite; a program needn't handle non-finite values.
Results may differ from a plain program's by a relative error of at most 0.02.
Values may be sent and summed in bfloat16 or wider, within the bound.
No kernel may reach another device: no remote copies, remote signals or barrier semaphores. Data moves between devices by JAX's collectives and lax.ppermute only.
A program may use at most 192 MiB of HBM per device.

v0:
```python
import jax
import jax.numpy as jnp
from jax import lax
from jax.sharding import PartitionSpec as P

HD = 64


EPSILON = 1e-06
MASKED = -1e30


def spread(block, axis, holder):
    block = jnp.where(lax.axis_index(axis) == holder, block, jnp.zeros_like(block))
    return lax.psum(block, axis)


def matmul(left, right):
    return jnp.dot(left, right, preferred_element_type=jnp.float32)


def matmul_nt(left, right):
    return lax.dot_general(
        left, right, (((1,), (1,)), ((), ())), preferred_element_type=jnp.float32
    )


def matmul_tn(left, right):
    return lax.dot_general(
        left, right, (((0,), (0,)), ((), ())), preferred_element_type=jnp.float32
    )


def layout(lengths_row, tokens, head_dim):
    seq_ends = jnp.cumsum(lengths_row)
    seq_starts = seq_ends - lengths_row
    places = jnp.arange(tokens, dtype=jnp.int32)
    segment = jnp.sum((places[:, None] >= seq_ends[None, :]).astype(jnp.int32), axis=1)
    seq_slots = jnp.arange(lengths_row.shape[0], dtype=jnp.int32)
    seq_first = jnp.sum(
        jnp.where(segment[:, None] == seq_slots[None, :], seq_starts[None, :], 0), axis=1
    )
    position = (places - seq_first).astype(jnp.float32)
    inv_freq = 10000.0 ** (-(jnp.arange(head_dim // 2, dtype=jnp.float32) * 2.0 / head_dim))
    angles = position[:, None] * inv_freq[None, :]
    rot_cos = jnp.concatenate([jnp.cos(angles), jnp.cos(angles)], axis=1)[:, None, :]
    rot_sin = jnp.concatenate([jnp.sin(angles), jnp.sin(angles)], axis=1)[:, None, :]
    return (segment, rot_cos, rot_sin)


def turn(values, rot_cos, rot_sin):
    half_dim = values.shape[-1] // 2
    swapped = jnp.concatenate([-values[..., half_dim:], values[..., :half_dim]], axis=-1)
    return values * rot_cos + swapped * rot_sin


def turn_back(grads, rot_cos, rot_sin):
    half_dim = grads.shape[-1] // 2
    scaled = grads * rot_sin
    swapped = jnp.concatenate([scaled[..., half_dim:], -scaled[..., :half_dim]], axis=-1)
    return grads * rot_cos + swapped


def norm_back(grad_normed, values, inv_rms, gain):
    weighted = grad_normed * gain
    inner = jnp.mean(weighted * values, axis=1, keepdims=True)
    grad_values = inv_rms * weighted - values * (inv_rms * inv_rms * inv_rms) * inner
    return (grad_values, jnp.sum(grad_normed * values * inv_rms, axis=0))


def block_scores(queries, keys_rot, segment, row_start, block_rows):
    q_block = lax.dynamic_slice_in_dim(queries, row_start, block_rows, 0)
    seg_block = lax.dynamic_slice_in_dim(segment, row_start, block_rows, 0)
    row_pos = row_start + jnp.arange(block_rows, dtype=jnp.int32)
    col_pos = jnp.arange(keys_rot.shape[0], dtype=jnp.int32)
    scores = jnp.einsum(
        "qhd,khd->hqk", q_block, keys_rot, preferred_element_type=jnp.float32
    ) * HD ** (-0.5)
    allowed = (seg_block[:, None] == segment[None, :]) & (col_pos[None, :] <= row_pos[:, None])
    return (q_block, jnp.where(allowed[None], scores, MASKED))


def attend_forward(queries, keys_rot, mixed, segment):
    tokens = queries.shape[0]
    block_rows = min(512, tokens)

    def one_block(block_idx):
        row_start = block_idx * block_rows
        q_block, scores = block_scores(queries, keys_rot, segment, row_start, block_rows)
        row_max = jnp.max(scores, axis=-1, keepdims=True)
        exps = jnp.exp(scores - row_max)
        row_total = jnp.sum(exps, axis=-1, keepdims=True)
        probs = (exps / row_total).astype(jnp.bfloat16)
        outputs = jnp.einsum("hqk,khd->qhd", probs, mixed, preferred_element_type=jnp.float32)
        return (outputs, (row_max + jnp.log(row_total))[..., 0])

    outputs, log_totals = lax.map(one_block, jnp.arange(tokens // block_rows, dtype=jnp.int32))
    return (outputs.reshape(queries.shape), log_totals)


def attend_back(queries, keys_rot, mixed, segment, log_totals, grad_heads):
    tokens = queries.shape[0]
    block_rows = min(512, tokens)
    scale = HD ** (-0.5)

    def one_block(carry, block_idx):
        key_acc, value_acc = carry
        row_start = block_idx * block_rows
        q_block, scores = block_scores(queries, keys_rot, segment, row_start, block_rows)
        probs_full = jnp.exp(scores - log_totals[block_idx][..., None])
        probs = probs_full.astype(jnp.bfloat16)
        grad_block = lax.dynamic_slice_in_dim(grad_heads, row_start, block_rows, 0)
        grad_probs = jnp.einsum(
            "qhd,khd->hqk", grad_block, mixed, preferred_element_type=jnp.float32
        )
        row_dot = jnp.sum(probs_full * grad_probs, axis=-1, keepdims=True)
        grad_scores = (probs_full * (grad_probs - row_dot)).astype(jnp.bfloat16)
        grad_query = (
            jnp.einsum("hqk,khd->qhd", grad_scores, keys_rot, preferred_element_type=jnp.float32)
            * scale
        )
        key_acc = (
            key_acc
            + jnp.einsum("hqk,qhd->khd", grad_scores, q_block, preferred_element_type=jnp.float32)
            * scale
        )
        value_acc = value_acc + jnp.einsum(
            "hqk,qhd->khd", probs, grad_block, preferred_element_type=jnp.float32
        )
        return ((key_acc, value_acc), grad_query)

    zeros = jnp.zeros(keys_rot.shape, jnp.float32)
    (grad_key, grad_value), grad_query = lax.scan(
        one_block, (zeros, zeros), jnp.arange(tokens // block_rows, dtype=jnp.int32)
    )
    return (grad_query.reshape(queries.shape), grad_key, grad_value)


def shards(
    inputs,
    lengths,
    gain_attn,
    w_query,
    w_key,
    w_value,
    w_out,
    gain_ffn,
    w_gate,
    w_up,
    w_down,
    cotangent,
):
    stream = inputs[0].astype(jnp.float32)
    tokens = stream.shape[0]
    segment, rot_cos, rot_sin = layout(lengths[0], tokens, HD)
    n_heads = w_query.shape[2] // HD
    head_shape = (tokens, n_heads, HD)
    section_idx = lax.axis_index("section")
    gain_one = gain_attn[0]
    gain_two = gain_ffn[0]

    def front(values):
        inv_rms_attn = lax.rsqrt(jnp.mean(values * values, axis=1, keepdims=True) + EPSILON)
        normed = (values * inv_rms_attn * gain_one).astype(jnp.bfloat16)
        queries = turn(matmul(normed, w_query[0]).reshape(head_shape), rot_cos, rot_sin).astype(
            jnp.bfloat16
        )
        keys_rot = turn(matmul(normed, w_key[0]).reshape(head_shape), rot_cos, rot_sin).astype(
            jnp.bfloat16
        )
        value_own = matmul(normed, w_value[0])
        return (inv_rms_attn, normed, queries, keys_rot, value_own)

    def blend(value_own, value_first):
        return (
            (0.5 * value_own + 0.5 * value_first.astype(jnp.float32))
            .astype(jnp.bfloat16)
            .reshape(head_shape)
        )

    def after(middle):
        inv_rms_ffn = lax.rsqrt(jnp.mean(middle * middle, axis=1, keepdims=True) + EPSILON)
        normed_ffn = (middle * inv_rms_ffn * gain_two).astype(jnp.bfloat16)
        gate_proj = matmul(normed_ffn, w_gate[0])
        up_proj = matmul(normed_ffn, w_up[0])
        hidden = (jax.nn.silu(gate_proj) * up_proj).astype(jnp.bfloat16)
        return (inv_rms_ffn, normed_ffn, gate_proj, up_proj, hidden)

    front_vals = front(stream)
    value_first = spread(front_vals[4].astype(jnp.bfloat16), "section", 0)
    mixed = blend(front_vals[4], value_first)
    outputs, log_totals = attend_forward(front_vals[2], front_vals[3], mixed, segment)
    heads_out = outputs.reshape(tokens, -1).astype(jnp.bfloat16)
    middle = stream + lax.psum(matmul(heads_out, w_out[0]).astype(jnp.bfloat16), "tensor").astype(
        jnp.float32
    )
    after_vals = after(middle)
    result = middle + lax.psum(
        matmul(after_vals[4], w_down[0]).astype(jnp.bfloat16), "tensor"
    ).astype(jnp.float32)
    again_front = front(stream)
    again_mixed = blend(again_front[4], value_first)
    again_out, again_totals = attend_forward(again_front[2], again_front[3], again_mixed, segment)
    again_heads = again_out.reshape(tokens, -1).astype(jnp.bfloat16)
    again_middle = stream + lax.psum(
        matmul(again_heads, w_out[0]).astype(jnp.bfloat16), "tensor"
    ).astype(jnp.float32)
    kept = (again_front, again_mixed, again_totals, again_heads, again_middle, after(again_middle))
    (
        (inv_rms_attn, normed, queries, keys_rot, value_own),
        mixed,
        log_totals,
        heads_out,
        middle,
        (inv_rms_ffn, normed_ffn, gate_proj, up_proj, hidden),
    ) = kept
    grad_out = cotangent[0]
    grad_hidden = matmul_nt(grad_out, w_down[0])
    gate_sig = jax.nn.sigmoid(gate_proj)
    grad_gate = (grad_hidden * up_proj * gate_sig * (1.0 + gate_proj * (1.0 - gate_sig))).astype(
        jnp.bfloat16
    )
    grad_up = (grad_hidden * gate_proj * gate_sig).astype(jnp.bfloat16)
    grad_w_down = matmul_tn(hidden, grad_out)
    grad_w_gate = matmul_tn(normed_ffn, grad_gate)
    grad_w_up = matmul_tn(normed_ffn, grad_up)
    grad_normed_ffn = lax.psum(
        (matmul_nt(grad_gate, w_gate[0]) + matmul_nt(grad_up, w_up[0])).astype(jnp.bfloat16),
        "tensor",
    ).astype(jnp.float32)
    grad_mid_norm, grad_gain_two = norm_back(grad_normed_ffn, middle, inv_rms_ffn, gain_two)
    grad_middle = grad_out.astype(jnp.float32) + grad_mid_norm
    ffn_full = ()
    grad_attn = grad_middle.astype(jnp.bfloat16)
    grad_w_out = matmul_tn(heads_out, grad_attn)
    grad_heads = matmul_nt(grad_attn, w_out[0]).astype(jnp.bfloat16).reshape(head_shape)
    grad_query, grad_key, grad_mixed = attend_back(
        queries, keys_rot, mixed, segment, log_totals, grad_heads
    )
    grad_query_lin = (
        turn_back(grad_query, rot_cos, rot_sin).reshape(tokens, -1).astype(jnp.bfloat16)
    )
    grad_key_lin = turn_back(grad_key, rot_cos, rot_sin).reshape(tokens, -1).astype(jnp.bfloat16)
    half_mixed = 0.5 * grad_mixed.reshape(tokens, -1)
    first_total = lax.psum(half_mixed.astype(jnp.bfloat16), "section").astype(jnp.float32)
    grad_value_lin = (half_mixed + jnp.where(section_idx == 0, first_total, 0.0)).astype(
        jnp.bfloat16
    )
    grad_w_query = matmul_tn(normed, grad_query_lin)
    grad_w_key = matmul_tn(normed, grad_key_lin)
    grad_w_value = matmul_tn(normed, grad_value_lin)
    grad_normed_part = (
        matmul_nt(grad_query_lin, w_query[0])
        + matmul_nt(grad_key_lin, w_key[0])
        + matmul_nt(grad_value_lin, w_value[0])
    )
    grad_normed = lax.psum(grad_normed_part.astype(jnp.bfloat16), "tensor").astype(jnp.float32)
    grad_in_norm, grad_gain_one = norm_back(grad_normed, stream, inv_rms_attn, gain_one)
    grad_input = grad_middle + grad_in_norm
    all_summed = (
        lax.psum_scatter(
            grad_w_query.astype(jnp.bfloat16), "dp", scatter_dimension=0, tiled=True
        ).astype(jnp.float32),
        lax.psum_scatter(
            grad_w_key.astype(jnp.bfloat16), "dp", scatter_dimension=0, tiled=True
        ).astype(jnp.float32),
        lax.psum_scatter(
            grad_w_value.astype(jnp.bfloat16), "dp", scatter_dimension=0, tiled=True
        ).astype(jnp.float32),
        lax.psum_scatter(
            grad_w_out.astype(jnp.bfloat16), "dp", scatter_dimension=0, tiled=True
        ).astype(jnp.float32),
        lax.psum_scatter(
            grad_gain_one[:, None].astype(jnp.bfloat16), "dp", scatter_dimension=0, tiled=True
        ).astype(jnp.float32),
        lax.psum_scatter(
            grad_w_gate.astype(jnp.bfloat16), "dp", scatter_dimension=0, tiled=True
        ).astype(jnp.float32),
        lax.psum_scatter(
            grad_w_up.astype(jnp.bfloat16), "dp", scatter_dimension=0, tiled=True
        ).astype(jnp.float32),
        lax.psum_scatter(
            grad_w_down.astype(jnp.bfloat16), "dp", scatter_dimension=0, tiled=True
        ).astype(jnp.float32),
        lax.psum_scatter(
            grad_gain_two[:, None].astype(jnp.bfloat16), "dp", scatter_dimension=0, tiled=True
        ).astype(jnp.float32),
    )
    all_full = (
        lax.all_gather(all_summed[0].astype(jnp.bfloat16), "dp", axis=0, tiled=True).astype(
            jnp.float32
        ),
        lax.all_gather(all_summed[1].astype(jnp.bfloat16), "dp", axis=0, tiled=True).astype(
            jnp.float32
        ),
        lax.all_gather(all_summed[2].astype(jnp.bfloat16), "dp", axis=0, tiled=True).astype(
            jnp.float32
        ),
        lax.all_gather(all_summed[3].astype(jnp.bfloat16), "dp", axis=0, tiled=True).astype(
            jnp.float32
        ),
        lax.all_gather(all_summed[4].astype(jnp.bfloat16), "dp", axis=0, tiled=True).astype(
            jnp.float32
        ),
        lax.all_gather(all_summed[5].astype(jnp.bfloat16), "dp", axis=0, tiled=True).astype(
            jnp.float32
        ),
        lax.all_gather(all_summed[6].astype(jnp.bfloat16), "dp", axis=0, tiled=True).astype(
            jnp.float32
        ),
        lax.all_gather(all_summed[7].astype(jnp.bfloat16), "dp", axis=0, tiled=True).astype(
            jnp.float32
        ),
        lax.all_gather(all_summed[8].astype(jnp.bfloat16), "dp", axis=0, tiled=True).astype(
            jnp.float32
        ),
    )
    attn_full = all_full[:5]
    ffn_full = all_full[5:]
    return (
        result.astype(jnp.bfloat16)[None],
        grad_input[None],
        attn_full[4][:, 0][None],
        attn_full[0][None],
        attn_full[1][None],
        attn_full[2][None],
        attn_full[3][None],
        ffn_full[3][:, 0][None],
        ffn_full[0][None],
        ffn_full[1][None],
        ffn_full[2][None],
    )


def solution(mesh):
    return jax.shard_map(
        shards,
        mesh=mesh,
        in_specs=(
            P("section", "dp", None),
            P("dp", None),
            P("section", None),
            P("section", None, "tensor"),
            P("section", None, "tensor"),
            P("section", None, "tensor"),
            P("section", "tensor", None),
            P("section", None),
            P("section", None, "tensor"),
            P("section", None, "tensor"),
            P("section", "tensor", None),
            P("section", "dp", None),
        ),
        out_specs=(
            P("section", "dp", None),
            P("section", "dp", None),
            P("section", None),
            P("section", None, "tensor"),
            P("section", None, "tensor"),
            P("section", None, "tensor"),
            P("section", "tensor", None),
            P("section", None),
            P("section", None, "tensor"),
            P("section", None, "tensor"),
            P("section", "tensor", None),
        ),
        check_vma=False,
    )
```

profile of v0, /device:TPU:0, one launch (start us, length us, event | category | flops | bytes accessed | tf_op | source)
XLA Modules:
  0.0 1170.6 jit_solution(9902456607402080255)
XLA Ops:
  38.2 32.3 %all-reduce.8.cloned.1.call-done = bf16[1024,512]{0,1:T(8,128)(2,1)} async-done(((bf16[1024,512]{0,1:T(8,128)(2,1)}), bf16[1024,512]{0,1:T(8,128)(2,1)}) %all-reduce.8.cloned.1.call-update) | async-done | bytes 1048592 | tf_op jit(solution)/shard_map/psum | solution.py:15
  74.8 35.1 %while.38 = (s32[]{:T(128)}, bf16[2,512,8,64]{1,3,2,0:T(8,128)(2,1)}, f32[2,8,512]{2,1,0:T(8,128)S(1)}, s32[2]{0:T(128)S(1)}, s32[1024]{0:T(1024)S(1)}, /*index=...) while((s32[]{:T(128)}, ...), condition=%wide.region_15.16_spmd, body=%wide.region_12.15_spmd.sunk | while | flops 1125642752 | bytes 68827416 | solution.py:97
  117.3 96.0 %while.37 = (s32[]{:T(128)}, bf16[2,512,8,64]{1,3,2,0:T(8,128)(2,1)}, s32[2]{0:T(128)S(1)}, s32[1024]{0:T(1024)S(1)}, bf16[1024,8,64]{0,2,1:T(8,128)(2,1)}, /*in...) while((s32[]{:T(128)}, ...), condition=%wide.region_8.9_spmd, body=%wide.region_5.8_spmd.sunk | while | flops 1108870656 | bytes 71874752 | solution.py:97
  128.9 21.8 %fusion.204 = (f32[8,512]{1,0:T(8,128)S(1)}, f32[8,512,1024]{2,1,0:T(8,128)}) fusion(f32[8,512,1024]{2,1,0:T(8,128)} %fusion.202, pred[512,1024]{1,0:T(8,128)(4,1)S(1)} %fusion.203), kind=kOutput, calls=%fused_computation.207.clone.1 | output fusion | flops 25166848 | bytes 34095104 | tf_op jit(solution)/shard_map/while/body/eval_jaxpr/sub | solution.py:91
  171.7 21.8 %fusion.204 = (f32[8,512]{1,0:T(8,128)S(1)}, f32[8,512,1024]{2,1,0:T(8,128)}) fusion(f32[8,512,1024]{2,1,0:T(8,128)} %fusion.202, pred[512,1024]{1,0:T(8,128)(4,1)S(1)} %fusion.203), kind=kOutput, calls=%fused_computation.207.clone.1 | output fusion | flops 25166848 | bytes 34095104 | tf_op jit(solution)/shard_map/while/body/eval_jaxpr/sub | solution.py:91
  242.3 28.9 %all-reduce.16.cloned.1.call-done = (bf16[1024,1024]{1,0:T(8,128)(2,1)}, bf16[1024,1024]{1,0:T(8,128)(2,1)}) async-done(((bf16[1024,1024]{1,0:T(8,128)(2,1)}, bf16[1024,1024]{1,0:T(8,128)(2,1)}), (bf16[1024,1024]{1,0:T(8,128)(2,1)}, bf16[1024,1024]{1,0:T(8,128)(2,1)})) %all-reduce.16.cloned.1.call-update) | async-done | bytes 4194320 | tf_op jit(solution)/shard_map/psum | solution.py:194
  281.9 159.2 %while.39 = (s32[]{:T(128)}, f32[1024,8,64]{0,2,1:T(8,128)}, f32[1024,8,64]{0,2,1:T(8,128)}, f32[2,512,8,64]{1,0,3,2:T(2,128)}, s32[2]{0:T(128)S(1)}, /*index=5*...) while((s32[]{:T(128)}, f32[1024,8,64]{0,2,1:T(8,128)}, ...), condition=%wide.region_22.23_spmd.clone, body=%wide.region_20.22_spmd.clone.sunk | while | flops 2726556160 | bytes 292649504 | solution.py:133
  341.9 19.6 %dynamic_update_slice.25 = f32[2,512,8,64]{1,0,3,2:T(2,128)} dynamic-update-slice(f32[2,512,8,64]{1,0,3,2:T(2,128)} %get-tuple-element.549, f32[1,512,8,64]{1,0,3,2:T(1,128)} %copy.57, s32[]{:T(128)S(6)} %copy.85, s32[]{:T(128)} %constant.68.clone.1..sunk.2, s32[]{:T(128)} %constant.68.clone.1..sunk.2, s32[]{:T(128)} %constant.68.clone.1..sunk.2) | dynamic-update-slice | bytes 2097156 | tf_op jit(solution)/shard_map/while/body/jit(dynamic_update_index_in_dim)/dynamic_update_slice | solution.py:97
  421.2 19.6 %dynamic_update_slice.25 = f32[2,512,8,64]{1,0,3,2:T(2,128)} dynamic-update-slice(f32[2,512,8,64]{1,0,3,2:T(2,128)} %get-tuple-element.549, f32[1,512,8,64]{1,0,3,2:T(1,128)} %copy.57, s32[]{:T(128)S(6)} %copy.85, s32[]{:T(128)} %constant.68.clone.1..sunk.2, s32[]{:T(128)} %constant.68.clone.1..sunk.2, s32[]{:T(128)} %constant.68.clone.1..sunk.2) | dynamic-update-slice | bytes 2097156 | tf_op jit(solution)/shard_map/while/body/jit(dynamic_update_index_in_dim)/dynamic_update_slice | solution.py:97
  483.7 15.4 %all-reduce.12.cloned.1.call-done = bf16[1024,512]{0,1:T(8,128)(2,1)} async-done(((bf16[1024,512]{0,1:T(8,128)(2,1)}), bf16[1024,512]{0,1:T(8,128)(2,1)}) %all-reduce.12.cloned.1.call-update) | async-done | bytes 1048592 | tf_op jit(solution)/shard_map/psum | solution.py:245
  557.2 28.1 %reduce-scatter.16.cloned.1.call-done = bf16[256,512]{1,0:T(8,128)(2,1)} async-done(((bf16[1024,512]{1,0:T(8,128)(2,1)}), bf16[256,512]{1,0:T(8,128)(2,1)}) %reduce-scatter.16.cloned.1.call-update) | async-done | bytes 262160 | tf_op jit(solution)/shard_map/reduce_scatter | solution.py:264
  585.3 28.7 %reduce-scatter.18.cloned.1.call-done = bf16[256,512]{1,0:T(8,128)(2,1)} async-done(((bf16[1024,512]{1,0:T(8,128)(2,1)}), bf16[256,512]{1,0:T(8,128)(2,1)}) %reduce-scatter.18.cloned.1.call-update) | async-done | bytes 262160 | tf_op jit(solution)/shard_map/reduce_scatter | solution.py:267
  614.1 30.3 %all-reduce.14.cloned.1.call-done = (bf16[1024,1024]{1,0:T(8,128)(2,1)}, bf16[1024,1024]{1,0:T(8,128)(2,1)}) async-done(((bf16[1024,1024]{1,0:T(8,128)(2,1)}, bf16[1024,1024]{1,0:T(8,128)(2,1)}), (bf16[1024,1024]{1,0:T(8,128)(2,1)}, bf16[1024,1024]{1,0:T(8,128)(2,1)})) %all-reduce.14.cloned.1.call-update) | async-done | bytes 4194320 | tf_op jit(solution)/shard_map/psum | solution.py:198
  649.2 54.8 %reduce-scatter.26.cloned.1.call-done = bf16[352,1024]{1,0:T(8,128)(2,1)} async-done(((bf16[1408,1024]{1,0:T(8,128)(2,1)}), bf16[352,1024]{1,0:T(8,128)(2,1)}) %reduce-scatter.26.cloned.1.call-update) | async-done | bytes 720912 | tf_op jit(solution)/shard_map/reduce_scatter | solution.py:282
  704.1 59.0 %reduce-scatter.24.cloned.1.call-done = bf16[256,1408]{1,0:T(8,128)(2,1)} async-done(((bf16[1024,1408]{1,0:T(8,128)(2,1)}), bf16[256,1408]{1,0:T(8,128)(2,1)}) %reduce-scatter.24.cloned.1.call-update) | async-done | bytes 720912 | tf_op jit(solution)/shard_map/reduce_scatter | solution.py:279
  763.1 58.8 %reduce-scatter.22.cloned.1.call-done = bf16[256,1408]{1,0:T(8,128)(2,1)} async-done(((bf16[1024,1408]{1,0:T(8,128)(2,1)}), bf16[256,1408]{1,0:T(8,128)(2,1)}) %reduce-scatter.22.cloned.1.call-update) | async-done | bytes 720912 | tf_op jit(solution)/shard_map/reduce_scatter | solution.py:276
  822.0 22.4 %reduce-scatter.30.cloned.1.call-done = bf16[256,1]{1,0:T(8,128)(2,1)} async-done(((bf16[1024,1]{1,0:T(8,128)(2,1)}), bf16[256,1]{1,0:T(8,128)(2,1)}) %reduce-scatter.30.cloned.1.call-update) | async-done | bytes 528
  853.9 18.1 %all-gather.14.cloned.1.call-done = bf16[512,1024]{1,0:T(8,128)(2,1)} async-done(((bf16[128,1024]{1,0:T(8,128)(2,1)}), bf16[512,1024]{1,0:T(8,128)(2,1)}) %all-gather.14.cloned.1.call-update) | async-done | bytes 1048592 | tf_op jit(solution)/shard_map/all_gather | solution.py:299
  874.8 26.1 %all-gather.8.cloned.1.call-done = bf16[1024,512]{1,0:T(8,128)(2,1)} async-done(((bf16[256,512]{1,0:T(8,128)(2,1)}), bf16[1024,512]{1,0:T(8,128)(2,1)}) %all-gather.8.cloned.1.call-update) | async-done | bytes 1048592 | tf_op jit(solution)/shard_map/all_gather | solution.py:290
  903.8 26.0 %all-gather.10.cloned.1.call-done = bf16[1024,512]{1,0:T(8,128)(2,1)} async-done(((bf16[256,512]{1,0:T(8,128)(2,1)}), bf16[1024,512]{1,0:T(8,128)(2,1)}) %all-gather.10.cloned.1.call-update) | async-done | bytes 1048592 | tf_op jit(solution)/shard_map/all_gather | solution.py:293
  932.6 26.0 %all-gather.12.cloned.1.call-done = bf16[1024,512]{1,0:T(8,128)(2,1)} async-done(((bf16[256,512]{1,0:T(8,128)(2,1)}), bf16[1024,512]{1,0:T(8,128)(2,1)}) %all-gather.12.cloned.1.call-update) | async-done | bytes 1048592 | tf_op jit(solution)/shard_map/all_gather | solution.py:296
  990.0 49.6 %all-gather.20.cloned.1.call-done = bf16[1408,1024]{1,0:T(8,128)(2,1)} async-done(((bf16[352,1024]{1,0:T(8,128)(2,1)}), bf16[1408,1024]{1,0:T(8,128)(2,1)}) %all-gather.20.cloned.1.call-update) | async-done | bytes 2883600 | tf_op jit(solution)/shard_map/all_gather | solution.py:311
  1044.7 54.3 %all-gather.18.cloned.1.call-done = bf16[1024,1408]{1,0:T(8,128)(2,1)} async-done(((bf16[256,1408]{1,0:T(8,128)(2,1)}), bf16[1024,1408]{1,0:T(8,128)(2,1)}) %all-gather.18.cloned.1.call-update) | async-done | bytes 2883600 | tf_op jit(solution)/shard_map/all_gather | solution.py:308
  1103.8 54.8 %all-gather.16.cloned.1.call-done = bf16[1024,1408]{1,0:T(8,128)(2,1)} async-done(((bf16[256,1408]{1,0:T(8,128)(2,1)}), bf16[1024,1408]{1,0:T(8,128)(2,1)}) %all-gather.16.cloned.1.call-update) | async-done | bytes 2883600 | tf_op jit(solution)/shard_map/all_gather | solution.py:305
  (331 shorter events, 439.4 us)
Async XLA Ops:
  7.2 220.1 %copy-start = (bf16[1,1024,1408]{2,1,0:T(8,128)(2,1)S(1)}, bf16[1,1024,1408]{2,1,0:T(8,128)(2,1)}, u32[]{:S(2)}) copy-start(bf16[1,1024,1408]{2,1,0:T(8,128)(2,1)} %param.26) | copy-start | bytes 8650756
  7.2 63.3 %all-reduce.8.cloned.1.call-start = ((), (), s32[]{:S(2)}) async-start(), calls=%async_computation.9 | async-start | bytes 2097152 | tf_op jit(solution)/shard_map/psum | solution.py:15
  15.1 203.5 %all-reduce.10.cloned.1.call-start = ((), (), s32[]{:S(2)}) async-start(), calls=%async_computation.10 | async-start | bytes 4194304 | tf_op jit(solution)/shard_map/psum | solution.py:205
  116.1 155.1 %all-reduce.16.cloned.1.call-start = ((), (), s32[]{:S(2)}) async-start(), calls=%async_computation.29 | async-start | bytes 8388608 | tf_op jit(solution)/shard_map/psum | solution.py:194
  242.3 256.9 %all-reduce.12.cloned.1.call-start = ((), (), s32[]{:S(2)}) async-start(), calls=%async_computation.11 | async-start | bytes 2097152 | tf_op jit(solution)/shard_map/psum | solution.py:245
  308.5 19.2 %copy-start.20 = (bf16[1024,8,64]{0,2,1:T(8,128)(2,1)S(1)}, bf16[1024,8,64]{0,2,1:T(8,128)(2,1)}, u32[]{:S(2)}) copy-start(bf16[1024,8,64]{0,2,1:T(8,128)(2,1)} %get-tuple-element.571) | copy-start | bytes 3145732 | tf_op jit(solution)/shard_map/while
  445.3 107.0 %reduce-scatter.20.cloned.1.call-start = ((), (), s32[]{:S(2)}) async-start(), calls=%async_computation.18 | async-start | bytes 1310720 | tf_op jit(solution)/shard_map/reduce_scatter | solution.py:270
  450.1 107.1 %reduce-scatter.14.cloned.1.call-start = ((), (), s32[]{:S(2)}) async-start(), calls=%async_computation.12 | async-start | bytes 1310720 | tf_op jit(solution)/shard_map/reduce_scatter | solution.py:261
  465.2 120.0 %reduce-scatter.16.cloned.1.call-start = ((), (), s32[]{:S(2)}) async-start(), calls=%async_computation.14 | async-start | bytes 1310720 | tf_op jit(solution)/shard_map/reduce_scatter | solution.py:264
  473.0 141.0 %reduce-scatter.18.cloned.1.call-start = ((), (), s32[]{:S(2)}) async-start(), calls=%async_computation.16 | async-start | bytes 1310720 | tf_op jit(solution)/shard_map/reduce_scatter | solution.py:267
  505.1 139.3 %all-reduce.14.cloned.1.call-start = ((), (), s32[]{:S(2)}) async-start(), calls=%async_computation.28 | async-start | bytes 8388608 | tf_op jit(solution)/shard_map/psum | solution.py:198
  525.1 178.9 %reduce-scatter.26.cloned.1.call-start = ((), (), s32[]{:S(2)}) async-start(), calls=%async_computation.24 | async-start | bytes 3604480 | tf_op jit(solution)/shard_map/reduce_scatter | solution.py:282
  535.1 228.0 %reduce-scatter.24.cloned.1.call-start = ((), (), s32[]{:S(2)}) async-start(), calls=%async_computation.22 | async-start | bytes 3604480 | tf_op jit(solution)/shard_map/reduce_scatter | solution.py:279
  543.0 279.0 %reduce-scatter.22.cloned.1.call-start = ((), (), s32[]{:S(2)}) async-start(), calls=%async_computation.20 | async-start | bytes 3604480 | tf_op jit(solution)/shard_map/reduce_scatter | solution.py:276
  550.6 293.8 %reduce-scatter.30.cloned.1.call-start = ((), (), s32[]{:S(2)}) async-start(), calls=%async_computation.27 | async-start | bytes 327680
  552.2 319.9 %all-gather.14.cloned.1.call-start = ((), (), s32[]{:S(2)}) async-start(), calls=%async_computation.19 | async-start | bytes 1310720 | tf_op jit(solution)/shard_map/all_gather | solution.py:299
  552.7 348.2 %all-gather.8.cloned.1.call-start = ((), (), s32[]{:S(2)}) async-start(), calls=%async_computation.13 | async-start | bytes 1310720 | tf_op jit(solution)/shard_map/all_gather | solution.py:290
  557.1 372.7 %all-gather.10.cloned.1.call-start = ((), (), s32[]{:S(2)}) async-start(), calls=%async_computation.15 | async-start | bytes 1310720 | tf_op jit(solution)/shard_map/all_gather | solution.py:293
  585.3 373.4 %all-gather.12.cloned.1.call-start = ((), (), s32[]{:S(2)}) async-start(), calls=%async_computation.17 | async-start | bytes 1310720 | tf_op jit(solution)/shard_map/all_gather | solution.py:296
  614.0 366.5 %reduce-scatter.28.cloned.1.call-start = ((), (), s32[]{:S(2)}) async-start(), calls=%async_computation.26 | async-start | bytes 327680
  649.2 390.5 %all-gather.20.cloned.1.call-start = ((), (), s32[]{:S(2)}) async-start(), calls=%async_computation.25 | async-start | bytes 3604480 | tf_op jit(solution)/shard_map/all_gather | solution.py:311
  704.0 395.0 %all-gather.18.cloned.1.call-start = ((), (), s32[]{:S(2)}) async-start(), calls=%async_computation.23 | async-start | bytes 3604480 | tf_op jit(solution)/shard_map/all_gather | solution.py:308
  763.1 395.5 %all-gather.16.cloned.1.call-start = ((), (), s32[]{:S(2)}) async-start(), calls=%async_computation.21 | async-start | bytes 3604480 | tf_op jit(solution)/shard_map/all_gather | solution.py:305
  903.8 57.9 %copy-start.49 = (f32[1024]{0:T(1024)S(1)}, f32[1024]{0:T(1024)}, u32[]{:S(2)}) copy-start(f32[1024]{0:T(1024)} %get-tuple-element.279) | copy-start | bytes 12292
  (71 other events, 370.1 us)
Sparse Core Ops, SparseCore 0:
  15.2 55.2 all-reduce.7
  116.3 21.2 all-reduce.9
  242.4 28.8 all-reduce.15
  445.4 53.7 all-reduce.11
  501.3 27.1 reduce-scatter.19
  531.3 25.7 reduce-scatter.13
  559.4 25.7 reduce-scatter.15
  588.2 25.7 reduce-scatter.17
  617.1 27.1 all-reduce.13
  646.6 57.3 reduce-scatter.25
  707.0 56.0 reduce-scatter.23
  765.9 56.0 reduce-scatter.21
  824.9 19.4 reduce-scatter.29
  845.8 26.2 all-gather.13
  873.5 27.4 all-gather.7
  902.3 27.4 all-gather.9
  931.2 27.4 all-gather.11
  961.4 19.1 reduce-scatter.27
  982.2 57.4 all-gather.19
  1041.1 57.8 all-gather.17
  1100.7 57.8 all-gather.15
where the time goes:
time: 1180 us; the launch traced here: 1170 us
  waiting for transfers between devices  631 us (53%)
  matrix products  242 us (21%)
  other arithmetic  156 us (13%)
  local copies, waits for them, and re-layouts  89.9 us (8%)
  loops' own time  19.3 us (2%)
  blocking collectives  16.1 us (1%)
  between operations  15.4 us (1%)
    reduce_scatter x1, waiting for transfers between devices, shards(): lax.psum_scatter(grad_w_up.astype(jnp.bfloat16), 'dp', scatter_dimension=...  59 us
    reduce_scatter x1, waiting for transfers between devices, shards(): lax.psum_scatter(grad_w_gate.astype(jnp.bfloat16), 'dp', scatter_dimensio...  58.8 us
    all_gather x1, waiting for transfers between devices, shards(): lax.all_gather(all_summed[5].astype(jnp.bfloat16), 'dp', axis=0, tiled=True)  54.8 us
    reduce_scatter x1, waiting for transfers between devices, shards(): lax.psum_scatter(grad_w_down.astype(jnp.bfloat16), 'dp', scatter_dimensio...  54.8 us
    all_gather x1, waiting for transfers between devices, shards(): lax.all_gather(all_summed[6].astype(jnp.bfloat16), 'dp', axis=0, tiled=True)  54.3 us
    dot_general x6, matrix products, block_scores(): jnp.einsum('qhd,khd->hqk', q_block, keys_rot, preferred_element_type=jnp....  54.2 us
    all_gather x1, waiting for transfers between devices, shards(): lax.all_gather(all_summed[7].astype(jnp.bfloat16), 'dp', axis=0, tiled=True)  49.6 us
    dot_general x9, matrix products, matmul(): return jnp.dot(left, right, preferred_element_type=jnp.float32)  47.1 us
  transfers between devices with their start and end apart: 21, of which 19 were waited for; matrix products, arithmetic and copies ran while one was open for 20% of the time, Pallas kernels for 0%

commit v1 on v0

v1 whole, which is shorter than its diff:
```python
import jax
import jax.numpy as jnp
from jax import lax
from jax.experimental import pallas as pl
from jax.experimental.pallas import tpu as pltpu
from jax.sharding import PartitionSpec as P

HD = 64
WINDOW = 512
EPSILON = 1e-06
MASKED = -1e30
F32 = jnp.float32
BF16 = jnp.bfloat16
MIB = 1024 * 1024
CHUNK = 256


def dot(left, right):
    return lax.dot_general(left, right, (((1,), (0,)), ((), ())), preferred_element_type=F32)


def dot_nt(left, right):
    return lax.dot_general(left, right, (((1,), (1,)), ((), ())), preferred_element_type=F32)


def dot_tn(left, right):
    return lax.dot_general(left, right, (((0,), (0,)), ((), ())), preferred_element_type=F32)


def call(kernel, grid, ins, outs, args, vmem, scratch=(), into=None):
    into = {o: array for o, array in (into or {}).items() if array is not None}
    ins, args, n = list(ins), list(args), len(args)
    body = kernel
    if into:
        ins += [pl.BlockSpec(memory_space=pl.ANY)] * len(into)
        args += list(into.values())

        def body(*refs):
            kernel(*refs[:n], *refs[n + len(into) :])

    return pl.pallas_call(
        body,
        grid=grid,
        in_specs=ins,
        out_specs=[spec for spec, _, _ in outs],
        out_shape=[jax.ShapeDtypeStruct(shape, dtype) for _, shape, dtype in outs],
        scratch_shapes=list(scratch),
        input_output_aliases={n + j: o for j, o in enumerate(into)},
        compiler_params=pltpu.CompilerParams(vmem_limit_bytes=vmem * MIB),
        cost_estimate=pl.CostEstimate(flops=1, bytes_accessed=1, transcendentals=0),
    )(*args)


def rows(block, width):
    return pl.BlockSpec((block, width), lambda i: (i, 0))


def whole(*shape):
    return pl.BlockSpec(shape, lambda i: (0,) * len(shape))


def columns(height, block, first=0):
    return pl.BlockSpec((height, block), lambda i: (0, i + first))


def value_kernel(x_ref, gain_ref, w_ref, normed_ref, *value_refs):
    x = x_ref[...].astype(F32)
    inv_rms = lax.rsqrt(jnp.mean(x * x, axis=1, keepdims=True) + EPSILON)
    normed = (x * inv_rms * gain_ref[...]).astype(BF16)
    normed_ref[...] = normed
    values = dot(normed, w_ref[...]).astype(BF16)
    cut = values.shape[1] // len(value_refs)
    for j, ref in enumerate(value_refs):
        ref[...] = values[:, j * cut : (j + 1) * cut]


def value_proj(x, gain, w_value):
    tokens, width = x.shape
    half = w_value.shape[1] // 2
    block = 256
    return call(
        value_kernel,
        (tokens // block,),
        [rows(block, width), whole(1, width), whole(width, 2 * half)],
        [(rows(block, width), (tokens, width), BF16)] + [(rows(block, half), (tokens, half), BF16)] * 2,
        (x, gain, w_value),
        60,
    )


def swap_halves(u):
    lane = lax.broadcasted_iota(jnp.int32, u.shape, 1) % HD
    return jnp.where(lane < HD // 2, pltpu.roll(u, 128 - HD // 2, 1), pltpu.roll(u, HD // 2, 1))


def query_key_kernel(n_ref, wq_ref, wk_ref, cos_ref, sin_ref, q_ref, k_ref):
    normed = n_ref[...]
    cos, sin = cos_ref[...], sin_ref[...]
    for w_ref, o_ref in ((wq_ref, q_ref), (wk_ref, k_ref)):
        u = dot(normed, w_ref[...])
        for lo in range(0, u.shape[1], 128):
            part = u[:, lo : lo + 128]
            o_ref[:, lo : lo + 128] = (part * cos + swap_halves(part) * sin).astype(BF16)


def query_key_proj(normed, w_query, w_key, cos, sin):
    tokens, width = normed.shape
    out = w_query.shape[1]
    block = 256
    return call(
        query_key_kernel,
        (tokens // block,),
        [rows(block, width), whole(width, out), whole(width, out), rows(block, 128), rows(block, 128)],
        [(rows(block, out), (tokens, out), BF16), (rows(block, out), (tokens, out), BF16)],
        (normed, w_query, w_key, cos, sin),
        32,
    )


def row_starts(len_ref, first, count):
    place = first + lax.broadcasted_iota(jnp.int32, (count, 1), 0)
    start = jnp.zeros((count, 1), jnp.int32)
    end = 0
    for j in range(len_ref.shape[1]):
        end = end + len_ref[0, j]
        start = jnp.where(place >= end, end, start)
    return place, start


def band(len_ref, first, count):
    low = max(0, first - WINDOW)
    place, start = row_starts(len_ref, first, count)
    col = low + lax.broadcasted_iota(jnp.int32, (count, first + count - low), 1)
    return low, (col >= start) & (col <= place)


def head_masks(count):
    lane = lax.broadcasted_iota(jnp.int32, (count, 2 * HD), 1)
    return lane < HD, lane >= HD


def probs_kernel(len_ref, q_ref, k_ref, probs_ref):
    tokens = q_ref.shape[0]
    block = 256
    for at in range(0, tokens, block):
        low, allowed = band(len_ref, at, block)
        queries = q_ref[at : at + block, :] * BF16(HD**-0.5)
        keys = k_ref[low : at + block, :]
        for h, mask in enumerate(head_masks(block)):
            scores = dot_nt(jnp.where(mask, queries, BF16(0)), keys)
            scores = jnp.where(allowed, scores, MASKED)
            exps = jnp.exp(scores - jnp.max(scores, axis=1, keepdims=True))
            total = jnp.sum(exps, axis=1, keepdims=True)
            probs_ref[h, at : at + block, : at + block - low] = (exps * (1.0 / total)).astype(BF16)


def band_width(tokens):
    return min(tokens, WINDOW + 256)


def probabilities(lengths, queries, keys):
    tokens, width = queries.shape
    pair = columns(tokens, 2 * HD)
    wide = band_width(tokens)
    return call(
        probs_kernel,
        (width // (2 * HD),),
        [pl.BlockSpec(memory_space=pltpu.SMEM), pair, pair],
        [(pl.BlockSpec((2, tokens, wide), lambda i: (i, 0, 0)), (width // HD, tokens, wide), BF16)],
        (lengths, queries, keys),
        40,
    )[0]


def heads_kernel(n_arrived, places, section_ref, *refs):
    probs_ref, own_refs, arrived = refs[0], refs[1:3], refs[3 : 3 + n_arrived]
    w_ref, heads_ref, mixed_ref, part_ref = refs[3 + n_arrived :]
    block = heads_ref.shape[0]
    half = own_refs[0].shape[1]
    step = pl.program_id(0)

    for section, sources in enumerate(places):

        @pl.when((step == 0) & (section_ref[0] == section))
        def _():
            for j, source in enumerate(sources):
                first_ref = own_refs[j] if source is None else arrived[source]
                mixed_ref[:, j * half : (j + 1) * half] = (
                    0.5 * own_refs[j][...].astype(F32) + 0.5 * first_ref[...].astype(F32)
                ).astype(BF16)

    first_mask, _ = head_masks(block)
    for i in range(own_refs[0].shape[0] // block):
        at = i * block
        low = max(0, at - WINDOW)

        @pl.when(step == i)
        def _():
            for pair in range(heads_ref.shape[1] // (2 * HD)):
                lanes = slice(pair * 2 * HD, (pair + 1) * 2 * HD)
                values = mixed_ref[low : at + block, lanes]
                both = [dot(probs_ref[2 * pair + h, :, : at + block - low], values) for h in range(2)]
                heads_ref[:, lanes] = jnp.where(first_mask, both[0], both[1]).astype(BF16)

    part_ref[...] = dot(heads_ref[...], w_ref[...]).astype(BF16)


def heads_proj(section, probs, own, arrived, places, w_out):
    tokens, half = own[0].shape
    width, model = w_out.shape
    n_heads, _, wide = probs.shape
    block = 256
    return call(
        lambda *refs: heads_kernel(len(arrived), places, *refs),
        (tokens // block,),
        [pl.BlockSpec(memory_space=pltpu.SMEM), pl.BlockSpec((n_heads, block, wide), lambda i: (0, i, 0))]
        + [whole(tokens, half)] * (2 + len(arrived))
        + [whole(width, model)],
        [
            (rows(block, width), (tokens, width), BF16),
            (whole(tokens, width), (tokens, width), BF16),
            (rows(block, model), (tokens, model), BF16),
        ],
        (section.astype(jnp.int32)[None], probs, *own, *arrived, w_out),
        40,
    )


def attend_back_kernel(
    q_ref, k_ref, mixed_ref, probs_ref, grad_ref, cos_ref, sin_ref, dq_ref, dk_ref, half_ref, key_acc, value_acc
):
    tokens = q_ref.shape[0]
    block = 256
    key_acc[...] = jnp.zeros_like(key_acc)
    value_acc[...] = jnp.zeros_like(value_acc)

    def turned_back(grads, at, count):
        cos, sin = cos_ref[at : at + count, :], sin_ref[at : at + count, :]
        return (grads * cos - swap_halves(grads) * sin).astype(BF16)

    masks = head_masks(block)
    for at in range(0, tokens, block):
        low = max(0, at - WINDOW)
        queries = q_ref[at : at + block, :] * BF16(HD**-0.5)
        grads = grad_ref[at : at + block, :]
        keys = k_ref[low : at + block, :]
        values = mixed_ref[low : at + block, :]
        parts = []
        for h, mask in enumerate(masks):
            q_head = jnp.where(mask, queries, BF16(0))
            g_head = jnp.where(mask, grads, BF16(0))
            probs_low = probs_ref[h, at : at + block, : at + block - low]
            probs = probs_low.astype(F32)
            grad_probs = dot_nt(g_head, values)
            inner = jnp.sum(probs * grad_probs, axis=1, keepdims=True)
            grad_scores = (probs * (grad_probs - inner)).astype(BF16)
            parts.append(dot(grad_scores, keys))
            key_acc[low : at + block, :] += dot_tn(grad_scores, q_head)
            value_acc[low : at + block, :] += dot_tn(probs_low, g_head)
        grad_query = jnp.where(masks[0], parts[0], parts[1]) * HD**-0.5
        dq_ref[at : at + block, :] = turned_back(grad_query, at, block)
    for at in range(0, tokens, block):
        dk_ref[at : at + block, :] = turned_back(key_acc[at : at + block, :], at, block)
    half_ref[...] = (0.5 * value_acc[...]).astype(BF16)


def attend_back(queries, keys, mixed, probs, grad_heads, cos, sin, first, count, into):
    tokens, width = queries.shape
    pair = columns(tokens, 2 * HD, first)
    wide = probs.shape[2]
    return call(
        attend_back_kernel,
        (count,),
        [pair, pair, pair, pl.BlockSpec((2, tokens, wide), lambda i: (i + first, 0, 0)), pair]
        + [whole(tokens, 128), whole(tokens, 128)],
        [(pair, (tokens, width), BF16)] * 3,
        (queries, keys, mixed, probs, grad_heads, cos, sin),
        40,
        scratch=[pltpu.VMEM((tokens, 2 * HD), F32), pltpu.VMEM((tokens, 2 * HD), F32)],
        into=dict(enumerate(into)),
    )


def units_step(normed, grad_out, wg_ref, wu_ref, wd_ref, hidden_ref, dg_ref, du_ref, stacked_ref):
    gate = dot(normed, wg_ref[...])
    up = dot(normed, wu_ref[...])
    grad_hidden = dot_nt(grad_out, wd_ref[...])
    sig = jax.nn.sigmoid(gate)
    silu = gate * sig
    hidden = (silu * up).astype(BF16)
    hidden_ref[...] = hidden
    dg_ref[...] = (grad_hidden * up * (sig * (1.0 + gate * (1.0 - sig)))).astype(BF16)
    du_ref[...] = (grad_hidden * silu).astype(BF16)
    turned = hidden.T
    height, wide = turned.shape[0], stacked_ref.shape[1]
    for j in range(grad_out.shape[1] // wide):
        stacked_ref[j * height : (j + 1) * height, :] = dot(turned, grad_out[:, j * wide : (j + 1) * wide]).astype(BF16)


def entry_kernel(
    x_ref, own_ref, other_ref, gain_ref, grad_ref, wg_ref, wu_ref, wd_ref,
    middle_ref, normed_ref, turned_ref, hidden_ref, dg_ref, du_ref, gwd_ref,
):
    step = pl.program_id(0)
    block = x_ref.shape[0]
    middle = x_ref[...].astype(F32) + (own_ref[...].astype(F32) + other_ref[...].astype(F32))
    middle_ref[...] = middle
    inv_rms = lax.rsqrt(jnp.mean(middle * middle, axis=1, keepdims=True) + EPSILON)
    normed = (middle * inv_rms * gain_ref[...]).astype(BF16)
    normed_ref[pl.ds(pl.multiple_of(step * block, block), block), :] = normed
    turned_ref[...] = normed.T

    @pl.when(step == pl.num_programs(0) - 1)
    def _():
        units_step(normed_ref[...], grad_ref[...], wg_ref, wu_ref, wd_ref, hidden_ref, dg_ref, du_ref, gwd_ref)


def ffn_kernel(normed_ref, grad_ref, wg_ref, wu_ref, wd_ref, hidden_ref, dg_ref, du_ref, gwd_ref):
    units_step(normed_ref[...], grad_ref[...], wg_ref, wu_ref, wd_ref, hidden_ref, dg_ref, du_ref, gwd_ref)


def entry(x, own, other, gain, grad_out, w_gate, w_up, w_down, units):
    tokens, width = x.shape
    block = 256
    tall = width * units // CHUNK
    first = pl.BlockSpec((width, units), lambda i: (0, 0))
    hidden = (pl.BlockSpec((tokens, units), lambda i: (0, 0)), (tokens, w_gate.shape[1]), BF16)
    return call(
        entry_kernel,
        (tokens // block,),
        [rows(block, width)] * 3
        + [whole(1, width), whole(tokens, width), first, first, pl.BlockSpec((units, width), lambda i: (0, 0))],
        [
            (rows(block, width), (tokens, width), F32),
            (whole(tokens, width), (tokens, width), BF16),
            (columns(width, block), (width, tokens), BF16),
            hidden,
            hidden,
            hidden,
            (whole(tall, CHUNK), (tall, CHUNK), BF16),
        ],
        (x, own, other, gain, grad_out, w_gate, w_up, w_down),
        60,
    )


def ffn(normed, grad_out, w_gate, w_up, w_down, units, number, count, into):
    tokens, width = normed.shape
    tall = width * units // CHUNK
    return call(
        ffn_kernel,
        (count,),
        [whole(tokens, width)] * 2
        + [columns(width, units, number)] * 2
        + [pl.BlockSpec((units, width), lambda i: (i + number, 0))],
        [(columns(tokens, units, number), (tokens, w_gate.shape[1]), BF16)] * 3
        + [(rows(tall, CHUNK), (tall * count, CHUNK), BF16)],
        (normed, grad_out, w_gate, w_up, w_down),
        48,
        into=dict(enumerate(into)),
    )


def weight_grads_kernel(turned_ref, *refs):
    half = len(refs) // 2
    for d_ref, o_ref in zip(refs[:half], refs[half:]):
        o_ref[...] = dot(turned_ref[...], d_ref[...]).astype(BF16)


def weight_grads(turned, grads, units, number):
    width, tokens = turned.shape
    block = 256
    column = pl.BlockSpec((tokens, units), lambda i: (0, number))
    return call(
        weight_grads_kernel,
        (width // block,),
        [rows(block, tokens)] + [column] * len(grads),
        [(rows(block, units), (width, units), BF16)] * len(grads),
        (turned, *grads),
        40,
    )


def stacked_grads_kernel(left_ref, right_ref, out_ref, turned):
    @pl.when(pl.program_id(0) == 0)
    def _():
        turned[...] = left_ref[...].T

    out_ref[...] = dot(turned[...], right_ref[...]).astype(BF16)


def stacked_grads(left, right, number):
    tokens, width = right.shape
    return call(
        stacked_grads_kernel,
        (width // CHUNK,),
        [pl.BlockSpec((tokens, CHUNK), lambda i: (0, number)), columns(tokens, CHUNK)],
        [(rows(CHUNK, CHUNK), (width, CHUNK), BF16)],
        (left, right),
        40,
        scratch=[pltpu.VMEM((CHUNK, tokens), BF16)],
    )[0]


def norm_back_kernel(dn_ref, do_ref, v_ref, gain_ref, base_ref, out_ref, *more):
    grad_normed = dn_ref[...].astype(F32) + do_ref[...].astype(F32)
    values = v_ref[...].astype(F32)
    inv_rms = lax.rsqrt(jnp.mean(values * values, axis=1, keepdims=True) + EPSILON)
    weighted = grad_normed * gain_ref[...]
    inner = jnp.mean(weighted * values, axis=1, keepdims=True)
    out = base_ref[...].astype(F32) + inv_rms * weighted - values * (inv_rms * inv_rms * inv_rms) * inner
    out_ref[...] = out
    gain_grad_ref = more[-1]
    if len(more) > 1:
        more[0][...] = out.astype(BF16)

    @pl.when(pl.program_id(0) == 0)
    def _():
        gain_grad_ref[...] = jnp.zeros_like(gain_grad_ref)

    gain_grad_ref[...] += jnp.sum(grad_normed * values * inv_rms, axis=0, keepdims=True)


def norm_back(own, other, values, gain, base, low):
    tokens, width = own.shape
    block = 256
    outs = [(rows(block, width), (tokens, width), F32)]
    if low:
        outs.append((rows(block, width), (tokens, width), BF16))
    outs.append((whole(1, width), (1, width), F32))
    return call(
        norm_back_kernel,
        (tokens // block,),
        [rows(block, width)] * 3 + [whole(1, width), rows(block, width)],
        outs,
        (own, other, values, gain, base),
        40,
    )


def tie(*values):
    return lax.optimization_barrier(values)


def tick_kernel(names, n_sums, flags_ref, *refs):
    refs = dict(zip(names, refs))

    def add(one, two):
        return (refs[one][...].astype(F32) + refs[two][...].astype(F32)).astype(BF16)

    def put_sum(source):
        value = refs[source][...].astype(F32)
        wide = value.shape[1] // max(n_sums, 1)
        for j in range(n_sums):
            refs[f"sum{j}"][...] = value[:, j * wide : (j + 1) * wide]

    is_left, is_end = flags_ref[0] == 1, flags_ref[1] == 1
    for side, inward, outward in ((is_left, "right", "left"), (jnp.logical_not(is_left), "left", "right")):
        go_in = refs.get("go_" + inward, refs.get("go"))
        go_out = refs.get("go_" + outward, refs.get("go"))

        @pl.when(side & is_end)
        def _():
            if "part" in refs:
                go_in[...] = refs["part"][...]
            if n_sums:
                put_sum("arrived_" + outward)

        @pl.when(side & jnp.logical_not(is_end))
        def _():
            if "old_part" in refs:
                go_in[...] = add("old_part", "arrived_" + inward)
            if "back" in refs:
                go_out[...] = add("gone_" + inward, "arrived_" + outward)
            if n_sums:
                put_sum("gone_" + outward)


def tick_call(flags, inputs, gos, back, sums, into):
    steps = {"part": 1, "arrived_right": 3, "arrived_left": 4, "old_part": 2, "gone_right": 2, "gone_left": 2}
    shape = next(iter(inputs.values())).shape
    block = (256, shape[1])
    ins = [
        pl.BlockSpec(block, lambda i, flags, f=steps[name]: (i * flags[f], 0)) for name in inputs
    ]
    outs = [pl.BlockSpec(block, lambda i, flags: (i, 0)) for _ in gos]
    outs += [pl.BlockSpec(b, lambda i, flags, at=at: at(i)) for b, at, _ in sums]
    shapes = [jax.ShapeDtypeStruct(shape, BF16) for _ in gos] + [jax.ShapeDtypeStruct(s, F32) for _, _, s in sums]
    held = [(j, array) for j, array in enumerate(into) if array is not None]
    n_in = len(inputs)
    names = list(inputs) + list(gos) + [f"sum{j}" for j in range(len(sums))] + (["back"] if back else [])

    def body(flags_ref, *refs):
        tick_kernel(names, len(sums), flags_ref, *refs[:n_in], *refs[n_in + len(held) :], *([None] if back else []))

    return pl.pallas_call(
        body,
        grid_spec=pltpu.PrefetchScalarGridSpec(
            num_scalar_prefetch=1,
            grid=(shape[0] // block[0],),
            in_specs=ins + [pl.BlockSpec(memory_space=pl.ANY)] * len(held),
            out_specs=outs,
        ),
        out_shape=shapes,
        input_output_aliases={1 + n_in + h: len(gos) + j for h, (j, _) in enumerate(held)},
        compiler_params=pltpu.CompilerParams(vmem_limit_bytes=24 * MIB),
        cost_estimate=pl.CostEstimate(flops=1, bytes_accessed=1, transcendentals=0),
    )(flags, *inputs.values(), *[array for _, array in held])


class Line:
    def __init__(self, axis, size, shapes):
        self.axis, self.size, self.shapes = axis, size, shapes
        place = lax.axis_index(axis)
        end, left = (place == 0) | (place == 3), place < 2
        mid = jnp.logical_not(end)
        self.flags = jnp.stack([left, end, mid, jnp.where(left, mid, True), jnp.where(left, True, mid)]).astype(jnp.int32)
        self.parts, self.places = [], []
        self.arrived, self.gone = {}, {}
        self.outs = {name: None for name in shapes}
        self.at = 0
        self.clock = []

    def after(self, *values):
        if not self.clock:
            return values if len(values) > 1 else values[0]
        held = tie(*values, *self.clock)[: len(values)]
        return held if len(values) > 1 else held[0]

    def mark(self, *values):
        self.clock = list(values)

    def push(self, part, *places):
        self.places.append(places)
        self.parts.append(part)

    def tick(self, times=1):
        if self.size != 4:
            return
        for _ in range(times):
            k, n = self.at, len(self.parts)
            self.at += 1
            old = k - 2
            inputs = {}
            if k < n:
                inputs["part"] = self.parts[k]
            if old in self.arrived:
                inputs["arrived_right"], inputs["arrived_left"] = self.arrived[old]
            if not inputs:
                continue
            inputs = dict(zip(inputs, tie(*inputs.values(), *self.clock)))
            if k < n:
                self.parts[k] = inputs["part"]
            halves, totals, done = 0 <= k - 2 < n, 0 <= k - 4 < n, 0 <= k - 6 < n
            if halves:
                inputs["old_part"] = self.parts[old]
            if totals or done:
                inputs["gone_right"], inputs["gone_left"] = self.gone[old]
            right, left = [], []
            for wanted, pairs in ((k < n, ((0, 1), (3, 2))), (halves, ((1, 2), (2, 1))), (totals, ((2, 3), (1, 0)))):
                if wanted:
                    right, left = right + [pairs[0]], left + [pairs[1]]
            inner = k < n or halves
            gos = ["go_right", "go_left"] if inner and totals else ["go"] if inner or totals else []
            places = self.places[k - 6] if done else ()
            if k < 2:
                results = [inputs["part"]]
            else:
                results = tick_call(
                    self.flags,
                    inputs,
                    gos,
                    totals,
                    [(block, at, self.shapes[name]) for name, block, at in places],
                    [self.outs[name] for name, _, _ in places],
                )
            go = results[: len(gos)]
            for (name, _, _), array in zip(places, results[len(gos) :]):
                self.outs[name] = array
            if go:
                self.gone[k] = (go[0], go[-1])
                self.arrived[k] = (lax.ppermute(go[0], self.axis, right), lax.ppermute(go[-1], self.axis, left))
                self.mark(*go)
            else:
                self.mark(*results)

    def finish(self):
        if self.size == 4:
            self.tick(len(self.parts) + 6 - self.at)
            return
        for part, places in zip(self.parts, self.places):
            value = lax.psum(part, self.axis).astype(F32)
            from_col = 0
            for name, block, at in places:
                if self.outs[name] is None:
                    self.outs[name] = jnp.zeros(self.shapes[name], F32)
                for i in range(part.shape[0] // 256):
                    where = tuple(b * o for b, o in zip(block, at(i)))
                    piece = value[i * 256 : (i + 1) * 256, from_col : from_col + block[1]]
                    self.outs[name] = lax.dynamic_update_slice(self.outs[name], piece, where)
                from_col += block[1]


def tables(lengths_row, tokens):
    seqs = lengths_row.shape[0]
    slot = jnp.arange(seqs, dtype=jnp.int32)
    ends = jnp.sum(jnp.where(slot[None, :] <= slot[:, None], lengths_row[None, :], 0), axis=1)
    places = jnp.arange(tokens, dtype=jnp.int32)
    start = jnp.sum(jnp.where(places[:, None] >= ends[None, :], lengths_row[None, :], 0), axis=1)
    position = (places - start).astype(F32)
    inv_freq = 10000.0 ** (-(jnp.arange(HD // 2, dtype=F32) * 2.0 / HD))
    angles = position[:, None] * inv_freq[None, :]
    cos, sin = jnp.cos(angles), jnp.sin(angles)
    return jnp.concatenate([cos] * 4, axis=1), jnp.concatenate([-sin, sin, -sin, sin], axis=1)


def exchange(part, axis):
    return lax.ppermute(part, axis, [(0, 1), (1, 0)])


def shards(sizes, *args):
    (x, lengths, gain_attn, w_query, w_key, w_value, w_out, gain_ffn, w_gate, w_up, w_down, grad_out) = args
    x, w_query, w_key, w_value, w_out, w_gate, w_up, w_down, grad_out = (
        a[0] for a in (x, w_query, w_key, w_value, w_out, w_gate, w_up, w_down, grad_out)
    )
    tokens, width = x.shape
    units = w_gate.shape[1]
    rest = units % CHUNK
    n_sections = sizes["section"]
    section = lax.axis_index("section")
    outputs = {"query": w_query, "key": w_key, "value": w_value, "out": w_out, "gate": w_gate, "up": w_up, "down": w_down}
    shapes = {name: w.shape for name, w in outputs.items()}
    shapes["tail"] = (width, CHUNK)
    line = Line("dp", sizes["dp"], shapes)

    def column(name, number, wide=CHUNK):
        return name, (256, wide), lambda i: (i, number)

    def stacked(name, number):
        return name, (CHUNK, CHUNK), lambda i: (number, i)

    normed, *own = value_proj(x, gain_attn, w_value)

    def send(block, *pairs):
        return lax.ppermute(block, "section", list(pairs))

    relay = n_sections == 4
    if relay:
        one, two = send(own[0], (0, 1)), send(own[1], (0, 2))
    cos, sin = tables(lengths[0], tokens)
    queries, keys = query_key_proj(normed, w_query, w_key, cos, sin)
    if relay:
        one, two, queries = tie(one, two, queries)
        three = send(jnp.where(section == 0, own[1], one), (0, 1), (1, 3))
        four = send(jnp.where(section == 0, own[0], two), (0, 2), (2, 3))
        queries, three_, four_ = queries, three, four
        arrived = [one, two, three, four]
        places = [(None, None), (0, 2), (3, 1), (2, 3)]
    else:
        arrived = [send(half, (0, s)) for s in range(1, n_sections) for half in own]
        places = [(None, None)] + [(2 * s, 2 * s + 1) for s in range(n_sections - 1)]
    probs = probabilities(lengths, queries, keys)
    probs, *arrived = tie(probs, *arrived)
    heads, mixed, part = heads_proj(section, probs, own, arrived, places, w_out)

    weights = (w_gate, w_up, w_down)
    middle, normed_ffn, turned_ffn, *acts, down = entry(
        x, part, exchange(part, "tensor"), gain_ffn, grad_out, *weights, CHUNK
    )
    line.push(down, stacked("down", 0))
    line.tick()

    def unit_grads(number, size=CHUNK):
        grads = weight_grads(line.after(turned_ffn), acts[1:3], size, number)
        if size == CHUNK:
            line.push(grads[0], column("gate", number))
            line.push(grads[1], column("up", number))
        else:
            line.push(jnp.concatenate(grads, axis=1), column("gate", number, size), column("up", number, size))
        line.mark(grads[0])

    unit_grads(0)
    line.tick()
    number = 1
    while number < units // CHUNK:
        count = min(2, units // CHUNK - number)
        *acts, down = ffn(line.after(normed_ffn), grad_out, *weights, CHUNK, number, count, acts)
        for j in range(count):
            line.push(down[j * width : (j + 1) * width], stacked("down", number + j))
        line.mark(down)
        number += count
        line.tick()
    tail = []
    if rest:
        *acts, down = ffn(line.after(normed_ffn), grad_out, *weights, rest, units // rest - 1, 1, acts)
        tail.append(down)
        line.mark(down)
    hidden, grad_gate, grad_up = acts
    unit_grads(1)
    line.tick()
    part = (dot_nt(line.after(grad_gate), w_gate) + dot_nt(grad_up, w_up)).astype(BF16)
    part_other = exchange(part, "tensor")
    line.mark(part)
    line.tick()
    unit_grads(2)
    line.tick()
    grad_middle, grad_attn, grad_gain_ffn = norm_back(
        line.after(part), part_other, middle, gain_ffn, grad_out, True
    )
    line.mark(grad_attn)
    line.tick()

    grad_heads = dot_nt(line.after(grad_attn), w_out).astype(BF16)
    line.mark(grad_heads)
    line.tick()
    pairs = queries.shape[1] // (2 * HD)
    grads = [None] * 3
    for first in range(pairs):
        grads = attend_back(queries, keys, mixed, probs, line.after(grad_heads), cos, sin, first, 1, grads)
        line.mark(grads[0])
        if first == 0:
            for number in range(3, units // CHUNK):
                unit_grads(number)
            if rest:
                unit_grads(units // rest - 1, rest)
        line.tick()
    grad_query, grad_key, half_mixed = grads
    arrived = [send(half_mixed, (s, 0)) for s in range(1, n_sections)]
    for number in range(heads.shape[1] // CHUNK):
        line.push(stacked_grads(line.after(heads), grad_attn, number), stacked("out", number))
    line.mark(line.parts[-1])
    line.tick()

    def column_grads(name, grad):
        for number in range(grad.shape[1] // CHUNK):
            lo = number * CHUNK
            line.push(dot_tn(normed, line.after(grad)[:, lo : lo + CHUNK]).astype(BF16), column(name, number))
        line.mark(*line.parts[-2:])

    column_grads("query", grad_query)
    line.tick()
    column_grads("key", grad_key)
    line.tick()
    part = dot_nt(line.after(grad_query), w_query) + dot_nt(grad_key, w_key)
    line.mark(part)
    line.tick()
    part_result = dot(line.after(hidden), w_down).astype(BF16)
    result_other = exchange(part_result, "tensor")
    line.mark(part_result)
    line.tick()
    result = (middle + (line.after(part_result).astype(F32) + result_other.astype(F32))).astype(BF16)
    line.mark(result)
    line.tick()
    half_mixed = line.after(half_mixed).astype(F32)
    first_total = half_mixed
    for block in arrived:
        first_total = first_total + block.astype(F32)
    grad_value = (half_mixed + jnp.where(section == 0, first_total, 0.0)).astype(BF16)
    column_grads("value", grad_value)
    line.tick()
    part = (part + dot_nt(line.after(grad_value), w_value)).astype(BF16)
    part_other = exchange(part, "tensor")
    line.mark(part)
    line.tick()
    grad_input, grad_gain_attn = norm_back(line.after(part), part_other, x, gain_attn, grad_middle, False)
    line.mark(grad_input)
    gains = jnp.concatenate([grad_gain_attn, grad_gain_ffn], axis=0).reshape(-1, CHUNK).astype(BF16)
    tail_rows = sum(t.shape[0] for t in tail)
    tail.append(jnp.pad(gains, ((0, width - tail_rows - gains.shape[0]), (0, 0))))
    line.push(jnp.concatenate(tail, axis=0), column("tail", 0))
    line.finish()

    outs = line.outs
    tail = outs["tail"]
    gains = tail[tail_rows : tail_rows + gains.shape[0]].reshape(2, width)
    if rest:
        last = jnp.concatenate([tail[lo : lo + rest] for lo in range(0, tail_rows, rest)], axis=1)
        outs["down"] = lax.dynamic_update_slice(outs["down"], last, (units - rest, 0))
    return (
        result[None],
        grad_input[None],
        gains[0:1],
        *(outs[name][None] for name in ("query", "key", "value", "out")),
        gains[1:2],
        *(outs[name][None] for name in ("gate", "up", "down")),
    )


def solution(mesh):
    sizes = dict(mesh.shape)
    token = P("section", "dp", None)
    gain = P("section", None)
    wide, tall = P("section", None, "tensor"), P("section", "tensor", None)
    return jax.shard_map(
        lambda *args: shards(sizes, *args),
        mesh=mesh,
        in_specs=(token, P("dp", None), gain, wide, wide, wide, tall, gain, wide, wide, tall, token),
        out_specs=(token, token, gain, wide, wide, wide, tall, gain, wide, wide, tall),
        check_vma=False,
    )
```

time: 1180 us -> 510 us (0.43)
  waiting for transfers between devices: 631 us -> 114 us
  matrix products: 242 us -> 20.6 us
  Pallas kernels: 0 us -> 182 us
  starting transfers between devices: 1.1 us -> 155 us
  other arithmetic: 156 us -> 8.38 us
  local copies, waits for them, and re-layouts: 89.9 us -> 19.6 us
  loops' own time: 19.3 us -> 0 us
  blocking collectives: 16.1 us -> 0 us
  between operations: 15.4 us -> 2.8 us
    all_gather x7 -> x0, waiting for transfers between devices: 255 us -> none  [the longest x1 54.8 us: shards(): lax.all_gather(all_summed[5].astype(jnp.bfloat16), 'dp', axis=0, tiled=True)]
    reduce_scatter x7 -> x0, waiting for transfers between devices: 234 us -> none  [the longest x1 59 us: shards(): lax.psum_scatter(grad_w_up.astype(jnp.bfloat16), 'dp', scatter_dimension=...]
    dot_general x41 -> x13, matrix products: 242 us -> 20.6 us  [the longest x6 12.4 us: dot_nt(): lax.dot_general(left, right, (((1,), (1,)), ((), ())), preferred_element_...]
    pallas_call x0 -> x51, Pallas kernels: none -> 182 us  [the longest x22 111 us: call(): pl.pallas_call(body, grid=grid, in_specs=ins, out_specs=[spec for spec, _...]
    ppermute x0 -> x69, starting transfers between devices: none -> 155 us  [the longest x29 98.6 us: tick(): lax.ppermute(go[0], self.axis, right)]
    ppermute x0 -> x69, waiting for transfers between devices: none -> 114 us  [the longest x29 64.5 us: tick(): lax.ppermute(go[-1], self.axis, left)]
    psum x5 -> x0, waiting for transfers between devices: 107 us -> none  [the longest x1 32.3 us: spread(): return lax.psum(block, axis)]
    sub x2 -> x0, other arithmetic: 43.5 us -> none  [one_block(): exps = jnp.exp(scores - row_max)]
  transfers between devices with their start and end apart: 21 -> 69, of which waited for: 19 -> 25; matrix products, arithmetic and copies ran while one was open for 20% -> 3% of each run, Pallas kernels for 0% -> 30%
where the time goes in v1:
time: 510 us; the launch traced here: 503 us
  Pallas kernels  182 us (36%)
  starting transfers between devices  155 us (30%)
  waiting for transfers between devices  114 us (22%)
  matrix products  20.6 us (4%)
  local copies, waits for them, and re-layouts  19.6 us (4%)
  other arithmetic  8.38 us (2%)
    pallas_call x22, Pallas kernels, call(): pl.pallas_call(body, grid=grid, in_specs=ins, out_specs=[spec for spec, _...  111 us
    ppermute x29, starting transfers between devices, tick(): lax.ppermute(go[0], self.axis, right)  98.6 us
    pallas_call x29, Pallas kernels, tick_call(): pl.pallas_call(body, grid_spec=pltpu.PrefetchScalarGridSpec(num_scalar_pr...  71.1 us
    ppermute x29, waiting for transfers between devices, tick(): lax.ppermute(go[-1], self.axis, left)  64.5 us
    ppermute x29, starting transfers between devices, tick(): lax.ppermute(go[-1], self.axis, left)  38.4 us
    ppermute x29, waiting for transfers between devices, tick(): lax.ppermute(go[0], self.axis, right)  27.5 us
    unnamed x121, local copies, waits for them, and re-layouts  19.3 us
    ppermute x7, waiting for transfers between devices, send(): return lax.ppermute(block, 'section', list(pairs))  18.3 us
  transfers between devices with their start and end apart: 69, of which 25 were waited for; matrix products, arithmetic and copies ran while one was open for 3% of the time, Pallas kernels for 30%

profile of v1, /device:TPU:0, one launch (start us, length us, event | category | flops | bytes accessed | tf_op | source)
XLA Modules:
  0.0 503.0 jit_solution(9002848069208903236)
XLA Ops:
  5.7 5.9 %collective-permute-start = (bf16[1024,256]{1,0:T(8,128)(2,1)}, bf16[1024,256]{1,0:T(8,128)(2,1)}, u32[]{:S(2)}, u32[]{:S(2)}) collective-permute-start(bf16[1024,256]{1,0:T(8,128)(2,1)} %get-tuple-element.254.refs_2_), channel_id=1, source_target_pairs={{0,8},{1,9},{2,10},{3,11},{4,12},{5,13},{6,14},{7,15}} | collective-permute-start | bytes 1572872 | tf_op jit(solution)/shard_map/ppermute | solution.py:645
  31.9 10.5 %shard_map.205.refs_1_.probs_ref.refs_3_ = bf16[8,1024,768]{2,1,0:T(8,128)(2,1)} custom-call(s32[1,4]{1,0:T(1,128)S(1)} %copy-done.51, bf16[1024,512]{1,0:T(8,128)(2,1)S(1)} %get-tuple-element.258.q_ref.refs_0_, bf16[1024,512]{1,0:T(8,128)(2,1)S(1)} %get-tuple-element.259.k_ref.refs_1_), custom_call_target="tpu_custom_call" | custom-call | flops 1 | bytes 1 | tf_op jit(solution)/shard_map/pallas_call | solution.py:41
  42.4 8.1 %shard_map.206 = (bf16[1024,512]{1,0:T(8,128)(2,1)S(1)}, bf16[1024,512]{1,0:T(8,128)(2,1)S(1)}, bf16[1024,1024]{1,0:T(8,128)(2,1)S(1)}) custom-call(s32[1]{0:T(128)} %bitcast.1.refs_0_, bf16[8,1024,768]{2,1,0:T(8,128)(2,1)} %shard_map.205.refs_1_.probs_ref.refs_3_, bf16[1024,256]{1,0:T(8,128)(2,1)S(1)} %copy-done.30, bf16[1024,256]{1,0:T(8,128)(2,1)S(1)} %copy-done.31, ...), custom_call_target="tpu_custom_call" | custom-call | flops 1 | bytes 1 | tf_op jit(solution)/shard_map/pallas_call | solution.py:41
  58.0 11.6 %shard_map.207 = (f32[1024,1024]{1,0:T(8,128)}, bf16[1024,1024]{1,0:T(8,128)(2,1)}, bf16[1024,1024]{1,0:T(8,128)(2,1)}, bf16[1024,1408]{1,0:T(8,128)(2,1)}, bf16...) custom-call(bf16[1024,1024]{1,0:T(8,128)(2,1)} %bitcast.70, ...), custom_call_target="tpu_custom_call" | custom-call | flops 1 | bytes 1 | tf_op jit(solution)/shard_map/pallas_call | solution.py:41
  89.7 7.7 %shard_map.209 = (bf16[1024,1408]{1,0:T(8,128)(2,1)}, bf16[1024,1408]{1,0:T(8,128)(2,1)}, bf16[1024,1408]{1,0:T(8,128)(2,1)}, bf16[2048,256]{1,0:T(8,128)(2,1)S(1)}) custom-call(bf16[1024,1024]{1,0:T(8,128)(2,1)S(1)} %copy-done.16, bf16[1024,1024]{1,0:T(8,128)(2,1)S(1)} %bitcast.65, ...), custom_call_target="tpu_custom_call", output_to_operand_aliasing={{0}: (5, {}), {1}: (6, {}), {2}: (7, {})} | custom-call | flops 1 | bytes 1 | tf_op jit(solution)/shard_map/pallas_call | solution.py:41
  102.1 7.6 %shard_map.211 = (bf16[1024,1408]{1,0:T(8,128)(2,1)}, bf16[1024,1408]{1,0:T(8,128)(2,1)}, bf16[1024,1408]{1,0:T(8,128)(2,1)}, bf16[2048,256]{1,0:T(8,128)(2,1)S(1)}) custom-call(bf16[1024,1024]{1,0:T(8,128)(2,1)S(1)} %copy-done.16, bf16[1024,1024]{1,0:T(8,128)(2,1)S(1)} %bitcast.66, ...), custom_call_target="tpu_custom_call", output_to_operand_aliasing={{0}: (5, {}), {1}: (6, {}), {2}: (7, {})} | custom-call | flops 1 | bytes 1 | tf_op jit(solution)/shard_map/pallas_call | solution.py:41
  140.1 7.6 %collective-permute-done.13.refs_1_ = bf16[1024,256]{1,0:T(8,128)(2,1)S(1)} collective-permute-done((bf16[1024,256]{1,0:T(8,128)(2,1)S(1)}, bf16[1024,256]{1,0:T(8,128)(2,1)S(1)}, u32[]{:S(2)}, u32[]{:S(2)}) %collective-permute-start.13) | collective-permute-done | bytes 524320 | tf_op jit(solution)/shard_map/ppermute | solution.py:582
  149.8 7.3 %collective-permute-start.16 = (bf16[1024,256]{1,0:T(8,128)(2,1)}, bf16[1024,256]{1,0:T(8,128)(2,1)}, u32[]{:S(2)}, u32[]{:S(2)}) collective-permute-start(bf16[1024,256]{1,0:T(8,128)(2,1)} %get-tuple-element.312.refs_4_), channel_id=1, source_target_pairs={{0,2},{2,4},{4,6},{1,3},{3,5},{5,7},{8,10},{10,12},{12,14},{9,11},... | collective-permute-start | bytes 1572872 | tf_op jit(solution)/shard_map/ppermute | solution.py:582
  162.5 5.0 %collective-permute-start.18 = (bf16[1024,256]{1,0:T(8,128)(2,1)S(1)}, bf16[1024,256]{1,0:T(8,128)(2,1)S(1)}, u32[]{:S(2)}, u32[]{:S(2)}) collective-permute-start(bf16[1024,256]{1,0:T(8,128)(2,1)S(1)} %get-tuple-element.319.refs_4_), channel_id=1, source_target_pairs={{0,2},{2,4},{4,6},{1,3},{3,5},{5,7},{8,10},{10,12},{12,14},{9,11},... | collective-permute-start | bytes 1572872 | tf_op jit(solution)/shard_map/ppermute | solution.py:582
  174.3 5.2 %shard_map.220 = (bf16[1024,256]{1,0:T(8,128)(2,1)S(1)}, bf16[1024,256]{1,0:T(8,128)(2,1)S(1)}, f32[1024,1408]{1,0:T(8,128)}) custom-call(s32[5]{0:T(128)S(1)} %convert_element_type.71.flags_ref, bf16[1024,256]{1,0:T(8,128)(2,1)S(1)} %get-tuple-element.323.refs_0_.refs_3_, bf16[1024,256]{1,0:T(8,128)(2,1)} %collective-permute-done.16.refs_1_, ...), custom_call_target="tpu_custom_call" | custom-call | flops 1 | bytes 1 | tf_op jit(solution)/shard_map/pallas_call | solution.py:496
  179.5 5.6 %collective-permute-start.22 = (bf16[1024,256]{1,0:T(8,128)(2,1)S(1)}, bf16[1024,256]{1,0:T(8,128)(2,1)}, u32[]{:S(2)}, u32[]{:S(2)}) collective-permute-start(bf16[1024,256]{1,0:T(8,128)(2,1)S(1)} %get-tuple-element.326.refs_4_), channel_id=1, source_target_pairs={{0,2},{2,4},{4,6},{1,3},{3,5},{5,7},{8,10},{10,12},{12,14},{9,11},... | collective-permute-start | bytes 1572872 | tf_op jit(solution)/shard_map/ppermute | solution.py:582
  190.1 5.5 %collective-permute-start.20 = (bf16[1024,256]{1,0:T(8,128)(2,1)S(1)}, bf16[1024,256]{1,0:T(8,128)(2,1)}, u32[]{:S(2)}, u32[]{:S(2)}) collective-permute-start(bf16[1024,256]{1,0:T(8,128)(2,1)S(1)} %get-tuple-element.333.refs_4_), channel_id=1, source_target_pairs={{0,2},{2,4},{4,6},{1,3},{3,5},{5,7},{8,10},{10,12},{12,14},{9,11},... | collective-permute-start | bytes 1572872 | tf_op jit(solution)/shard_map/ppermute | solution.py:582
  196.9 6.9 %shard_map.222 = (bf16[1024,512]{1,0:T(8,128)(2,1)S(1)}, bf16[1024,512]{1,0:T(8,128)(2,1)S(1)}, bf16[1024,512]{1,0:T(8,128)(2,1)S(1)}) custom-call(bf16[1024,512]{1,0:T(8,128)(2,1)S(1)} %get-tuple-element.258.q_ref.refs_0_, bf16[1024,512]{1,0:T(8,128)(2,1)S(1)} %copy-done.10, bf16[1024,512]{1,0:T(8,128)(2,1)S(1)} %copy-done.18, ...), custom_call_target="tpu_custom_call" | custom-call | flops 1 | bytes 1 | tf_op jit(solution)/shard_map/pallas_call | solution.py:41
  219.8 6.8 %shard_map.227 = (bf16[1024,512]{1,0:T(8,128)(2,1)S(1)}, bf16[1024,512]{1,0:T(8,128)(2,1)S(1)}, bf16[1024,512]{1,0:T(8,128)(2,1)S(1)}) custom-call(bf16[1024,512]{1,0:T(8,128)(2,1)S(1)} %get-tuple-element.258.q_ref.refs_0_, bf16[1024,512]{1,0:T(8,128)(2,1)S(1)} %copy-done.10, ...), custom_call_target="tpu_custom_call", output_to_operand_aliasing={{0}: (7, {}), {1}: (8, {}), {2}: (9, {})} | custom-call | flops 1 | bytes 1 | tf_op jit(solution)/shard_map/pallas_call | solution.py:41
  236.7 6.8 %shard_map.229 = (bf16[1024,512]{1,0:T(8,128)(2,1)S(1)}, bf16[1024,512]{1,0:T(8,128)(2,1)S(1)}, bf16[1024,512]{1,0:T(8,128)(2,1)S(1)}) custom-call(bf16[1024,512]{1,0:T(8,128)(2,1)S(1)} %get-tuple-element.258.q_ref.refs_0_, bf16[1024,512]{1,0:T(8,128)(2,1)S(1)} %copy-done.10, ...), custom_call_target="tpu_custom_call", output_to_operand_aliasing={{0}: (7, {}), {1}: (8, {}), {2}: (9, {})} | custom-call | flops 1 | bytes 1 | tf_op jit(solution)/shard_map/pallas_call | solution.py:41
  252.0 6.8 %shard_map.231 = (bf16[1024,512]{1,0:T(8,128)(2,1)S(1)}, bf16[1024,512]{1,0:T(8,128)(2,1)S(1)}, bf16[1024,512]{1,0:T(8,128)(2,1)S(1)}) custom-call(bf16[1024,512]{1,0:T(8,128)(2,1)S(1)} %get-tuple-element.258.q_ref.refs_0_, bf16[1024,512]{1,0:T(8,128)(2,1)S(1)} %copy-done.10, ...), custom_call_target="tpu_custom_call", output_to_operand_aliasing={{0}: (7, {}), {1}: (8, {}), {2}: (9, {})} | custom-call | flops 1 | bytes 1 | tf_op jit(solution)/shard_map/pallas_call | solution.py:41
  312.7 7.9 %collective-permute-done.36.refs_1_ = bf16[1024,256]{1,0:T(8,128)(2,1)S(1)} collective-permute-done((bf16[1024,256]{1,0:T(8,128)(2,1)S(1)}, bf16[1024,256]{1,0:T(8,128)(2,1)S(1)}, u32[]{:S(2)}, u32[]{:S(2)}) %collective-permute-start.36) | collective-permute-done | bytes 524320 | tf_op jit(solution)/shard_map/ppermute | solution.py:582
  345.5 15.5 %collective-permute-done.42 = bf16[1024,512]{1,0:T(8,128)(2,1)S(1)} collective-permute-done((bf16[1024,512]{1,0:T(8,128)(2,1)S(1)}, bf16[1024,512]{1,0:T(8,128)(2,1)S(1)}, u32[]{:S(2)}, u32[]{:S(2)}) %collective-permute-start.42) | collective-permute-done | bytes 1048608 | tf_op jit(solution)/shard_map/ppermute | solution.py:645
  417.4 5.2 %collective-permute-done.56.refs_2_ = bf16[1024,256]{1,0:T(8,128)(2,1)} collective-permute-done((bf16[1024,256]{1,0:T(8,128)(2,1)}, bf16[1024,256]{1,0:T(8,128)(2,1)}, u32[]{:S(2)}, u32[]{:S(2)}) %collective-permute-start.56) | collective-permute-done | bytes 524320 | tf_op jit(solution)/shard_map/ppermute | solution.py:582
  450.5 5.4 %collective-permute-done.58.refs_1_ = bf16[1024,256]{1,0:T(8,128)(2,1)S(1)} collective-permute-done((bf16[1024,256]{1,0:T(8,128)(2,1)S(1)}, bf16[1024,256]{1,0:T(8,128)(2,1)S(1)}, u32[]{:S(2)}, u32[]{:S(2)}) %collective-permute-start.58) | collective-permute-done | bytes 524320 | tf_op jit(solution)/shard_map/ppermute | solution.py:582
  460.1 7.1 %collective-permute-done.64.refs_1_ = bf16[1024,256]{1,0:T(8,128)(2,1)S(1)} collective-permute-done((bf16[1024,256]{1,0:T(8,128)(2,1)S(1)}, bf16[1024,256]{1,0:T(8,128)(2,1)S(1)}, u32[]{:S(2)}, u32[]{:S(2)}) %collective-permute-start.64) | collective-permute-done | bytes 524320 | tf_op jit(solution)/shard_map/ppermute | solution.py:582
  471.3 7.1 %collective-permute-done.62.refs_1_ = bf16[1024,256]{1,0:T(8,128)(2,1)S(1)} collective-permute-done((bf16[1024,256]{1,0:T(8,128)(2,1)S(1)}, bf16[1024,256]{1,0:T(8,128)(2,1)S(1)}, u32[]{:S(2)}, u32[]{:S(2)}) %collective-permute-start.62) | collective-permute-done | bytes 524320 | tf_op jit(solution)/shard_map/ppermute | solution.py:582
  482.5 7.1 %collective-permute-done.68.refs_1_ = bf16[1024,256]{1,0:T(8,128)(2,1)S(1)} collective-permute-done((bf16[1024,256]{1,0:T(8,128)(2,1)S(1)}, bf16[1024,256]{1,0:T(8,128)(2,1)S(1)}, u32[]{:S(2)}, u32[]{:S(2)}) %collective-permute-start.68) | collective-permute-done | bytes 524320 | tf_op jit(solution)/shard_map/ppermute | solution.py:582
  491.8 7.8 %collective-permute-done.66.refs_1_ = bf16[1024,256]{1,0:T(8,128)(2,1)S(1)} collective-permute-done((bf16[1024,256]{1,0:T(8,128)(2,1)S(1)}, bf16[1024,256]{1,0:T(8,128)(2,1)S(1)}, u32[]{:S(2)}, u32[]{:S(2)}) %collective-permute-start.66) | collective-permute-done | bytes 524320 | tf_op jit(solution)/shard_map/ppermute | solution.py:582
  (321 shorter events, 322.2 us)
Async XLA Ops:
  69.6 27.7 %collective-permute-start.7 = (bf16[1024,256]{1,0:T(8,128)(2,1)}, bf16[1024,256]{1,0:T(8,128)(2,1)}, u32[]{:S(2)}, u32[]{:S(2)}) collective-permute-start(bf16[1024,256]{1,0:T(8,128)(2,1)} %get-tuple-element.271.refs_3_), channel_id=1, source_target_pairs={{0,2},{1,3},{8,10},{9,11},{16,18},{17,19},{24,26},{25,27}} | collective-permute-start | bytes 1572872 | tf_op jit(solution)/shard_map/ppermute | solution.py:582
  74.0 23.4 %collective-permute-start.8 = (bf16[1024,256]{1,0:T(8,128)(2,1)}, bf16[1024,256]{1,0:T(8,128)(2,1)}, u32[]{:S(2)}, u32[]{:S(2)}) collective-permute-start(bf16[1024,256]{1,0:T(8,128)(2,1)} %get-tuple-element.271.refs_3_), channel_id=1, source_target_pairs={{6,4},{7,5},{14,12},{15,13},{22,20},{23,21},{30,28},{31,29}} | collective-permute-start | bytes 1572872 | tf_op jit(solution)/shard_map/ppermute | solution.py:582
  84.2 25.5 %collective-permute-start.5 = (bf16[1024,256]{1,0:T(8,128)(2,1)}, bf16[1024,256]{1,0:T(8,128)(2,1)}, u32[]{:S(2)}, u32[]{:S(2)}) collective-permute-start(bf16[1024,256]{1,0:T(8,128)(2,1)} %get-tuple-element.275.refs_3_), channel_id=1, source_target_pairs={{0,2},{1,3},{8,10},{9,11},{16,18},{17,19},{24,26},{25,27}} | collective-permute-start | bytes 1572872 | tf_op jit(solution)/shard_map/ppermute | solution.py:582
  86.3 23.4 %collective-permute-start.6 = (bf16[1024,256]{1,0:T(8,128)(2,1)}, bf16[1024,256]{1,0:T(8,128)(2,1)}, u32[]{:S(2)}, u32[]{:S(2)}) collective-permute-start(bf16[1024,256]{1,0:T(8,128)(2,1)} %get-tuple-element.275.refs_3_), channel_id=1, source_target_pairs={{6,4},{7,5},{14,12},{15,13},{22,20},{23,21},{30,28},{31,29}} | collective-permute-start | bytes 1572872 | tf_op jit(solution)/shard_map/ppermute | solution.py:582
  100.0 22.1 %collective-permute-start.10 = (bf16[1024,256]{1,0:T(8,128)(2,1)S(1)}, bf16[1024,256]{1,0:T(8,128)(2,1)S(1)}, u32[]{:S(2)}, u32[]{:S(2)}) collective-permute-start(bf16[1024,256]{1,0:T(8,128)(2,1)S(1)} %shard_map.210.refs_4_.refs_5_), channel_id=1, source_target_pairs={{6,4},{4,2},{7,5},{5,3},{14,12},{12,10},{15,13},{13,11},{22,20},{2... | collective-permute-start | bytes 1572872 | tf_op jit(solution)/shard_map/ppermute | solution.py:582
  131.4 37.9 %collective-permute-start.15 = (bf16[1024,1024]{1,0:T(8,128)(2,1)S(1)}, bf16[1024,1024]{1,0:T(8,128)(2,1)S(1)}, u32[]{:S(2)}, u32[]{:S(2)}) collective-permute-start(bf16[1024,1024]{1,0:T(8,128)(2,1)S(1)} %add_convert_fusion.2.dn_ref), channel_id=1, source_target_pairs={{0,1},{1,0},{2,3},{3,2},{4,5},{5,4},{6,7},{7,6},{8,9},{9,8},{10,11... | collective-permute-start | bytes 6291464 | tf_op jit(solution)/shard_map/ppermute | solution.py:618
  136.2 24.1 %collective-permute-start.11 = (bf16[1024,256]{1,0:T(8,128)(2,1)S(1)}, bf16[1024,256]{1,0:T(8,128)(2,1)S(1)}, u32[]{:S(2)}, u32[]{:S(2)}) collective-permute-start(bf16[1024,256]{1,0:T(8,128)(2,1)S(1)} %get-tuple-element.306.refs_4_), channel_id=1, source_target_pairs={{0,2},{2,4},{4,6},{1,3},{3,5},{5,7},{8,10},{10,12},{12,14},{9,11},... | collective-permute-start | bytes 1572872 | tf_op jit(solution)/shard_map/ppermute | solution.py:582
  149.8 24.5 %collective-permute-start.16 = (bf16[1024,256]{1,0:T(8,128)(2,1)}, bf16[1024,256]{1,0:T(8,128)(2,1)}, u32[]{:S(2)}, u32[]{:S(2)}) collective-permute-start(bf16[1024,256]{1,0:T(8,128)(2,1)} %get-tuple-element.312.refs_4_), channel_id=1, source_target_pairs={{0,2},{2,4},{4,6},{1,3},{3,5},{5,7},{8,10},{10,12},{12,14},{9,11},... | collective-permute-start | bytes 1572872 | tf_op jit(solution)/shard_map/ppermute | solution.py:582
  162.5 25.3 %collective-permute-start.18 = (bf16[1024,256]{1,0:T(8,128)(2,1)S(1)}, bf16[1024,256]{1,0:T(8,128)(2,1)S(1)}, u32[]{:S(2)}, u32[]{:S(2)}) collective-permute-start(bf16[1024,256]{1,0:T(8,128)(2,1)S(1)} %get-tuple-element.319.refs_4_), channel_id=1, source_target_pairs={{0,2},{2,4},{4,6},{1,3},{3,5},{5,7},{8,10},{10,12},{12,14},{9,11},... | collective-permute-start | bytes 1572872 | tf_op jit(solution)/shard_map/ppermute | solution.py:582
  179.5 30.1 %collective-permute-start.22 = (bf16[1024,256]{1,0:T(8,128)(2,1)S(1)}, bf16[1024,256]{1,0:T(8,128)(2,1)}, u32[]{:S(2)}, u32[]{:S(2)}) collective-permute-start(bf16[1024,256]{1,0:T(8,128)(2,1)S(1)} %get-tuple-element.326.refs_4_), channel_id=1, source_target_pairs={{0,2},{2,4},{4,6},{1,3},{3,5},{5,7},{8,10},{10,12},{12,14},{9,11},... | collective-permute-start | bytes 1572872 | tf_op jit(solution)/shard_map/ppermute | solution.py:582
  185.1 24.5 %collective-permute-start.23 = (bf16[1024,256]{1,0:T(8,128)(2,1)S(1)}, bf16[1024,256]{1,0:T(8,128)(2,1)}, u32[]{:S(2)}, u32[]{:S(2)}) collective-permute-start(bf16[1024,256]{1,0:T(8,128)(2,1)S(1)} %get-tuple-element.327.refs_5_), channel_id=1, source_target_pairs={{6,4},{4,2},{2,0},{7,5},{5,3},{3,1},{14,12},{12,10},{10,8},{15,13}... | collective-permute-start | bytes 1572872 | tf_op jit(solution)/shard_map/ppermute | solution.py:582
  190.1 36.6 %collective-permute-start.20 = (bf16[1024,256]{1,0:T(8,128)(2,1)S(1)}, bf16[1024,256]{1,0:T(8,128)(2,1)}, u32[]{:S(2)}, u32[]{:S(2)}) collective-permute-start(bf16[1024,256]{1,0:T(8,128)(2,1)S(1)} %get-tuple-element.333.refs_4_), channel_id=1, source_target_pairs={{0,2},{2,4},{4,6},{1,3},{3,5},{5,7},{8,10},{10,12},{12,14},{9,11},... | collective-permute-start | bytes 1572872 | tf_op jit(solution)/shard_map/ppermute | solution.py:582
  195.6 31.1 %collective-permute-start.21 = (bf16[1024,256]{1,0:T(8,128)(2,1)S(1)}, bf16[1024,256]{1,0:T(8,128)(2,1)}, u32[]{:S(2)}, u32[]{:S(2)}) collective-permute-start(bf16[1024,256]{1,0:T(8,128)(2,1)S(1)} %get-tuple-element.334.refs_5_), channel_id=1, source_target_pairs={{6,4},{4,2},{2,0},{7,5},{5,3},{3,1},{14,12},{12,10},{10,8},{15,13}... | collective-permute-start | bytes 1572872 | tf_op jit(solution)/shard_map/ppermute | solution.py:582
  213.6 29.9 %collective-permute-start.26 = (bf16[1024,256]{1,0:T(8,128)(2,1)S(1)}, bf16[1024,256]{1,0:T(8,128)(2,1)S(1)}, u32[]{:S(2)}, u32[]{:S(2)}) collective-permute-start(bf16[1024,256]{1,0:T(8,128)(2,1)S(1)} %get-tuple-element.349.refs_4_), channel_id=1, source_target_pairs={{0,2},{2,4},{4,6},{1,3},{3,5},{5,7},{8,10},{10,12},{12,14},{9,11},... | collective-permute-start | bytes 1572872 | tf_op jit(solution)/shard_map/ppermute | solution.py:582
  218.3 25.1 %collective-permute-start.27 = (bf16[1024,256]{1,0:T(8,128)(2,1)S(1)}, bf16[1024,256]{1,0:T(8,128)(2,1)S(1)}, u32[]{:S(2)}, u32[]{:S(2)}) collective-permute-start(bf16[1024,256]{1,0:T(8,128)(2,1)S(1)} %get-tuple-element.350.refs_5_), channel_id=1, source_target_pairs={{6,4},{4,2},{2,0},{7,5},{5,3},{3,1},{14,12},{12,10},{10,8},{15,13}... | collective-permute-start | bytes 1572872 | tf_op jit(solution)/shard_map/ppermute | solution.py:582
  230.6 28.2 %collective-permute-start.24 = (bf16[1024,256]{1,0:T(8,128)(2,1)S(1)}, bf16[1024,256]{1,0:T(8,128)(2,1)S(1)}, u32[]{:S(2)}, u32[]{:S(2)}) collective-permute-start(bf16[1024,256]{1,0:T(8,128)(2,1)S(1)} %get-tuple-element.359.refs_4_), channel_id=1, source_target_pairs={{0,2},{2,4},{4,6},{1,3},{3,5},{5,7},{8,10},{10,12},{12,14},{9,11},... | collective-permute-start | bytes 1572872 | tf_op jit(solution)/shard_map/ppermute | solution.py:582
  235.4 23.5 %collective-permute-start.25 = (bf16[1024,256]{1,0:T(8,128)(2,1)S(1)}, bf16[1024,256]{1,0:T(8,128)(2,1)S(1)}, u32[]{:S(2)}, u32[]{:S(2)}) collective-permute-start(bf16[1024,256]{1,0:T(8,128)(2,1)S(1)} %get-tuple-element.360.refs_5_), channel_id=1, source_target_pairs={{6,4},{4,2},{2,0},{7,5},{5,3},{3,1},{14,12},{12,10},{10,8},{15,13}... | collective-permute-start | bytes 1572872 | tf_op jit(solution)/shard_map/ppermute | solution.py:582
  245.7 25.0 %collective-permute-start.30 = (bf16[1024,256]{1,0:T(8,128)(2,1)S(1)}, bf16[1024,256]{1,0:T(8,128)(2,1)S(1)}, u32[]{:S(2)}, u32[]{:S(2)}) collective-permute-start(bf16[1024,256]{1,0:T(8,128)(2,1)S(1)} %get-tuple-element.369.refs_4_), channel_id=1, source_target_pairs={{0,2},{2,4},{4,6},{1,3},{3,5},{5,7},{8,10},{10,12},{12,14},{9,11},... | collective-permute-start | bytes 1572872 | tf_op jit(solution)/shard_map/ppermute | solution.py:582
  310.1 35.4 %collective-permute-start.41 = (bf16[1024,512]{1,0:T(8,128)(2,1)S(1)}, bf16[1024,512]{1,0:T(8,128)(2,1)S(1)}, u32[]{:S(2)}, u32[]{:S(2)}) collective-permute-start(bf16[1024,512]{1,0:T(8,128)(2,1)S(1)} %get-tuple-element.427), channel_id=1, source_target_pairs={{8,0},{9,1},{10,2},{11,3},{12,4},{13,5},{14,6},{15,7}} | collective-permute-start | bytes 3145736 | tf_op jit(solution)/shard_map/ppermute | solution.py:645
  311.4 49.6 %collective-permute-start.42 = (bf16[1024,512]{1,0:T(8,128)(2,1)S(1)}, bf16[1024,512]{1,0:T(8,128)(2,1)S(1)}, u32[]{:S(2)}, u32[]{:S(2)}) collective-permute-start(bf16[1024,512]{1,0:T(8,128)(2,1)S(1)} %get-tuple-element.427), channel_id=1, source_target_pairs={{16,0},{17,1},{18,2},{19,3},{20,4},{21,5},{22,6},{23,7}} | collective-permute-start | bytes 3145736 | tf_op jit(solution)/shard_map/ppermute | solution.py:645
  320.6 40.5 %collective-permute-start.43 = (bf16[1024,512]{1,0:T(8,128)(2,1)S(1)}, bf16[1024,512]{1,0:T(8,128)(2,1)S(1)}, u32[]{:S(2)}, u32[]{:S(2)}) collective-permute-start(bf16[1024,512]{1,0:T(8,128)(2,1)S(1)} %get-tuple-element.427), channel_id=1, source_target_pairs={{24,0},{25,1},{26,2},{27,3},{28,4},{29,5},{30,6},{31,7}} | collective-permute-start | bytes 3145736 | tf_op jit(solution)/shard_map/ppermute | solution.py:645
  337.6 25.6 %collective-permute-start.44 = (bf16[1024,256]{1,0:T(8,128)(2,1)S(1)}, bf16[1024,256]{1,0:T(8,128)(2,1)S(1)}, u32[]{:S(2)}, u32[]{:S(2)}) collective-permute-start(bf16[1024,256]{1,0:T(8,128)(2,1)S(1)} %get-tuple-element.417.refs_4_), channel_id=1, source_target_pairs={{0,2},{2,4},{4,6},{1,3},{3,5},{5,7},{8,10},{10,12},{12,14},{9,11},... | collective-permute-start | bytes 1572872 | tf_op jit(solution)/shard_map/ppermute | solution.py:582
  366.8 26.9 %collective-permute-start.48 = (bf16[1024,1024]{1,0:T(8,128)(2,1)S(1)}, bf16[1024,1024]{1,0:T(8,128)(2,1)S(1)}, u32[]{:S(2)}, u32[]{:S(2)}) collective-permute-start(bf16[1024,1024]{1,0:T(8,128)(2,1)S(1)} %add_convert_fusion.dn_ref), channel_id=1, source_target_pairs={{0,1},{1,0},{2,3},{3,2},{4,5},{5,4},{6,7},{7,6},{8,9},{9,8},{10,11... | collective-permute-start | bytes 6291464 | tf_op jit(solution)/shard_map/ppermute | solution.py:618
  372.6 25.0 %collective-permute-start.51 = (bf16[1024,256]{1,0:T(8,128)(2,1)S(1)}, bf16[1024,256]{1,0:T(8,128)(2,1)S(1)}, u32[]{:S(2)}, u32[]{:S(2)}) collective-permute-start(bf16[1024,256]{1,0:T(8,128)(2,1)S(1)} %get-tuple-element.433.refs_4_), channel_id=1, source_target_pairs={{0,2},{2,4},{4,6},{1,3},{3,5},{5,7},{8,10},{10,12},{12,14},{9,11},... | collective-permute-start | bytes 1572872 | tf_op jit(solution)/shard_map/ppermute | solution.py:582
  (104 other events, 1138.8 us)

commit v2 on v1

v2 whole, which is shorter than its diff:
```python
import jax
import jax.numpy as jnp
from jax import lax
from jax.experimental import pallas as pl
from jax.experimental.pallas import tpu as pltpu
from jax.sharding import PartitionSpec as P

HD = 64
WINDOW = 512
EPSILON = 1e-06
MASKED = -1e30
F32 = jnp.float32
BF16 = jnp.bfloat16
MIB = 1024 * 1024
UNITS = 384
CHUNK = 256


def dot(left, right):
    return lax.dot_general(left, right, (((1,), (0,)), ((), ())), preferred_element_type=F32)


def dot_nt(left, right):
    return lax.dot_general(left, right, (((1,), (1,)), ((), ())), preferred_element_type=F32)


def dot_tn(left, right):
    return lax.dot_general(left, right, (((0,), (0,)), ((), ())), preferred_element_type=F32)


def call(kernel, grid, ins, outs, args, vmem, scratch=(), into=None):
    into = {o: array for o, array in (into or {}).items() if array is not None}
    ins, args, n = list(ins), list(args), len(args)
    body = kernel
    if into:
        ins += [pl.BlockSpec(memory_space=pl.ANY)] * len(into)
        args += list(into.values())

        def body(*refs):
            kernel(*refs[:n], *refs[n + len(into) :])

    return pl.pallas_call(
        body,
        grid=grid,
        in_specs=ins,
        out_specs=[spec for spec, _, _ in outs],
        out_shape=[jax.ShapeDtypeStruct(shape, dtype) for _, shape, dtype in outs],
        scratch_shapes=list(scratch),
        input_output_aliases={n + j: o for j, o in enumerate(into)},
        compiler_params=pltpu.CompilerParams(vmem_limit_bytes=vmem * MIB),
        cost_estimate=pl.CostEstimate(flops=1, bytes_accessed=1, transcendentals=0),
    )(*args)


def rows(block, width):
    return pl.BlockSpec((block, width), lambda i: (i, 0))


def whole(*shape):
    return pl.BlockSpec(shape, lambda i: (0,) * len(shape))


def columns(height, block, first=0):
    return pl.BlockSpec((height, block), lambda i: (0, i + first))


def value_kernel(x_ref, gain_ref, w_ref, normed_ref, *value_refs):
    x = x_ref[...].astype(F32)
    inv_rms = lax.rsqrt(jnp.mean(x * x, axis=1, keepdims=True) + EPSILON)
    normed = (x * inv_rms * gain_ref[...]).astype(BF16)
    normed_ref[...] = normed
    values = dot(normed, w_ref[...]).astype(BF16)
    cut = values.shape[1] // len(value_refs)
    for j, ref in enumerate(value_refs):
        ref[...] = values[:, j * cut : (j + 1) * cut]


def value_proj(x, gain, w_value):
    tokens, width = x.shape
    half = w_value.shape[1] // 2
    block = 256
    return call(
        value_kernel,
        (tokens // block,),
        [rows(block, width), whole(1, width), whole(width, 2 * half)],
        [(rows(block, width), (tokens, width), BF16)] + [(rows(block, half), (tokens, half), BF16)] * 2,
        (x, gain, w_value),
        60,
    )


def swap_halves(u):
    lane = lax.broadcasted_iota(jnp.int32, u.shape, 1) % HD
    return jnp.where(lane < HD // 2, pltpu.roll(u, 128 - HD // 2, 1), pltpu.roll(u, HD // 2, 1))


def query_key_kernel(n_ref, wq_ref, wk_ref, cos_ref, sin_ref, q_ref, k_ref, turned_ref):
    normed = n_ref[...]
    cos, sin = cos_ref[...], sin_ref[...]
    for w_ref, o_ref in ((wq_ref, q_ref), (wk_ref, k_ref)):
        u = dot(normed, w_ref[...])
        for lo in range(0, u.shape[1], 128):
            part = u[:, lo : lo + 128]
            o_ref[:, lo : lo + 128] = (part * cos + swap_halves(part) * sin).astype(BF16)
    turned_ref[...] = normed.T


def query_key_proj(normed, w_query, w_key, cos, sin):
    tokens, width = normed.shape
    out = w_query.shape[1]
    block = 256
    return call(
        query_key_kernel,
        (tokens // block,),
        [rows(block, width), whole(width, out), whole(width, out), rows(block, 128), rows(block, 128)],
        [
            (rows(block, out), (tokens, out), BF16),
            (rows(block, out), (tokens, out), BF16),
            (columns(width, block), (width, tokens), BF16),
        ],
        (normed, w_query, w_key, cos, sin),
        32,
    )


def row_starts(len_ref, first, count):
    place = first + lax.broadcasted_iota(jnp.int32, (count, 1), 0)
    start = jnp.zeros((count, 1), jnp.int32)
    end = 0
    for j in range(len_ref.shape[1]):
        end = end + len_ref[0, j]
        start = jnp.where(place >= end, end, start)
    return place, start


def band(len_ref, first, count):
    low = max(0, first - WINDOW)
    place, start = row_starts(len_ref, first, count)
    col = low + lax.broadcasted_iota(jnp.int32, (count, first + count - low), 1)
    return low, (col >= start) & (col <= place)


def head_masks(count):
    lane = lax.broadcasted_iota(jnp.int32, (count, 2 * HD), 1)
    return lane < HD, lane >= HD


def probs_kernel(len_ref, q_ref, k_ref, probs_ref):
    tokens = q_ref.shape[0]
    block = 256
    for at in range(0, tokens, block):
        low, allowed = band(len_ref, at, block)
        queries = q_ref[at : at + block, :] * BF16(HD**-0.5)
        keys = k_ref[low : at + block, :]
        for h, mask in enumerate(head_masks(block)):
            scores = dot_nt(jnp.where(mask, queries, BF16(0)), keys)
            scores = jnp.where(allowed, scores, MASKED)
            exps = jnp.exp(scores - jnp.max(scores, axis=1, keepdims=True))
            total = jnp.sum(exps, axis=1, keepdims=True)
            probs_ref[h, at : at + block, : at + block - low] = (exps * (1.0 / total)).astype(BF16)


def band_width(tokens):
    return min(tokens, WINDOW + 256)


def probabilities(lengths, queries, keys):
    tokens, width = queries.shape
    pair = columns(tokens, 2 * HD)
    wide = band_width(tokens)
    return call(
        probs_kernel,
        (width // (2 * HD),),
        [pl.BlockSpec(memory_space=pltpu.SMEM), pair, pair],
        [(pl.BlockSpec((2, tokens, wide), lambda i: (i, 0, 0)), (width // HD, tokens, wide), BF16)],
        (lengths, queries, keys),
        40,
    )[0]


def heads_kernel(n_arrived, places, section_ref, *refs):
    probs_ref, own_refs, arrived = refs[0], refs[1:3], refs[3 : 3 + n_arrived]
    w_ref, heads_ref, mixed_ref, part_ref = refs[3 + n_arrived :]
    block = heads_ref.shape[0]
    half = own_refs[0].shape[1]
    step = pl.program_id(0)

    for section, sources in enumerate(places):

        @pl.when((step == 0) & (section_ref[0] == section))
        def _():
            for j, source in enumerate(sources):
                first_ref = own_refs[j] if source is None else arrived[source]
                mixed_ref[:, j * half : (j + 1) * half] = (
                    0.5 * own_refs[j][...].astype(F32) + 0.5 * first_ref[...].astype(F32)
                ).astype(BF16)

    first_mask, _ = head_masks(block)
    for i in range(own_refs[0].shape[0] // block):
        at = i * block
        low = max(0, at - WINDOW)

        @pl.when(step == i)
        def _():
            for pair in range(heads_ref.shape[1] // (2 * HD)):
                lanes = slice(pair * 2 * HD, (pair + 1) * 2 * HD)
                values = mixed_ref[low : at + block, lanes]
                both = [dot(probs_ref[2 * pair + h, :, : at + block - low], values) for h in range(2)]
                heads_ref[:, lanes] = jnp.where(first_mask, both[0], both[1]).astype(BF16)

    part_ref[...] = dot(heads_ref[...], w_ref[...]).astype(BF16)


def heads_proj(section, probs, own, arrived, places, w_out):
    tokens, half = own[0].shape
    width, model = w_out.shape
    n_heads, _, wide = probs.shape
    block = 256
    return call(
        lambda *refs: heads_kernel(len(arrived), places, *refs),
        (tokens // block,),
        [pl.BlockSpec(memory_space=pltpu.SMEM), pl.BlockSpec((n_heads, block, wide), lambda i: (0, i, 0))]
        + [whole(tokens, half)] * (2 + len(arrived))
        + [whole(width, model)],
        [
            (rows(block, width), (tokens, width), BF16),
            (whole(tokens, width), (tokens, width), BF16),
            (rows(block, model), (tokens, model), BF16),
        ],
        (section.astype(jnp.int32)[None], probs, *own, *arrived, w_out),
        40,
    )


def attend_back_kernel(
    q_ref, k_ref, mixed_ref, probs_ref, attn_ref, w_ref, cos_ref, sin_ref, dq_ref, dk_ref, half_ref, grad_ref, key_acc, value_acc
):
    tokens = q_ref.shape[0]
    block = 256
    key_acc[...] = jnp.zeros_like(key_acc)
    value_acc[...] = jnp.zeros_like(value_acc)
    grad_ref[...] = dot_nt(attn_ref[...], w_ref[...]).astype(BF16)

    def turned_back(grads, at, count):
        cos, sin = cos_ref[at : at + count, :], sin_ref[at : at + count, :]
        return (grads * cos - swap_halves(grads) * sin).astype(BF16)

    masks = head_masks(block)
    for at in range(0, tokens, block):
        low = max(0, at - WINDOW)
        grads = grad_ref[at : at + block, :]
        queries_turned = (q_ref[at : at + block, :] * BF16(HD**-0.5)).T
        grads_turned = grads.T
        keys = k_ref[low : at + block, :]
        values = mixed_ref[low : at + block, :]
        parts = []
        for h, mask in enumerate(masks):
            lanes = slice(h * HD, (h + 1) * HD)
            probs_low = probs_ref[h, at : at + block, : at + block - low]
            probs = probs_low.astype(F32)
            grad_probs = dot_nt(jnp.where(mask, grads, BF16(0)), values)
            inner = jnp.sum(probs * grad_probs, axis=1, keepdims=True)
            grad_scores = (probs * (grad_probs - inner)).astype(BF16)
            parts.append(dot(grad_scores, keys))
            key_acc[lanes, low : at + block] += dot(queries_turned[lanes], grad_scores)
            value_acc[lanes, low : at + block] += dot(grads_turned[lanes], probs_low)
        grad_query = jnp.where(masks[0], parts[0], parts[1]) * HD**-0.5
        dq_ref[at : at + block, :] = turned_back(grad_query, at, block)
    for at in range(0, tokens, block):
        dk_ref[at : at + block, :] = turned_back(key_acc[:, at : at + block].T, at, block)
        half_ref[at : at + block, :] = (0.5 * value_acc[:, at : at + block].T).astype(BF16)


def attend_back(queries, keys, mixed, probs, grad_attn, w_out, cos, sin, first, count, into):
    tokens, width = queries.shape
    model = w_out.shape[1]
    pair = columns(tokens, 2 * HD, first)
    wide = probs.shape[2]
    return call(
        attend_back_kernel,
        (count,),
        [pair, pair, pair, pl.BlockSpec((2, tokens, wide), lambda i: (i + first, 0, 0)), whole(tokens, model)]
        + [pl.BlockSpec((2 * HD, model), lambda i: (i + first, 0)), whole(tokens, 128), whole(tokens, 128)],
        [(pair, (tokens, width), BF16)] * 3,
        (queries, keys, mixed, probs, grad_attn, w_out, cos, sin),
        26,
        scratch=[pltpu.VMEM((tokens, 2 * HD), BF16)] + [pltpu.VMEM((2 * HD, tokens), F32)] * 2,
        into=dict(enumerate(into)),
    )


def unit_acts(normed, grad_out, w_gate, w_up, w_down, hidden_ref, dg_ref, du_ref):
    gate = dot(normed, w_gate)
    up = dot(normed, w_up)
    grad_hidden = dot_nt(grad_out, w_down)
    sig = jax.nn.sigmoid(gate)
    silu = gate * sig
    hidden = (silu * up).astype(BF16)
    hidden_ref[...] = hidden
    dg_ref[...] = (grad_hidden * up * (sig * (1.0 + gate * (1.0 - sig)))).astype(BF16)
    du_ref[...] = (grad_hidden * silu).astype(BF16)
    return hidden


def entry_kernel(n, x_ref, own_ref, other_ref, gain_ref, grad_ref, *refs):
    gates, ups, downs = (refs[j * n : (j + 1) * n] for j in range(3))
    normed_ref, hidden_ref, dg_ref, du_ref, gwd_ref, acc = refs[3 * n :]
    step = pl.program_id(0)
    middle = x_ref[...].astype(F32) + (own_ref[...].astype(F32) + other_ref[...].astype(F32))
    inv_rms = lax.rsqrt(jnp.mean(middle * middle, axis=1, keepdims=True) + EPSILON)
    normed = (middle * inv_rms * gain_ref[...]).astype(BF16)
    normed_ref[...] = normed
    w_gate, w_up = (jnp.concatenate([r[...] for r in group], axis=1) for group in (gates, ups))
    w_down = jnp.concatenate([r[...] for r in downs], axis=0)
    grad_out = grad_ref[...]
    hidden = unit_acts(normed, grad_out, w_gate, w_up, w_down, hidden_ref, dg_ref, du_ref)
    term = dot(hidden.T, grad_out)
    last = pl.num_programs(0) - 1

    @pl.when(step == 0)
    def _():
        acc[...] = term

    @pl.when((step > 0) & (step < last))
    def _():
        acc[...] += term

    @pl.when(step == last)
    def _():
        gwd_ref[...] = (acc[...] + term).astype(BF16)


def entry(x, own, other, gain, grad_out, w_gate, w_up, w_down, units):
    tokens, width = x.shape
    block = 512
    n = units // 128
    at = w_gate.shape[1] // 128 - n

    def wide(j):
        return pl.BlockSpec((width, 128), lambda i: (0, at + j))

    def tall(j):
        return pl.BlockSpec((128, width), lambda i: (at + j, 0))

    return call(
        lambda *refs: entry_kernel(n, *refs),
        (tokens // block,),
        [rows(block, width)] * 3
        + [whole(1, width), rows(block, width)]
        + [wide(j) for j in range(n)] * 2
        + [tall(j) for j in range(n)],
        [(rows(block, width), (tokens, width), BF16)]
        + [(rows(block, units), (tokens, units), BF16)] * 3
        + [(whole(units, width), (units, width), BF16)],
        (x, own, other, gain, grad_out, *[w_gate] * n, *[w_up] * n, *[w_down] * n),
        60,
        scratch=[pltpu.VMEM((units, width), F32)],
    )


def ffn_kernel(normed_ref, grad_ref, wg_ref, wu_ref, wd_ref, hidden_ref, dg_ref, du_ref, gwd_ref):
    grad_out = grad_ref[...]
    hidden = unit_acts(normed_ref[...], grad_out, wg_ref[...], wu_ref[...], wd_ref[...], hidden_ref, dg_ref, du_ref)
    gwd_ref[...] = dot(hidden.T, grad_out).astype(BF16)


def ffn(normed, grad_out, w_gate, w_up, w_down, units, number, count, into):
    tokens, width = normed.shape
    return call(
        ffn_kernel,
        (1,),
        [whole(tokens, width)] * 2
        + [columns(width, units, number)] * 2
        + [pl.BlockSpec((units, width), lambda i: (number, 0))],
        [(columns(tokens, units, number), (tokens, units * count), BF16)] * 3
        + [(whole(units, width), (units, width), BF16)],
        (normed, grad_out, w_gate, w_up, w_down),
        40,
        into=dict(enumerate(into)),
    )


def turn_kernel(ref, out_ref):
    out_ref[...] = ref[...].T


def turned(array):
    tall, wide = array.shape
    block = 256
    return call(
        turn_kernel, (tall // block,), [rows(block, wide)], [(columns(wide, block), (wide, tall), array.dtype)], (array,), 24
    )[0]


def weight_grads_kernel(turned_ref, *refs):
    half = len(refs) // 2
    for d_ref, o_ref in zip(refs[:half], refs[half:]):
        o_ref[...] = dot(turned_ref[...], d_ref[...]).astype(BF16)


def weight_grads(left, grads, units, numbers):
    width, tokens = left.shape
    block = 512
    return call(
        weight_grads_kernel,
        (width // block,),
        [rows(block, tokens)] + [pl.BlockSpec((tokens, units), lambda i, at=at: (0, at)) for at in numbers],
        [(rows(block, units), (width, units), BF16)] * len(grads),
        (left, *grads),
        20,
    )


def row_grads_kernel(left_ref, right_ref, out_ref, left):
    @pl.when(pl.program_id(0) == 0)
    def _():
        left[...] = left_ref[...].T

    out_ref[...] = dot(left[...], right_ref[...]).astype(BF16)


def row_grads(left, right, number):
    tokens, width = right.shape
    block = 512
    return call(
        row_grads_kernel,
        (width // block,),
        [pl.BlockSpec((tokens, CHUNK), lambda i: (0, number)), columns(tokens, block)],
        [(columns(CHUNK, block), (CHUNK, width), BF16)],
        (left, right),
        24,
        scratch=[pltpu.VMEM((CHUNK, tokens), BF16)],
    )[0]


def products_kernel(turn, counts, *refs):
    out_ref = refs[-1]
    n = sum(counts)
    lefts, weights = list(refs[:n]), refs[n:-1]
    total = None
    for count, w_ref in zip(counts, weights):
        at = 0
        for _ in range(count):
            left = lefts.pop(0)
            deep = left.shape[1]
            if turn:
                term = dot_nt(left[...], w_ref[:, at : at + deep])
            else:
                term = dot(left[...], w_ref[at : at + deep, :])
            at += deep
            total = term if total is None else total + term
    out_ref[...] = total.astype(BF16)


def products(pairs, turn):
    counts = [len(lefts) for lefts, _ in pairs]
    lefts = [left for group, _ in pairs for left in group]
    weights = [w for _, w in pairs]
    tokens = lefts[0].shape[0]
    width = weights[0].shape[0 if turn else 1]
    block = 256
    specs = [rows(block, w.shape[1]) if turn else columns(w.shape[0], block) for w in weights]
    return call(
        lambda *refs: products_kernel(turn, counts, *refs),
        (width // block,),
        [whole(*left.shape) for left in lefts] + specs,
        [(columns(tokens, block), (tokens, width), BF16)],
        (*lefts, *weights),
        26,
    )[0]


def summed(refs):
    total = refs[0][...].astype(F32)
    if len(refs) > 1:
        total = total + (refs[1][...].astype(F32) + refs[2][...].astype(F32))
    return total


def norm_back_kernel(n, low, dn_ref, do_ref, gain_ref, base_ref, *refs):
    values = summed(refs[:n])
    out_ref, more, gain_grad_ref = refs[n], refs[n + 1 : -1], refs[-1]
    grad_normed = dn_ref[...].astype(F32) + do_ref[...].astype(F32)
    inv_rms = lax.rsqrt(jnp.mean(values * values, axis=1, keepdims=True) + EPSILON)
    weighted = grad_normed * gain_ref[...]
    inner = jnp.mean(weighted * values, axis=1, keepdims=True)
    out = base_ref[...].astype(F32) + inv_rms * weighted - values * (inv_rms * inv_rms * inv_rms) * inner
    out_ref[...] = out
    if low:
        more[0][...] = out.astype(BF16)

    @pl.when(pl.program_id(0) == 0)
    def _():
        gain_grad_ref[...] = jnp.zeros_like(gain_grad_ref)

    gain_grad_ref[...] += jnp.sum(grad_normed * values * inv_rms, axis=0, keepdims=True)


def norm_back(own, other, values, gain, base, low):
    tokens, width = own.shape
    block = 256
    outs = [(rows(block, width), (tokens, width), F32)]
    if low:
        outs.append((rows(block, width), (tokens, width), BF16))
    outs.append((whole(1, width), (1, width), F32))
    return call(
        lambda *refs: norm_back_kernel(len(values), low, *refs),
        (tokens // block,),
        [rows(block, width)] * 2 + [whole(1, width)] + [rows(block, width)] * (1 + len(values)),
        outs,
        (own, other, gain, base, *values),
        28,
    )


def result_kernel(own_ref, other_ref, *refs):
    refs[-1][...] = (summed(refs[:-1]) + (own_ref[...].astype(F32) + other_ref[...].astype(F32))).astype(BF16)


def block_result(own, other, values):
    tokens, width = own.shape
    block = 256
    return call(
        result_kernel,
        (tokens // block,),
        [rows(block, width)] * (2 + len(values)),
        [(rows(block, width), (tokens, width), BF16)],
        (own, other, *values),
        24,
    )[0]


def relay_kernel(section_ref, half_ref, left_ref, right_ref, out_ref):
    cut = left_ref.shape[1]
    out_ref[...] = half_ref[...]
    for section, ref, lanes in ((1, left_ref, slice(0, cut)), (2, right_ref, slice(cut, 2 * cut))):

        @pl.when(section_ref[0] == section)
        def _():
            out_ref[:, lanes] = (half_ref[:, lanes].astype(F32) + ref[...].astype(F32)).astype(BF16)


def relayed(section, half, left, right):
    tokens, width = half.shape
    block = 512
    return call(
        relay_kernel,
        (tokens // block,),
        [pl.BlockSpec(memory_space=pltpu.SMEM), rows(block, width)] + [rows(block, width // 2)] * 2,
        [(rows(block, width), (tokens, width), BF16)],
        (section.astype(jnp.int32)[None], half, left, right),
        16,
    )[0]


def first_grad_kernel(section_ref, half_ref, *refs):
    out_ref = refs[-1]

    @pl.when(section_ref[0] == 0)
    def _():
        half = half_ref[...].astype(F32)
        total = half
        for ref in refs[:-1]:
            total = total + ref[...].astype(F32)
        out_ref[...] = (half + total).astype(BF16)

    @pl.when(section_ref[0] != 0)
    def _():
        out_ref[...] = half_ref[...]


def first_grad(section, half, arrived):
    tokens, width = half.shape
    block = 256
    return call(
        first_grad_kernel,
        (tokens // block,),
        [pl.BlockSpec(memory_space=pltpu.SMEM)] + [rows(block, width)] * (1 + len(arrived)),
        [(rows(block, width), (tokens, width), BF16)],
        (section.astype(jnp.int32)[None], half, *arrived),
        24,
    )[0]


def tie(*values):
    return lax.optimization_barrier(values)


def chosen_call(kernel, grid, flags, ins, out, shape, dtype, args, into=None):
    def spec(block, flag):
        return pl.BlockSpec(block, lambda i, j, flags: (i * flags[flag], j * flags[flag]))

    block, at = out
    held = [] if into is None else [into]
    n = len(args)

    def body(flags_ref, *refs):
        kernel(flags_ref, *refs[:n], *refs[n + len(held) :])

    return pl.pallas_call(
        body,
        grid_spec=pltpu.PrefetchScalarGridSpec(
            num_scalar_prefetch=1,
            grid=grid,
            in_specs=[spec(*one) for one in ins] + [pl.BlockSpec(memory_space=pl.ANY)] * len(held),
            out_specs=pl.BlockSpec(block, lambda i, j, flags: at(i, j)),
        ),
        out_shape=jax.ShapeDtypeStruct(shape, dtype),
        input_output_aliases={1 + n: 0} if held else {},
        compiler_params=pltpu.CompilerParams(vmem_limit_bytes=10 * MIB),
        cost_estimate=pl.CostEstimate(flops=1, bytes_accessed=1, transcendentals=0),
    )(flags, *args, *held)


MID, END = 0, 1


def add_kernel(flags_ref, one_ref, two_ref, out_ref):
    @pl.when(flags_ref[MID] == 1)
    def _():
        out_ref[...] = (one_ref[...].astype(F32) + two_ref[...].astype(F32)).astype(BF16)


def put_kernel(flags_ref, mid_ref, end_ref, out_ref):
    @pl.when(flags_ref[MID] == 1)
    def _():
        out_ref[...] = mid_ref[...].astype(F32)

    @pl.when(flags_ref[END] == 1)
    def _():
        out_ref[...] = end_ref[...].astype(F32)


class Line:
    def __init__(self, axis, size, shapes, depth=3):
        self.axis, self.size, self.shapes, self.depth = axis, size, shapes, depth
        place = lax.axis_index(axis)
        end = (place == 0) | (place == 3)
        self.flags = jnp.stack([jnp.logical_not(end), end]).astype(jnp.int32)
        self.parts, self.places = [], []
        self.inward, self.across, self.outward, self.half, self.total = {}, {}, {}, {}, {}
        self.outs = {name: None for name in shapes}
        self.at = self.started = 0
        self.clock = []

    def after(self, *values):
        if not self.clock:
            return values if len(values) > 1 else values[0]
        held = tie(*values, *self.clock)[: len(values)]
        return held if len(values) > 1 else held[0]

    def mark(self, *values):
        self.clock = list(values)

    def push(self, part, *place):
        self.parts.append(part)
        self.places.append(place)
        self.start()

    def start(self):
        while self.size == 4 and self.started < len(self.parts) and self.started < self.at + self.depth:
            i = self.started
            self.parts[i] = self.after(self.parts[i])
            self.inward[i] = lax.ppermute(self.parts[i], self.axis, [(0, 1), (3, 2)])
            self.started += 1

    def add(self, one, two):
        tall, wide = one.shape
        block = (min(tall, 512), wide)
        ins = [(block, MID)] * 2
        return chosen_call(
            add_kernel, (tall // block[0], 1), self.flags, ins, (block, lambda i, j: (i, j)), one.shape, BF16, (one, two)
        )

    def step(self, drain=False):
        i, n = self.at, len(self.parts)
        if self.size != 4 or i >= n and not drain:
            return
        self.at += 1
        if i < n:
            part, arrived = self.after(self.parts[i], self.inward[i])
            self.half[i] = self.add(part, arrived)
            self.across[i] = lax.ppermute(self.half[i], self.axis, [(1, 2), (2, 1)])
            self.mark(self.half[i])
        if 0 <= i - 1 < n:
            half, arrived = self.after(self.half[i - 1], self.across[i - 1])
            self.total[i - 1] = self.add(half, arrived)
            self.outward[i - 1] = lax.ppermute(self.total[i - 1], self.axis, [(1, 0), (2, 3)])
            self.mark(self.total[i - 1])
        self.start()
        if 0 <= i - 2 < n:
            total, arrived = self.after(self.total[i - 2], self.outward[i - 2])
            name, block, at = self.places[i - 2]
            grid = tuple(s // b for s, b in zip(total.shape, block))
            self.outs[name] = chosen_call(
                put_kernel,
                grid,
                self.flags,
                [(block, MID), (block, END)],
                (block, at),
                self.shapes[name],
                F32,
                (total, arrived),
                self.outs[name],
            )
            self.mark(self.outs[name])

    def finish(self):
        if self.size == 4:
            while self.at < len(self.parts) + 2:
                self.step(True)
            return
        for part, (name, block, at) in zip(self.parts, self.places):
            if self.outs[name] is None:
                self.outs[name] = jnp.zeros(self.shapes[name], F32)
            where = tuple(b * o for b, o in zip(block, at(0, 0)))
            self.outs[name] = lax.dynamic_update_slice(self.outs[name], lax.psum(part, self.axis).astype(F32), where)


def tables(lengths_row, tokens):
    seqs = lengths_row.shape[0]
    slot = jnp.arange(seqs, dtype=jnp.int32)
    ends = jnp.sum(jnp.where(slot[None, :] <= slot[:, None], lengths_row[None, :], 0), axis=1)
    places = jnp.arange(tokens, dtype=jnp.int32)
    start = jnp.sum(jnp.where(places[:, None] >= ends[None, :], lengths_row[None, :], 0), axis=1)
    position = (places - start).astype(F32)
    inv_freq = 10000.0 ** (-(jnp.arange(HD // 2, dtype=F32) * 2.0 / HD))
    angles = position[:, None] * inv_freq[None, :]
    cos, sin = jnp.cos(angles), jnp.sin(angles)
    return jnp.concatenate([cos] * 4, axis=1), jnp.concatenate([-sin, sin, -sin, sin], axis=1)


def exchange(part, axis):
    return lax.ppermute(part, axis, [(0, 1), (1, 0)])


def shards(sizes, *args):
    (x, lengths, gain_attn, w_query, w_key, w_value, w_out, gain_ffn, w_gate, w_up, w_down, grad_out) = args
    x, w_query, w_key, w_value, w_out, w_gate, w_up, w_down, grad_out = (
        a[0] for a in (x, w_query, w_key, w_value, w_out, w_gate, w_up, w_down, grad_out)
    )
    tokens, width = x.shape
    units = w_gate.shape[1]
    n_blocks = (units - 1) // UNITS
    rest = units - n_blocks * UNITS
    n_sections = sizes["section"]
    section = lax.axis_index("section")
    outputs = {"query": w_query, "key": w_key, "value": w_value, "out": w_out, "gate": w_gate, "up": w_up, "down": w_down}
    shapes = {name: w.shape for name, w in outputs.items()}
    shapes["gains"] = (16, width)
    line = Line("dp", sizes["dp"], shapes)

    def put_columns(name, first, wide):
        return name, (512, wide), lambda i, j: (i, first + j)

    def put_rows(name, first, tall):
        return name, (tall, width), lambda i, j: (first + i, 0)

    normed, *own = value_proj(x, gain_attn, w_value)

    def send(block, *pairs):
        return lax.ppermute(block, "section", list(pairs))

    relay = n_sections == 4
    if relay:
        one, two = send(own[0], (0, 1)), send(own[1], (0, 2))
    cos, sin = tables(lengths[0], tokens)
    queries, keys, turned_attn = query_key_proj(normed, w_query, w_key, cos, sin)
    if relay:
        one, two, queries = tie(one, two, queries)
        three = send(jnp.where(section == 0, own[1], one), (0, 1), (1, 3))
        four = send(jnp.where(section == 0, own[0], two), (0, 2), (2, 3))
        arrived = [one, two, three, four]
        places = [(None, None), (0, 2), (3, 1), (2, 3)]
    else:
        arrived = [send(half, (0, s)) for s in range(1, n_sections) for half in own]
        places = [(None, None)] + [(2 * s, 2 * s + 1) for s in range(n_sections - 1)]
    probs = probabilities(lengths, queries, keys)
    probs, *arrived = tie(probs, *arrived)
    heads, mixed, part = heads_proj(section, probs, own, arrived, places, w_out)
    middle = (x, part, exchange(part, "tensor"))

    weights = (w_gate, w_up, w_down)
    normed_ffn, *rest_acts, down = entry(*middle, gain_ffn, grad_out, *weights, rest)
    line.push(down, *put_rows("down", n_blocks * UNITS // 128, 128))
    line.mark(normed_ffn)
    turned_ffn = turned(line.after(normed_ffn))
    gate, up = weight_grads(turned_ffn, rest_acts[1:], rest, (0, 0))
    line.mark(gate, up)
    line.push(gate, *put_columns("gate", n_blocks * UNITS // 128, 128))
    line.push(up, *put_columns("up", n_blocks * UNITS // 128, 128))
    acts = [None] * 3
    for number in range(n_blocks):
        *acts, down = ffn(line.after(normed_ffn), grad_out, *weights, UNITS, number, n_blocks, acts)
        line.mark(down)
        line.push(down, *put_rows("down", number * UNITS // 128, 128))
        line.step()

    def unit_grads(number):
        if number < n_blocks:
            gate, up = weight_grads(line.after(turned_ffn), acts[1:], UNITS, (number, number))
            line.mark(gate, up)
            line.push(gate, *put_columns("gate", number, UNITS))
            line.push(up, *put_columns("up", number, UNITS))

    unit_grads(0)
    line.step()
    part = products([((acts[1], line.after(rest_acts[1])), w_gate), ((acts[2], rest_acts[2]), w_up)], True)
    part_other = exchange(part, "tensor")
    line.mark(part)
    line.step()
    unit_grads(1)
    line.step()
    grad_middle, grad_attn, grad_gain_ffn = norm_back(line.after(part), part_other, middle, gain_ffn, grad_out, True)
    line.mark(grad_attn)
    line.step()
    for number in range(2, n_blocks):
        unit_grads(number)
    for number in range(heads.shape[1] // CHUNK):
        part = row_grads(line.after(heads), grad_attn, number)
        line.mark(part)
        line.push(part, *put_rows("out", number * CHUNK // 128, 128))
    line.step()

    def column_grads(name, grad):
        numbers = tuple(range(grad.shape[1] // CHUNK))
        parts = weight_grads(line.after(turned_attn), [grad] * len(numbers), CHUNK, numbers)
        line.mark(*parts)
        for number, part in zip(numbers, parts):
            line.push(part, *put_columns(name, number, CHUNK))

    pairs = queries.shape[1] // (2 * HD)
    grads = [None] * 3
    for first in range(pairs):
        grads = attend_back(queries, keys, mixed, probs, line.after(grad_attn), w_out, cos, sin, first, 1, grads)
        line.mark(*grads)
        if first < pairs - 1:
            line.step()
    grad_query, grad_key, half_mixed = grads
    if relay:
        from_left, from_right = send(half_mixed[:, : half_mixed.shape[1] // 2], (3, 1)), send(
            half_mixed[:, half_mixed.shape[1] // 2 :], (3, 2)
        )
    else:
        arrived = [send(half_mixed, (s, 0)) for s in range(1, n_sections)]
    column_grads("query", grad_query)
    column_grads("key", grad_key)
    line.step()
    part_result = products([((acts[0], line.after(rest_acts[0])), w_down)], False)
    result_other = exchange(part_result, "tensor")
    line.mark(part_result)
    line.step()
    if relay:
        both = relayed(section, line.after(half_mixed), from_left, from_right)
        arrived = [send(both, (s, 0)) for s in (1, 2)]
        line.mark(both)
    line.step()
    result = block_result(line.after(part_result), result_other, middle)
    line.mark(result)
    line.step()
    grad_value = first_grad(section, line.after(half_mixed), arrived)
    column_grads("value", grad_value)
    part = products(
        [((line.after(grad_query),), w_query), ((grad_key,), w_key), ((grad_value,), w_value)], True
    )
    part_other = exchange(part, "tensor")
    line.mark(part)
    line.step()
    line.step()
    grad_input, grad_gain_attn = norm_back(line.after(part), part_other, (x,), gain_attn, grad_middle, False)
    line.mark(grad_input)
    gains = jnp.concatenate([grad_gain_attn, grad_gain_ffn], axis=0)
    gains = jnp.pad(gains, ((0, 14), (0, 0))).astype(BF16)
    line.push(gains, "gains", (16, width), lambda i, j: (0, 0))
    line.finish()

    outs = line.outs
    return (
        result[None],
        grad_input[None],
        outs["gains"][0:1],
        *(outs[name][None] for name in ("query", "key", "value", "out")),
        outs["gains"][1:2],
        *(outs[name][None] for name in ("gate", "up", "down")),
    )


def solution(mesh):
    sizes = dict(mesh.shape)
    token = P("section", "dp", None)
    gain = P("section", None)
    wide, tall = P("section", None, "tensor"), P("section", "tensor", None)
    return jax.shard_map(
        lambda *args: shards(sizes, *args),
        mesh=mesh,
        in_specs=(token, P("dp", None), gain, wide, wide, wide, tall, gain, wide, wide, tall, token),
        out_specs=(token, token, gain, wide, wide, wide, tall, gain, wide, wide, tall),
        check_vma=False,
    )
```

time: 510 us -> 470 us (0.922)
  matrix products: 20.6 us -> 0 us
  waiting for transfers between devices: 114 us -> 96.8 us
  local copies, waits for them, and re-layouts: 19.6 us -> 11.5 us
  Pallas kernels: 182 us -> 188 us
  starting transfers between devices: 155 us -> 161 us
  other arithmetic: 8.38 us -> 3.23 us
    dot_general x13 -> x0, matrix products: 20.6 us -> none  [the longest x6 12.4 us: dot_nt(): lax.dot_general(left, right, (((1,), (1,)), ((), ())), preferred_element_...]
    ppermute x7 -> x8, waiting for transfers between devices: 18.3 us -> 1.96 us  [send(): return lax.ppermute(block, 'section', list(pairs))]
    pallas_call x22 -> x30, Pallas kernels: 111 us -> 125 us  [call(): pl.pallas_call(body, grid=grid, in_specs=ins, out_specs=[spec for spec, _...]
    unnamed x121 -> x120, local copies, waits for them, and re-layouts: 19.3 us -> 10.8 us
    pallas_call x29 -> x63, Pallas kernels: 71.1 us -> 63.5 us  [chosen_call(): pl.pallas_call(body, grid_spec=pltpu.PrefetchScalarGridSpec(num_scalar_pr...]
    ppermute x58 -> x63, starting transfers between devices: 137 us -> 142 us  [the longest x21 98.8 us: start(): self.inward[i] = lax.ppermute(self.parts[i], self.axis, [(0, 1), (3, 2)])]
    ppermute x58 -> x63, waiting for transfers between devices: 92 us -> 90.7 us  [the longest x21 57 us: step(): lax.ppermute(self.total[i - 1], self.axis, [(1, 0), (2, 3)])]
    ppermute x7 -> x8, starting transfers between devices: 18.2 us -> 19.5 us  [send(): return lax.ppermute(block, 'section', list(pairs))]
  transfers between devices with their start and end apart: 69 -> 75, of which waited for: 25 -> 23; matrix products, arithmetic and copies ran while one was open for 3% -> 1% of each run, Pallas kernels for 30% -> 31%
where the time goes in v2:
time: 470 us; the launch traced here: 464 us
  Pallas kernels  188 us (40%)
  starting transfers between devices  161 us (34%)
  waiting for transfers between devices  96.8 us (21%)
  local copies, waits for them, and re-layouts  11.5 us (2%)
    pallas_call x30, Pallas kernels, call(): pl.pallas_call(body, grid=grid, in_specs=ins, out_specs=[spec for spec, _...  125 us
    ppermute x21, starting transfers between devices, start(): self.inward[i] = lax.ppermute(self.parts[i], self.axis, [(0, 1), (3, 2)])  98.8 us
    pallas_call x63, Pallas kernels, chosen_call(): pl.pallas_call(body, grid_spec=pltpu.PrefetchScalarGridSpec(num_scalar_pr...  63.5 us
    ppermute x21, waiting for transfers between devices, step(): lax.ppermute(self.total[i - 1], self.axis, [(1, 0), (2, 3)])  57 us
    ppermute x21, waiting for transfers between devices, start(): self.inward[i] = lax.ppermute(self.parts[i], self.axis, [(0, 1), (3, 2)])  33.6 us
    ppermute x21, starting transfers between devices, step(): lax.ppermute(self.total[i - 1], self.axis, [(1, 0), (2, 3)])  28.1 us
    ppermute x8, starting transfers between devices, send(): return lax.ppermute(block, 'section', list(pairs))  19.5 us
    ppermute x21, starting transfers between devices, step(): self.across[i] = lax.ppermute(self.half[i], self.axis, [(1, 2), (2, 1)])  14.9 us
  transfers between devices with their start and end apart: 75, of which 23 were waited for; matrix products, arithmetic and copies ran while one was open for 1% of the time, Pallas kernels for 31%

profile of v2, /device:TPU:0, one launch (start us, length us, event | category | flops | bytes accessed | tf_op | source)
XLA Modules:
  0.0 464.3 jit_solution(5344380843462410298)
XLA Ops:
  5.7 5.9 %collective-permute-start = (bf16[1024,256]{1,0:T(8,128)(2,1)}, bf16[1024,256]{1,0:T(8,128)(2,1)}, u32[]{:S(2)}, u32[]{:S(2)}) collective-permute-start(bf16[1024,256]{1,0:T(8,128)(2,1)} %get-tuple-element.246.refs_2_), channel_id=1, source_target_pairs={{0,8},{1,9},{2,10},{3,11},{4,12},{5,13},{6,14},{7,15}} | collective-permute-start | bytes 1572872 | tf_op jit(solution)/shard_map/ppermute | solution.py:762
  32.0 10.5 %shard_map.205.refs_1_.probs_ref.refs_3_ = bf16[8,1024,768]{2,1,0:T(8,128)(2,1)} custom-call(s32[1,4]{1,0:T(1,128)S(1)} %copy-done.56, bf16[1024,512]{1,0:T(8,128)(2,1)S(1)} %get-tuple-element.250.q_ref.refs_0_, bf16[1024,512]{1,0:T(8,128)(2,1)S(1)} %get-tuple-element.251.k_ref.refs_1_), custom_call_target="tpu_custom_call" | custom-call | flops 1 | bytes 1 | tf_op jit(solution)/shard_map/pallas_call | solution.py:42
  42.6 8.1 %shard_map.206 = (bf16[1024,512]{1,0:T(8,128)(2,1)S(1)}, bf16[1024,512]{1,0:T(8,128)(2,1)S(1)}, bf16[1024,1024]{1,0:T(8,128)(2,1)S(1)}) custom-call(s32[1]{0:T(128)} %bitcast.1.refs_0_.section_ref, bf16[8,1024,768]{2,1,0:T(8,128)(2,1)} %shard_map.205.refs_1_.probs_ref.refs_3_, bf16[1024,256]{1,0:T(8,128)(2,1)S(1)} %copy-done.42, ...), custom_call_target="tpu_custom_call" | custom-call | flops 1 | bytes 1 | tf_op jit(solution)/shard_map/pallas_call | solution.py:42
  58.2 8.3 %shard_map.207 = (bf16[1024,1024]{1,0:T(8,128)(2,1)}, bf16[1024,256]{1,0:T(8,128)(2,1)}, bf16[1024,256]{1,0:T(8,128)(2,1)}, bf16[1024,256]{1,0:T(8,128)(2,1)}, bf16[256,1024]{1,0:T(8,128)(2,1)}) custom-call(bf16[1024,1024]{1,0:T(8,128)(2,1)} %bitcast.48, bf16[1024,1024]{1,0:T(8,128)(2,1)} %copy-done.24, bf16[1024,1024]{1,0:T(8,128)(2,1)} %copy-done.27, ...), custom_call_target="tpu_custom_call" | custom-call | flops 1 | bytes 1 | tf_op jit(solution)/shard_map/pallas_call | solution.py:42
  82.4 6.4 %shard_map.210 = (bf16[1024,1152]{1,0:T(8,128)(2,1)S(1)}, bf16[1024,1152]{1,0:T(8,128)(2,1)S(1)}, bf16[1024,1152]{1,0:T(8,128)(2,1)S(1)}, bf16[384,1024]{1,0:T(8,128)(2,1)S(1)}) custom-call(bf16[1024,1024]{1,0:T(8,128)(2,1)S(1)} %copy-done.10, bf16[1024,1024]{1,0:T(8,128)(2,1)S(1)} %bitcast.43, bf16[1024,1408]{1,0:T(8,128)(2,1)} %bitcast.26, ...), custom_call_target="tpu_custom_call" | custom-call | flops 1 | bytes 1 | tf_op jit(solution)/shard_map/pallas_call | solution.py:42
  93.7 6.2 %shard_map.212 = (bf16[1024,1152]{1,0:T(8,128)(2,1)S(1)}, bf16[1024,1152]{1,0:T(8,128)(2,1)S(1)}, bf16[1024,1152]{1,0:T(8,128)(2,1)S(1)}, bf16[384,1024]{1,0:T(8,128)(2,1)S(1)}) custom-call(bf16[1024,1024]{1,0:T(8,128)(2,1)S(1)} %copy-done.10, bf16[1024,1024]{1,0:T(8,128)(2,1)S(1)} %bitcast.44, ...), custom_call_target="tpu_custom_call", output_to_operand_aliasing={{0}: (5, {}), {1}: (6, {}), {2}: (7, {})} | custom-call | flops 1 | bytes 1 | tf_op jit(solution)/shard_map/pallas_call | solution.py:42
  107.4 6.3 %shard_map.215 = (bf16[1024,1152]{1,0:T(8,128)(2,1)S(1)}, bf16[1024,1152]{1,0:T(8,128)(2,1)S(1)}, bf16[1024,1152]{1,0:T(8,128)(2,1)S(1)}, bf16[384,1024]{1,0:T(8,128)(2,1)S(1)}) custom-call(bf16[1024,1024]{1,0:T(8,128)(2,1)S(1)} %copy-done.10, bf16[1024,1024]{1,0:T(8,128)(2,1)S(1)} %bitcast.45, ...), custom_call_target="tpu_custom_call", output_to_operand_aliasing={{0}: (5, {}), {1}: (6, {}), {2}: (7, {})} | custom-call | flops 1 | bytes 1 | tf_op jit(solution)/shard_map/pallas_call | solution.py:42
  126.8 6.6 %collective-permute-done.16.refs_1_ = bf16[1024,256]{1,0:T(8,128)(2,1)S(1)} collective-permute-done((bf16[1024,256]{1,0:T(8,128)(2,1)S(1)}, bf16[1024,256]{1,0:T(8,128)(2,1)S(1)}, u32[]{:S(2)}, u32[]{:S(2)}) %collective-permute-start.16) | collective-permute-done | bytes 524320 | tf_op jit(solution)/shard_map/ppermute | solution.py:688
  135.7 7.5 %shard_map.223.refs_0_ = bf16[1024,1024]{1,0:T(8,128)(2,1)S(1)} custom-call(bf16[1024,1152]{1,0:T(8,128)(2,1)S(1)} %get-tuple-element.297.refs_0_, bf16[1024,256]{1,0:T(8,128)(2,1)S(1)} %copy-done.47, bf16[1024,1152]{1,0:T(8,128)(2,1)S(1)} %get-tuple-element.298.refs_1_.refs_2_, bf16[1024,256]{1,0:T(8,128)(2,1)S(1)} %copy-done.49, ...), custom_call_target="tpu_custom_call" | custom-call | flops 1 | bytes 1 | tf_op jit(solution)/shard_map/pallas_call | solution.py:42
  151.9 11.1 %collective-permute-done.15.refs_1_ = bf16[384,1024]{1,0:T(8,128)(2,1)S(1)} collective-permute-done((bf16[384,1024]{1,0:T(8,128)(2,1)S(1)}, bf16[384,1024]{1,0:T(8,128)(2,1)S(1)}, u32[]{:S(2)}, u32[]{:S(2)}) %collective-permute-start.15) | collective-permute-done | bytes 786464 | tf_op jit(solution)/shard_map/ppermute | solution.py:664
  166.2 7.6 %collective-permute-start.19 = (bf16[1024,384]{1,0:T(8,128)(2,1)S(1)}, bf16[1024,384]{1,0:T(8,128)(2,1)S(1)}, u32[]{:S(2)}, u32[]{:S(2)}) collective-permute-start(bf16[1024,384]{1,0:T(8,128)(2,1)S(1)} %get-tuple-element.328.refs_0_), channel_id=1, source_target_pairs={{0,2},{6,4},{1,3},{7,5},{8,10},{14,12},{9,11},{15,13},{16,18},{22,... | collective-permute-start | bytes 2359304 | tf_op jit(solution)/shard_map/ppermute | solution.py:664
  199.1 6.4 %collective-permute-start.29 = (bf16[1024,384]{1,0:T(8,128)(2,1)S(1)}, bf16[1024,384]{1,0:T(8,128)(2,1)S(1)}, u32[]{:S(2)}, u32[]{:S(2)}) collective-permute-start(bf16[1024,384]{1,0:T(8,128)(2,1)S(1)} %get-tuple-element.354.refs_0_), channel_id=1, source_target_pairs={{0,2},{6,4},{1,3},{7,5},{8,10},{14,12},{9,11},{15,13},{16,18},{22,... | collective-permute-start | bytes 2359304 | tf_op jit(solution)/shard_map/ppermute | solution.py:664
  218.9 7.2 %collective-permute-start.23 = (bf16[1024,384]{1,0:T(8,128)(2,1)S(1)}, bf16[1024,384]{1,0:T(8,128)(2,1)S(1)}, u32[]{:S(2)}, u32[]{:S(2)}) collective-permute-start(bf16[1024,384]{1,0:T(8,128)(2,1)S(1)} %get-tuple-element.364.refs_0_), channel_id=1, source_target_pairs={{0,2},{6,4},{1,3},{7,5},{8,10},{14,12},{9,11},{15,13},{16,18},{22,... | collective-permute-start | bytes 2359304 | tf_op jit(solution)/shard_map/ppermute | solution.py:664
  230.9 6.0 %shard_map.241 = (bf16[1024,512]{1,0:T(8,128)(2,1)S(1)}, bf16[1024,512]{1,0:T(8,128)(2,1)S(1)}, bf16[1024,512]{1,0:T(8,128)(2,1)S(1)}) custom-call(bf16[1024,512]{1,0:T(8,128)(2,1)S(1)} %copy-done.13, bf16[1024,512]{1,0:T(8,128)(2,1)S(1)} %copy-done.15, bf16[1024,512]{1,0:T(8,128)(2,1)S(1)} %copy-done.31, bf16[8,1024,768]{2,1,0:T(8,128)(2,1)S(1)} %bitcast.23, ...), custom_call_target="tpu_custom_call" | custom-call | flops 1 | bytes 1 | tf_op jit(solution)/shard_map/pallas_call | solution.py:42
  247.3 6.0 %shard_map.245 = (bf16[1024,512]{1,0:T(8,128)(2,1)S(1)}, bf16[1024,512]{1,0:T(8,128)(2,1)S(1)}, bf16[1024,512]{1,0:T(8,128)(2,1)S(1)}) custom-call(bf16[1024,512]{1,0:T(8,128)(2,1)S(1)} %copy-done.13, bf16[1024,512]{1,0:T(8,128)(2,1)S(1)} %copy-done.15, ...), custom_call_target="tpu_custom_call", output_to_operand_aliasing={{0}: (8, {}), {1}: (9, {}), {2}: (10, {})} | custom-call | flops 1 | bytes 1 | tf_op jit(solution)/shard_map/pallas_call | solution.py:42
  264.1 6.0 %shard_map.249 = (bf16[1024,512]{1,0:T(8,128)(2,1)S(1)}, bf16[1024,512]{1,0:T(8,128)(2,1)S(1)}, bf16[1024,512]{1,0:T(8,128)(2,1)S(1)}) custom-call(bf16[1024,512]{1,0:T(8,128)(2,1)S(1)} %copy-done.13, bf16[1024,512]{1,0:T(8,128)(2,1)S(1)} %copy-done.15, ...), custom_call_target="tpu_custom_call", output_to_operand_aliasing={{0}: (8, {}), {1}: (9, {}), {2}: (10, {})} | custom-call | flops 1 | bytes 1 | tf_op jit(solution)/shard_map/pallas_call | solution.py:42
  273.4 5.8 %collective-permute-done.38.refs_1_ = bf16[1024,384]{1,0:T(8,128)(2,1)S(1)} collective-permute-done((bf16[1024,384]{1,0:T(8,128)(2,1)S(1)}, bf16[1024,384]{1,0:T(8,128)(2,1)S(1)}, u32[]{:S(2)}, u32[]{:S(2)}) %collective-permute-start.38) | collective-permute-done | bytes 786464 | tf_op jit(solution)/shard_map/ppermute | solution.py:688
  281.0 6.0 %shard_map.253 = (bf16[1024,512]{1,0:T(8,128)(2,1)S(1)}, bf16[1024,512]{1,0:T(8,128)(2,1)S(1)}, bf16[1024,512]{1,0:T(8,128)(2,1)S(1)}) custom-call(bf16[1024,512]{1,0:T(8,128)(2,1)S(1)} %copy-done.13, bf16[1024,512]{1,0:T(8,128)(2,1)S(1)} %copy-done.15, ...), custom_call_target="tpu_custom_call", output_to_operand_aliasing={{0}: (8, {}), {1}: (9, {}), {2}: (10, {})} | custom-call | flops 1 | bytes 1 | tf_op jit(solution)/shard_map/pallas_call | solution.py:42
  306.1 9.4 %collective-permute-done.40.refs_1_ = bf16[256,1024]{1,0:T(8,128)(2,1)S(1)} collective-permute-done((bf16[256,1024]{1,0:T(8,128)(2,1)S(1)}, bf16[256,1024]{1,0:T(8,128)(2,1)S(1)}, u32[]{:S(2)}, u32[]{:S(2)}) %collective-permute-start.40) | collective-permute-done | bytes 524320 | tf_op jit(solution)/shard_map/ppermute | solution.py:664
  316.2 7.2 %collective-permute-start.43 = (bf16[256,1024]{1,0:T(8,128)(2,1)S(1)}, bf16[256,1024]{1,0:T(8,128)(2,1)S(1)}, u32[]{:S(2)}, u32[]{:S(2)}) collective-permute-start(bf16[256,1024]{1,0:T(8,128)(2,1)S(1)} %shard_map.237.refs_0_), channel_id=1, source_target_pairs={{0,2},{6,4},{1,3},{7,5},{8,10},{14,12},{9,11},{15,13},{16,18},{22,... | collective-permute-start | bytes 1572872 | tf_op jit(solution)/shard_map/ppermute | solution.py:664
  335.8 9.7 %collective-permute-start.50 = (bf16[1024,256]{1,0:T(8,128)(2,1)S(1)}, bf16[1024,256]{1,0:T(8,128)(2,1)S(1)}, u32[]{:S(2)}, u32[]{:S(2)}) collective-permute-start(bf16[1024,256]{1,0:T(8,128)(2,1)S(1)} %get-tuple-element.417.refs_0_), channel_id=1, source_target_pairs={{0,2},{6,4},{1,3},{7,5},{8,10},{14,12},{9,11},{15,13},{16,18},{22,... | collective-permute-start | bytes 1572872 | tf_op jit(solution)/shard_map/ppermute | solution.py:664
  431.2 5.7 %collective-permute-start.62 = (bf16[16,1024]{1,0:T(8,128)(2,1)S(1)}, bf16[16,1024]{1,0:T(8,128)(2,1)S(1)}, u32[]{:S(2)}, u32[]{:S(2)}) collective-permute-start(bf16[16,1024]{1,0:T(8,128)(2,1)S(1)} %fusion.3.refs_0_), channel_id=1, source_target_pairs={{0,2},{6,4},{1,3},{7,5},{8,10},{14,12},{9,11},{15,13},{16,18},{22,... | collective-permute-start | bytes 98312 | tf_op jit(solution)/shard_map/ppermute | solution.py:664
  443.5 7.0 %collective-permute-done.71.refs_1_ = bf16[1024,256]{1,0:T(8,128)(2,1)S(1)} collective-permute-done((bf16[1024,256]{1,0:T(8,128)(2,1)S(1)}, bf16[1024,256]{1,0:T(8,128)(2,1)S(1)}, u32[]{:S(2)}, u32[]{:S(2)}) %collective-permute-start.71) | collective-permute-done | bytes 524320 | tf_op jit(solution)/shard_map/ppermute | solution.py:688
  453.9 7.4 %collective-permute-done.74.refs_1_ = bf16[1024,256]{1,0:T(8,128)(2,1)S(1)} collective-permute-done((bf16[1024,256]{1,0:T(8,128)(2,1)S(1)}, bf16[1024,256]{1,0:T(8,128)(2,1)S(1)}, u32[]{:S(2)}, u32[]{:S(2)}) %collective-permute-start.74) | collective-permute-done | bytes 524320 | tf_op jit(solution)/shard_map/ppermute | solution.py:688
  (354 shorter events, 287.0 us)
Async XLA Ops:
  76.5 23.4 %collective-permute-start.7 = (bf16[1024,256]{1,0:T(8,128)(2,1)}, bf16[1024,256]{1,0:T(8,128)(2,1)}, u32[]{:S(2)}, u32[]{:S(2)}) collective-permute-start(bf16[1024,256]{1,0:T(8,128)(2,1)} %get-tuple-element.277.refs_0_), channel_id=1, source_target_pairs={{0,2},{6,4},{1,3},{7,5},{8,10},{14,12},{9,11},{15,13},{16,18},{22,... | collective-permute-start | bytes 1572872 | tf_op jit(solution)/shard_map/ppermute | solution.py:664
  91.1 22.6 %collective-permute-start.8 = (bf16[1024,256]{1,0:T(8,128)(2,1)S(1)}, bf16[1024,256]{1,0:T(8,128)(2,1)S(1)}, u32[]{:S(2)}, u32[]{:S(2)}) collective-permute-start(bf16[1024,256]{1,0:T(8,128)(2,1)S(1)} %copy-done.51), channel_id=1, source_target_pairs={{0,2},{6,4},{1,3},{7,5},{8,10},{14,12},{9,11},{15,13},{16,18},{22,... | collective-permute-start | bytes 1572872 | tf_op jit(solution)/shard_map/ppermute | solution.py:664
  102.3 23.1 %collective-permute-start.10 = (bf16[384,1024]{1,0:T(8,128)(2,1)S(1)}, bf16[384,1024]{1,0:T(8,128)(2,1)S(1)}, u32[]{:S(2)}, u32[]{:S(2)}) collective-permute-start(bf16[384,1024]{1,0:T(8,128)(2,1)S(1)} %get-tuple-element.301.refs_0_), channel_id=1, source_target_pairs={{0,2},{6,4},{1,3},{7,5},{8,10},{14,12},{9,11},{15,13},{16,18},{22,... | collective-permute-start | bytes 2359304 | tf_op jit(solution)/shard_map/ppermute | solution.py:664
  143.1 50.7 %collective-permute-start.22 = (bf16[1024,1024]{1,0:T(8,128)(2,1)S(1)}, bf16[1024,1024]{1,0:T(8,128)(2,1)S(1)}, u32[]{:S(2)}, u32[]{:S(2)}) collective-permute-start(bf16[1024,1024]{1,0:T(8,128)(2,1)S(1)} %shard_map.223.refs_0_), channel_id=1, source_target_pairs={{0,1},{1,0},{2,3},{3,2},{4,5},{5,4},{6,7},{7,6},{8,9},{9,8},{10,11... | collective-permute-start | bytes 6291464 | tf_op jit(solution)/shard_map/ppermute | solution.py:734
  147.3 32.6 %collective-permute-start.17 = (bf16[384,1024]{1,0:T(8,128)(2,1)S(1)}, bf16[384,1024]{1,0:T(8,128)(2,1)S(1)}, u32[]{:S(2)}, u32[]{:S(2)}) collective-permute-start(bf16[384,1024]{1,0:T(8,128)(2,1)S(1)} %get-tuple-element.319.refs_0_), channel_id=1, source_target_pairs={{0,2},{6,4},{1,3},{7,5},{8,10},{14,12},{9,11},{15,13},{16,18},{22,... | collective-permute-start | bytes 2359304 | tf_op jit(solution)/shard_map/ppermute | solution.py:664
  164.9 23.6 %collective-permute-start.20 = (bf16[384,1024]{1,0:T(8,128)(2,1)S(1)}, bf16[384,1024]{1,0:T(8,128)(2,1)S(1)}, u32[]{:S(2)}, u32[]{:S(2)}) collective-permute-start(bf16[384,1024]{1,0:T(8,128)(2,1)S(1)} %shard_map.225.refs_0_), channel_id=1, source_target_pairs={{2,0},{4,6},{3,1},{5,7},{10,8},{12,14},{11,9},{13,15},{18,16},{20,... | collective-permute-start | bytes 2359304 | tf_op jit(solution)/shard_map/ppermute | solution.py:688
  166.2 31.5 %collective-permute-start.19 = (bf16[1024,384]{1,0:T(8,128)(2,1)S(1)}, bf16[1024,384]{1,0:T(8,128)(2,1)S(1)}, u32[]{:S(2)}, u32[]{:S(2)}) collective-permute-start(bf16[1024,384]{1,0:T(8,128)(2,1)S(1)} %get-tuple-element.328.refs_0_), channel_id=1, source_target_pairs={{0,2},{6,4},{1,3},{7,5},{8,10},{14,12},{9,11},{15,13},{16,18},{22,... | collective-permute-start | bytes 2359304 | tf_op jit(solution)/shard_map/ppermute | solution.py:664
  180.5 25.0 %collective-permute-start.18 = (bf16[384,1024]{1,0:T(8,128)(2,1)S(1)}, bf16[384,1024]{1,0:T(8,128)(2,1)S(1)}, u32[]{:S(2)}, u32[]{:S(2)}) collective-permute-start(bf16[384,1024]{1,0:T(8,128)(2,1)S(1)} %shard_map.228.refs_0_), channel_id=1, source_target_pairs={{2,4},{4,2},{3,5},{5,3},{10,12},{12,10},{11,13},{13,11},{18,20},{2... | collective-permute-start | bytes 2359304 | tf_op jit(solution)/shard_map/ppermute | solution.py:683
  181.8 25.7 %collective-permute-start.26 = (bf16[384,1024]{1,0:T(8,128)(2,1)S(1)}, bf16[384,1024]{1,0:T(8,128)(2,1)S(1)}, u32[]{:S(2)}, u32[]{:S(2)}) collective-permute-start(bf16[384,1024]{1,0:T(8,128)(2,1)S(1)} %shard_map.229.refs_0_), channel_id=1, source_target_pairs={{2,0},{4,6},{3,1},{5,7},{10,8},{12,14},{11,9},{13,15},{18,16},{20,... | collective-permute-start | bytes 2359304 | tf_op jit(solution)/shard_map/ppermute | solution.py:688
  188.5 26.7 %collective-permute-start.25 = (bf16[1024,384]{1,0:T(8,128)(2,1)S(1)}, bf16[1024,384]{1,0:T(8,128)(2,1)S(1)}, u32[]{:S(2)}, u32[]{:S(2)}) collective-permute-start(bf16[1024,384]{1,0:T(8,128)(2,1)S(1)} %get-tuple-element.343.refs_0_), channel_id=1, source_target_pairs={{0,2},{6,4},{1,3},{7,5},{8,10},{14,12},{9,11},{15,13},{16,18},{22,... | collective-permute-start | bytes 2359304 | tf_op jit(solution)/shard_map/ppermute | solution.py:664
  199.1 37.8 %collective-permute-start.29 = (bf16[1024,384]{1,0:T(8,128)(2,1)S(1)}, bf16[1024,384]{1,0:T(8,128)(2,1)S(1)}, u32[]{:S(2)}, u32[]{:S(2)}) collective-permute-start(bf16[1024,384]{1,0:T(8,128)(2,1)S(1)} %get-tuple-element.354.refs_0_), channel_id=1, source_target_pairs={{0,2},{6,4},{1,3},{7,5},{8,10},{14,12},{9,11},{15,13},{16,18},{22,... | collective-permute-start | bytes 2359304 | tf_op jit(solution)/shard_map/ppermute | solution.py:664
  206.1 22.5 %collective-permute-start.30 = (bf16[384,1024]{1,0:T(8,128)(2,1)S(1)}, bf16[384,1024]{1,0:T(8,128)(2,1)S(1)}, u32[]{:S(2)}, u32[]{:S(2)}) collective-permute-start(bf16[384,1024]{1,0:T(8,128)(2,1)S(1)} %shard_map.233.refs_0_), channel_id=1, source_target_pairs={{2,0},{4,6},{3,1},{5,7},{10,8},{12,14},{11,9},{13,15},{18,16},{20,... | collective-permute-start | bytes 2359304 | tf_op jit(solution)/shard_map/ppermute | solution.py:688
  215.8 22.5 %collective-permute-start.28 = (bf16[1024,384]{1,0:T(8,128)(2,1)S(1)}, bf16[1024,384]{1,0:T(8,128)(2,1)S(1)}, u32[]{:S(2)}, u32[]{:S(2)}) collective-permute-start(bf16[1024,384]{1,0:T(8,128)(2,1)S(1)} %shard_map.238.refs_0_), channel_id=1, source_target_pairs={{2,4},{4,2},{3,5},{5,3},{10,12},{12,10},{11,13},{13,11},{18,20},{2... | collective-permute-start | bytes 2359304 | tf_op jit(solution)/shard_map/ppermute | solution.py:683
  217.4 28.1 %collective-permute-start.27 = (bf16[1024,384]{1,0:T(8,128)(2,1)S(1)}, bf16[1024,384]{1,0:T(8,128)(2,1)S(1)}, u32[]{:S(2)}, u32[]{:S(2)}) collective-permute-start(bf16[1024,384]{1,0:T(8,128)(2,1)S(1)} %shard_map.239.refs_0_), channel_id=1, source_target_pairs={{2,0},{4,6},{3,1},{5,7},{10,8},{12,14},{11,9},{13,15},{18,16},{20,... | collective-permute-start | bytes 2359304 | tf_op jit(solution)/shard_map/ppermute | solution.py:688
  218.9 34.3 %collective-permute-start.23 = (bf16[1024,384]{1,0:T(8,128)(2,1)S(1)}, bf16[1024,384]{1,0:T(8,128)(2,1)S(1)}, u32[]{:S(2)}, u32[]{:S(2)}) collective-permute-start(bf16[1024,384]{1,0:T(8,128)(2,1)S(1)} %get-tuple-element.364.refs_0_), channel_id=1, source_target_pairs={{0,2},{6,4},{1,3},{7,5},{8,10},{14,12},{9,11},{15,13},{16,18},{22,... | collective-permute-start | bytes 2359304 | tf_op jit(solution)/shard_map/ppermute | solution.py:664
  238.9 23.4 %collective-permute-start.33 = (bf16[1024,384]{1,0:T(8,128)(2,1)S(1)}, bf16[1024,384]{1,0:T(8,128)(2,1)S(1)}, u32[]{:S(2)}, u32[]{:S(2)}) collective-permute-start(bf16[1024,384]{1,0:T(8,128)(2,1)S(1)} %shard_map.243.refs_0_), channel_id=1, source_target_pairs={{2,0},{4,6},{3,1},{5,7},{10,8},{12,14},{11,9},{13,15},{18,16},{20,... | collective-permute-start | bytes 2359304 | tf_op jit(solution)/shard_map/ppermute | solution.py:688
  240.2 29.9 %collective-permute-start.32 = (bf16[1024,384]{1,0:T(8,128)(2,1)S(1)}, bf16[1024,384]{1,0:T(8,128)(2,1)S(1)}, u32[]{:S(2)}, u32[]{:S(2)}) collective-permute-start(bf16[1024,384]{1,0:T(8,128)(2,1)S(1)} %get-tuple-element.375.refs_0_), channel_id=1, source_target_pairs={{0,2},{6,4},{1,3},{7,5},{8,10},{14,12},{9,11},{15,13},{16,18},{22,... | collective-permute-start | bytes 2359304 | tf_op jit(solution)/shard_map/ppermute | solution.py:664
  255.2 24.0 %collective-permute-start.38 = (bf16[1024,384]{1,0:T(8,128)(2,1)S(1)}, bf16[1024,384]{1,0:T(8,128)(2,1)S(1)}, u32[]{:S(2)}, u32[]{:S(2)}) collective-permute-start(bf16[1024,384]{1,0:T(8,128)(2,1)S(1)} %shard_map.247.refs_0_), channel_id=1, source_target_pairs={{2,0},{4,6},{3,1},{5,7},{10,8},{12,14},{11,9},{13,15},{18,16},{20,... | collective-permute-start | bytes 2359304 | tf_op jit(solution)/shard_map/ppermute | solution.py:688
  256.5 33.5 %collective-permute-start.37 = (bf16[1024,384]{1,0:T(8,128)(2,1)S(1)}, bf16[1024,384]{1,0:T(8,128)(2,1)S(1)}, u32[]{:S(2)}, u32[]{:S(2)}) collective-permute-start(bf16[1024,384]{1,0:T(8,128)(2,1)S(1)} %get-tuple-element.393.refs_0_), channel_id=1, source_target_pairs={{0,2},{6,4},{1,3},{7,5},{8,10},{14,12},{9,11},{15,13},{16,18},{22,... | collective-permute-start | bytes 2359304 | tf_op jit(solution)/shard_map/ppermute | solution.py:664
  300.1 47.2 %collective-permute-start.47 = (bf16[1024,1024]{1,0:T(8,128)(2,1)S(1)}, bf16[1024,1024]{1,0:T(8,128)(2,1)S(1)}, u32[]{:S(2)}, u32[]{:S(2)}) collective-permute-start(bf16[1024,1024]{1,0:T(8,128)(2,1)S(1)} %shard_map.259.own_ref), channel_id=1, source_target_pairs={{0,1},{1,0},{2,3},{3,2},{4,5},{5,4},{6,7},{7,6},{8,9},{9,8},{10,11... | collective-permute-start | bytes 6291464 | tf_op jit(solution)/shard_map/ppermute | solution.py:734
  328.6 34.3 %collective-permute-start.51 = (bf16[1024,512]{1,0:T(8,128)(2,1)S(1)}, bf16[1024,512]{1,0:T(8,128)(2,1)S(1)}, u32[]{:S(2)}, u32[]{:S(2)}) collective-permute-start(bf16[1024,512]{1,0:T(8,128)(2,1)S(1)} %shard_map.263), channel_id=1, source_target_pairs={{8,0},{9,1},{10,2},{11,3},{12,4},{13,5},{14,6},{15,7}} | collective-permute-start | bytes 3145736 | tf_op jit(solution)/shard_map/ppermute | solution.py:762
  334.5 28.4 %collective-permute-start.52 = (bf16[1024,512]{1,0:T(8,128)(2,1)S(1)}, bf16[1024,512]{1,0:T(8,128)(2,1)S(1)}, u32[]{:S(2)}, u32[]{:S(2)}) collective-permute-start(bf16[1024,512]{1,0:T(8,128)(2,1)S(1)} %shard_map.263), channel_id=1, source_target_pairs={{16,0},{17,1},{18,2},{19,3},{20,4},{21,5},{22,6},{23,7}} | collective-permute-start | bytes 3145736 | tf_op jit(solution)/shard_map/ppermute | solution.py:762
  369.5 37.9 %collective-permute-start.59 = (bf16[1024,1024]{1,0:T(8,128)(2,1)S(1)}, bf16[1024,1024]{1,0:T(8,128)(2,1)S(1)}, u32[]{:S(2)}, u32[]{:S(2)}) collective-permute-start(bf16[1024,1024]{1,0:T(8,128)(2,1)S(1)} %shard_map.273.refs_0_), channel_id=1, source_target_pairs={{0,1},{1,0},{2,3},{3,2},{4,5},{5,4},{6,7},{7,6},{8,9},{9,8},{10,11... | collective-permute-start | bytes 6291464 | tf_op jit(solution)/shard_map/ppermute | solution.py:734
  388.1 23.2 %collective-permute-start.61 = (bf16[1024,256]{1,0:T(8,128)(2,1)S(1)}, bf16[1024,256]{1,0:T(8,128)(2,1)S(1)}, u32[]{:S(2)}, u32[]{:S(2)}) collective-permute-start(bf16[1024,256]{1,0:T(8,128)(2,1)S(1)} %get-tuple-element.448.refs_0_), channel_id=1, source_target_pairs={{0,2},{6,4},{1,3},{7,5},{8,10},{14,12},{9,11},{15,13},{16,18},{22,... | collective-permute-start | bytes 1572872 | tf_op jit(solution)/shard_map/ppermute | solution.py:664
  (111 other events, 1379.7 us)

commit v3 on v2

--- a/solution.py
+++ b/solution.py
@@ -13,7 +13,9 @@
 BF16 = jnp.bfloat16
 MIB = 1024 * 1024
 UNITS = 384
-CHUNK = 256
+GWAIT = 4
+LAST = 2
+DEPTH = 3
 
 
 def dot(left, right):
@@ -28,7 +30,7 @@
     return lax.dot_general(left, right, (((0,), (0,)), ((), ())), preferred_element_type=F32)
 
 
-def call(kernel, grid, ins, outs, args, vmem, scratch=(), into=None):
+def call(kernel, grid, ins, outs, args, vmem, scratch=(), into=None, name=None):
     into = {o: array for o, array in (into or {}).items() if array is not None}
     ins, args, n = list(ins), list(args), len(args)
     body = kernel
@@ -42,6 +44,7 @@
     return pl.pallas_call(
         body,
         grid=grid,
+        name=name or kernel.__name__.removesuffix("_kernel"),
         in_specs=ins,
         out_specs=[spec for spec, _, _ in outs],
         out_shape=[jax.ShapeDtypeStruct(shape, dtype) for _, shape, dtype in outs],
@@ -58,6 +61,10 @@
 
 def whole(*shape):
     return pl.BlockSpec(shape, lambda i: (0,) * len(shape))
+
+
+def held(*shape):
+    return pl.BlockSpec(shape, lambda i: (0,) * len(shape), pipeline_mode=pl.Buffered(1))
 
 
 def columns(height, block, first=0):
@@ -82,7 +89,7 @@
     return call(
         value_kernel,
         (tokens // block,),
-        [rows(block, width), whole(1, width), whole(width, 2 * half)],
+        [rows(block, width), held(1, width), held(width, 2 * half)],
         [(rows(block, width), (tokens, width), BF16)] + [(rows(block, half), (tokens, half), BF16)] * 2,
         (x, gain, w_value),
         60,
@@ -112,7 +119,7 @@
     return call(
         query_key_kernel,
         (tokens // block,),
-        [rows(block, width), whole(width, out), whole(width, out), rows(block, 128), rows(block, 128)],
+        [rows(block, width), held(width, out), held(width, out), rows(block, 128), rows(block, 128)],
         [
             (rows(block, out), (tokens, out), BF16),
             (rows(block, out), (tokens, out), BF16),
@@ -220,8 +227,8 @@
         lambda *refs: heads_kernel(len(arrived), places, *refs),
         (tokens // block,),
         [pl.BlockSpec(memory_space=pltpu.SMEM), pl.BlockSpec((n_heads, block, wide), lambda i: (0, i, 0))]
-        + [whole(tokens, half)] * (2 + len(arrived))
-        + [whole(width, model)],
+        + [held(tokens, half)] * (2 + len(arrived))
+        + [held(width, model)],
         [
             (rows(block, width), (tokens, width), BF16),
             (whole(tokens, width), (tokens, width), BF16),
@@ -229,17 +236,48 @@
         ],
         (section.astype(jnp.int32)[None], probs, *own, *arrived, w_out),
         40,
-    )
-
-
-def attend_back_kernel(
-    q_ref, k_ref, mixed_ref, probs_ref, attn_ref, w_ref, cos_ref, sin_ref, dq_ref, dk_ref, half_ref, grad_ref, key_acc, value_acc
-):
+        name="heads",
+    )
+
+
+def value_back_kernel(probs_ref, attn_ref, w_ref, grad_ref, half_ref, acc):
+    tokens = attn_ref.shape[0]
+    block = 256
+    acc[...] = jnp.zeros_like(acc)
+    grad_ref[...] = dot_nt(attn_ref[...], w_ref[...]).astype(BF16)
+    for at in range(0, tokens, block):
+        low = max(0, at - WINDOW)
+        turned_grads = grad_ref[at : at + block, :].T
+        for h in range(2):
+            lanes = slice(h * HD, (h + 1) * HD)
+            acc[lanes, low : at + block] += dot(turned_grads[lanes], probs_ref[h, at : at + block, : at + block - low])
+    for at in range(0, tokens, block):
+        half_ref[at : at + block, :] = (0.5 * acc[:, at : at + block].T).astype(BF16)
+
+
+def value_back(probs, grad_attn, w_out):
+    tokens, model = grad_attn.shape
+    width = w_out.shape[0]
+    pair = columns(tokens, 2 * HD)
+    return call(
+        value_back_kernel,
+        (width // (2 * HD),),
+        [
+            pl.BlockSpec((2, tokens, probs.shape[2]), lambda i: (i, 0, 0)),
+            held(tokens, model),
+            pl.BlockSpec((2 * HD, model), lambda i: (i, 0)),
+        ],
+        [(pair, (tokens, width), BF16)] * 2,
+        (probs, grad_attn, w_out),
+        26,
+        scratch=[pltpu.VMEM((2 * HD, tokens), F32)],
+    )
+
+
+def attend_back_kernel(q_ref, k_ref, mixed_ref, probs_ref, grad_ref, cos_ref, sin_ref, dq_ref, dk_ref, key_acc):
     tokens = q_ref.shape[0]
     block = 256
     key_acc[...] = jnp.zeros_like(key_acc)
-    value_acc[...] = jnp.zeros_like(value_acc)
-    grad_ref[...] = dot_nt(attn_ref[...], w_ref[...]).astype(BF16)
 
     def turned_back(grads, at, count):
         cos, sin = cos_ref[at : at + count, :], sin_ref[at : at + count, :]
@@ -250,41 +288,36 @@
         low = max(0, at - WINDOW)
         grads = grad_ref[at : at + block, :]
         queries_turned = (q_ref[at : at + block, :] * BF16(HD**-0.5)).T
-        grads_turned = grads.T
         keys = k_ref[low : at + block, :]
         values = mixed_ref[low : at + block, :]
         parts = []
         for h, mask in enumerate(masks):
             lanes = slice(h * HD, (h + 1) * HD)
-            probs_low = probs_ref[h, at : at + block, : at + block - low]
-            probs = probs_low.astype(F32)
+            probs = probs_ref[h, at : at + block, : at + block - low].astype(F32)
             grad_probs = dot_nt(jnp.where(mask, grads, BF16(0)), values)
             inner = jnp.sum(probs * grad_probs, axis=1, keepdims=True)
             grad_scores = (probs * (grad_probs - inner)).astype(BF16)
             parts.append(dot(grad_scores, keys))
             key_acc[lanes, low : at + block] += dot(queries_turned[lanes], grad_scores)
-            value_acc[lanes, low : at + block] += dot(grads_turned[lanes], probs_low)
         grad_query = jnp.where(masks[0], parts[0], parts[1]) * HD**-0.5
         dq_ref[at : at + block, :] = turned_back(grad_query, at, block)
     for at in range(0, tokens, block):
         dk_ref[at : at + block, :] = turned_back(key_acc[:, at : at + block].T, at, block)
-        half_ref[at : at + block, :] = (0.5 * value_acc[:, at : at + block].T).astype(BF16)
-
-
-def attend_back(queries, keys, mixed, probs, grad_attn, w_out, cos, sin, first, count, into):
+
+
+def attend_back(queries, keys, mixed, probs, grad_heads, cos, sin, first, count, into):
     tokens, width = queries.shape
-    model = w_out.shape[1]
     pair = columns(tokens, 2 * HD, first)
     wide = probs.shape[2]
     return call(
         attend_back_kernel,
         (count,),
-        [pair, pair, pair, pl.BlockSpec((2, tokens, wide), lambda i: (i + first, 0, 0)), whole(tokens, model)]
-        + [pl.BlockSpec((2 * HD, model), lambda i: (i + first, 0)), whole(tokens, 128), whole(tokens, 128)],
-        [(pair, (tokens, width), BF16)] * 3,
-        (queries, keys, mixed, probs, grad_attn, w_out, cos, sin),
+        [pair, pair, pair, pl.BlockSpec((2, tokens, wide), lambda i: (i + first, 0, 0)), pair]
+        + [held(tokens, 128), held(tokens, 128)],
+        [(pair, (tokens, width), BF16)] * 2,
+        (queries, keys, mixed, probs, grad_heads, cos, sin),
         26,
-        scratch=[pltpu.VMEM((tokens, 2 * HD), BF16)] + [pltpu.VMEM((2 * HD, tokens), F32)] * 2,
+        scratch=[pltpu.VMEM((2 * HD, tokens), F32)],
         into=dict(enumerate(into)),
     )
 
@@ -337,10 +370,10 @@
     at = w_gate.shape[1] // 128 - n
 
     def wide(j):
-        return pl.BlockSpec((width, 128), lambda i: (0, at + j))
+        return pl.BlockSpec((width, 128), lambda i: (0, at + j), pipeline_mode=pl.Buffered(1))
 
     def tall(j):
-        return pl.BlockSpec((128, width), lambda i: (at + j, 0))
+        return pl.BlockSpec((128, width), lambda i: (at + j, 0), pipeline_mode=pl.Buffered(1))
 
     return call(
         lambda *refs: entry_kernel(n, *refs),
@@ -355,23 +388,32 @@
         (x, own, other, gain, grad_out, *[w_gate] * n, *[w_up] * n, *[w_down] * n),
         60,
         scratch=[pltpu.VMEM((units, width), F32)],
+        name="entry",
     )
 
 
 def ffn_kernel(normed_ref, grad_ref, wg_ref, wu_ref, wd_ref, hidden_ref, dg_ref, du_ref, gwd_ref):
-    grad_out = grad_ref[...]
-    hidden = unit_acts(normed_ref[...], grad_out, wg_ref[...], wu_ref[...], wd_ref[...], hidden_ref, dg_ref, du_ref)
-    gwd_ref[...] = dot(hidden.T, grad_out).astype(BF16)
+    total = None
+    block = normed_ref.shape[0] // 2
+    for at in range(0, normed_ref.shape[0], block):
+        some = pl.ds(at, block)
+        grad_out = grad_ref[some, :]
+        outs = (ref.at[some, :] for ref in (hidden_ref, dg_ref, du_ref))
+        hidden = unit_acts(normed_ref[some, :], grad_out, wg_ref[...], wu_ref[...], wd_ref[...], *outs)
+        term = dot(hidden.T, grad_out)
+        total = term if total is None else total + term
+    gwd_ref[...] = total.astype(BF16)
 
 
 def ffn(normed, grad_out, w_gate, w_up, w_down, units, number, count, into):
     tokens, width = normed.shape
+    one = pl.Buffered(1)
     return call(
         ffn_kernel,
         (1,),
-        [whole(tokens, width)] * 2
-        + [columns(width, units, number)] * 2
-        + [pl.BlockSpec((units, width), lambda i: (number, 0))],
+        [held(tokens, width)] * 2
+        + [pl.BlockSpec((width, units), lambda i: (0, number), pipeline_mode=one)] * 2
+        + [pl.BlockSpec((units, width), lambda i: (number, 0), pipeline_mode=one)],
         [(columns(tokens, units, number), (tokens, units * count), BF16)] * 3
         + [(whole(units, width), (units, width), BF16)],
         (normed, grad_out, w_gate, w_up, w_down),
@@ -404,7 +446,8 @@
     return call(
         weight_grads_kernel,
         (width // block,),
-        [rows(block, tokens)] + [pl.BlockSpec((tokens, units), lambda i, at=at: (0, at)) for at in numbers],
+        [rows(block, tokens)]
+        + [pl.BlockSpec((tokens, units), lambda i, at=at: (0, at), pipeline_mode=pl.Buffered(1)) for at in numbers],
         [(rows(block, units), (width, units), BF16)] * len(grads),
         (left, *grads),
         20,
@@ -419,17 +462,17 @@
     out_ref[...] = dot(left[...], right_ref[...]).astype(BF16)
 
 
-def row_grads(left, right, number):
+def row_grads(left, right, number, tall):
     tokens, width = right.shape
     block = 512
     return call(
         row_grads_kernel,
         (width // block,),
-        [pl.BlockSpec((tokens, CHUNK), lambda i: (0, number)), columns(tokens, block)],
-        [(columns(CHUNK, block), (CHUNK, width), BF16)],
+        [pl.BlockSpec((tokens, tall), lambda i: (0, number)), columns(tokens, block)],
+        [(columns(tall, block), (tall, width), BF16)],
         (left, right),
         24,
-        scratch=[pltpu.VMEM((CHUNK, tokens), BF16)],
+        scratch=[pltpu.VMEM((tall, tokens), BF16)],
     )[0]
 
 
@@ -463,10 +506,11 @@
     return call(
         lambda *refs: products_kernel(turn, counts, *refs),
         (width // block,),
-        [whole(*left.shape) for left in lefts] + specs,
+        [held(*left.shape) for left in lefts] + specs,
         [(columns(tokens, block), (tokens, width), BF16)],
         (*lefts, *weights),
         26,
+        name="products",
     )[0]
 
 
@@ -477,10 +521,10 @@
     return total
 
 
-def norm_back_kernel(n, low, dn_ref, do_ref, gain_ref, base_ref, *refs):
+def norm_back_kernel(n, low, own_ref, other_ref, gain_ref, base_ref, *refs):
     values = summed(refs[:n])
     out_ref, more, gain_grad_ref = refs[n], refs[n + 1 : -1], refs[-1]
-    grad_normed = dn_ref[...].astype(F32) + do_ref[...].astype(F32)
+    grad_normed = own_ref[...].astype(F32) + other_ref[...].astype(F32)
     inv_rms = lax.rsqrt(jnp.mean(values * values, axis=1, keepdims=True) + EPSILON)
     weighted = grad_normed * gain_ref[...]
     inner = jnp.mean(weighted * values, axis=1, keepdims=True)
@@ -510,6 +554,7 @@
         outs,
         (own, other, gain, base, *values),
         28,
+        name="norm_back",
     )
 
 
@@ -530,26 +575,23 @@
     )[0]
 
 
-def relay_kernel(section_ref, half_ref, left_ref, right_ref, out_ref):
-    cut = left_ref.shape[1]
-    out_ref[...] = half_ref[...]
-    for section, ref, lanes in ((1, left_ref, slice(0, cut)), (2, right_ref, slice(cut, 2 * cut))):
-
-        @pl.when(section_ref[0] == section)
-        def _():
-            out_ref[:, lanes] = (half_ref[:, lanes].astype(F32) + ref[...].astype(F32)).astype(BF16)
-
-
-def relayed(section, half, left, right):
-    tokens, width = half.shape
+def sum_kernel(*refs):
+    total = refs[0][...].astype(F32)
+    for ref in refs[1:-1]:
+        total = total + ref[...].astype(F32)
+    refs[-1][...] = total.astype(BF16)
+
+
+def total_of(*arrays):
+    tokens, width = arrays[0].shape
     block = 512
     return call(
-        relay_kernel,
+        sum_kernel,
         (tokens // block,),
-        [pl.BlockSpec(memory_space=pltpu.SMEM), rows(block, width)] + [rows(block, width // 2)] * 2,
+        [rows(block, width)] * len(arrays),
         [(rows(block, width), (tokens, width), BF16)],
-        (section.astype(jnp.int32)[None], half, left, right),
-        16,
+        arrays,
+        24,
     )[0]
 
 
@@ -558,26 +600,25 @@
 
     @pl.when(section_ref[0] == 0)
     def _():
-        half = half_ref[...].astype(F32)
-        total = half
+        total = half_ref[...].astype(F32)
         for ref in refs[:-1]:
             total = total + ref[...].astype(F32)
-        out_ref[...] = (half + total).astype(BF16)
+        out_ref[...] = total.astype(BF16)
 
     @pl.when(section_ref[0] != 0)
     def _():
         out_ref[...] = half_ref[...]
 
 
-def first_grad(section, half, arrived):
+def first_grad(section, half, terms):
     tokens, width = half.shape
-    block = 256
+    block = 512
     return call(
         first_grad_kernel,
         (tokens // block,),
-        [pl.BlockSpec(memory_space=pltpu.SMEM)] + [rows(block, width)] * (1 + len(arrived)),
+        [pl.BlockSpec(memory_space=pltpu.SMEM)] + [rows(block, width)] * (1 + len(terms)),
         [(rows(block, width), (tokens, width), BF16)],
-        (section.astype(jnp.int32)[None], half, *arrived),
+        (section.astype(jnp.int32)[None], half, *terms),
         24,
     )[0]
 
@@ -591,25 +632,26 @@
         return pl.BlockSpec(block, lambda i, j, flags: (i * flags[flag], j * flags[flag]))
 
     block, at = out
-    held = [] if into is None else [into]
+    kept = [] if into is None else [into]
     n = len(args)
 
     def body(flags_ref, *refs):
-        kernel(flags_ref, *refs[:n], *refs[n + len(held) :])
+        kernel(flags_ref, *refs[:n], *refs[n + len(kept) :])
 
     return pl.pallas_call(
         body,
+        name=kernel.__name__.removesuffix("_kernel"),
         grid_spec=pltpu.PrefetchScalarGridSpec(
             num_scalar_prefetch=1,
             grid=grid,
-            in_specs=[spec(*one) for one in ins] + [pl.BlockSpec(memory_space=pl.ANY)] * len(held),
+            in_specs=[spec(*one) for one in ins] + [pl.BlockSpec(memory_space=pl.ANY)] * len(kept),
             out_specs=pl.BlockSpec(block, lambda i, j, flags: at(i, j)),
         ),
         out_shape=jax.ShapeDtypeStruct(shape, dtype),
-        input_output_aliases={1 + n: 0} if held else {},
+        input_output_aliases={1 + n: 0} if kept else {},
         compiler_params=pltpu.CompilerParams(vmem_limit_bytes=10 * MIB),
         cost_estimate=pl.CostEstimate(flops=1, bytes_accessed=1, transcendentals=0),
-    )(flags, *args, *held)
+    )(flags, *args, *kept)
 
 
 MID, END = 0, 1
@@ -632,7 +674,7 @@
 
 
 class Line:
-    def __init__(self, axis, size, shapes, depth=3):
+    def __init__(self, axis, size, shapes, depth=DEPTH):
         self.axis, self.size, self.shapes, self.depth = axis, size, shapes, depth
         place = lax.axis_index(axis)
         end = (place == 0) | (place == 3)
@@ -646,8 +688,8 @@
     def after(self, *values):
         if not self.clock:
             return values if len(values) > 1 else values[0]
-        held = tie(*values, *self.clock)[: len(values)]
-        return held if len(values) > 1 else held[0]
+        tied = tie(*values, *self.clock)[: len(values)]
+        return tied if len(values) > 1 else tied[0]
 
     def mark(self, *values):
         self.clock = list(values)
@@ -666,8 +708,9 @@
 
     def add(self, one, two):
         tall, wide = one.shape
-        block = (min(tall, 512), wide)
+        block = (max(tall // 2, 16), wide)
         ins = [(block, MID)] * 2
+        block = (tall, wide) if tall < 32 else block
         return chosen_call(
             add_kernel, (tall // block[0], 1), self.flags, ins, (block, lambda i, j: (i, j)), one.shape, BF16, (one, two)
         )
@@ -687,7 +730,6 @@
             self.total[i - 1] = self.add(half, arrived)
             self.outward[i - 1] = lax.ppermute(self.total[i - 1], self.axis, [(1, 0), (2, 3)])
             self.mark(self.total[i - 1])
-        self.start()
         if 0 <= i - 2 < n:
             total, arrived = self.after(self.total[i - 2], self.outward[i - 2])
             name, block, at = self.places[i - 2]
@@ -704,11 +746,14 @@
                 self.outs[name],
             )
             self.mark(self.outs[name])
-
-    def finish(self):
+        self.start()
+
+    def finish(self, left=0):
         if self.size == 4:
-            while self.at < len(self.parts) + 2:
+            while self.at < len(self.parts) + 2 - left:
                 self.step(True)
+            return
+        if left:
             return
         for part, (name, block, at) in zip(self.parts, self.places):
             if self.outs[name] is None:
@@ -797,11 +842,10 @@
         line.step()
 
     def unit_grads(number):
-        if number < n_blocks:
-            gate, up = weight_grads(line.after(turned_ffn), acts[1:], UNITS, (number, number))
-            line.mark(gate, up)
-            line.push(gate, *put_columns("gate", number, UNITS))
-            line.push(up, *put_columns("up", number, UNITS))
+        gate, up = weight_grads(line.after(turned_ffn), acts[1:], UNITS, (number, number))
+        line.mark(gate, up)
+        line.push(gate, *put_columns("gate", number, UNITS))
+        line.push(up, *put_columns("up", number, UNITS))
 
     unit_grads(0)
     line.step()
@@ -811,68 +855,73 @@
     line.step()
     unit_grads(1)
     line.step()
+    unit_grads(2)
+    line.step()
+    line.step()
     grad_middle, grad_attn, grad_gain_ffn = norm_back(line.after(part), part_other, middle, gain_ffn, grad_out, True)
     line.mark(grad_attn)
     line.step()
-    for number in range(2, n_blocks):
-        unit_grads(number)
-    for number in range(heads.shape[1] // CHUNK):
-        part = row_grads(line.after(heads), grad_attn, number)
-        line.mark(part)
-        line.push(part, *put_rows("out", number * CHUNK // 128, 128))
-    line.step()
-
-    def column_grads(name, grad):
-        numbers = tuple(range(grad.shape[1] // CHUNK))
-        parts = weight_grads(line.after(turned_attn), [grad] * len(numbers), CHUNK, numbers)
-        line.mark(*parts)
-        for number, part in zip(numbers, parts):
-            line.push(part, *put_columns(name, number, CHUNK))
-
-    pairs = queries.shape[1] // (2 * HD)
-    grads = [None] * 3
-    for first in range(pairs):
-        grads = attend_back(queries, keys, mixed, probs, line.after(grad_attn), w_out, cos, sin, first, 1, grads)
-        line.mark(*grads)
-        if first < pairs - 1:
-            line.step()
-    grad_query, grad_key, half_mixed = grads
+
+    grad_heads, half_mixed = value_back(probs, line.after(grad_attn), w_out)
+    line.mark(grad_heads)
     if relay:
-        from_left, from_right = send(half_mixed[:, : half_mixed.shape[1] // 2], (3, 1)), send(
-            half_mixed[:, half_mixed.shape[1] // 2 :], (3, 2)
-        )
+        arrived = [send(half_mixed, (1, 0), (3, 2))]
     else:
         arrived = [send(half_mixed, (s, 0)) for s in range(1, n_sections)]
+    line.step()
+    wide = heads.shape[1] // 2
+    for number in range(2):
+        part = row_grads(line.after(heads), grad_attn, number, wide)
+        line.mark(part)
+        line.push(part, *put_rows("out", number * wide // 128, 128))
+    line.step()
+    pairs = queries.shape[1] // (2 * HD)
+    grads = attend_back(queries, keys, mixed, probs, line.after(grad_heads), cos, sin, 0, pairs // 2, [None] * 2)
+    line.mark(*grads)
+    line.step()
+    terms = [half_mixed, line.after(arrived[0])] + arrived[1:]
+    if relay:
+        both = total_of(*terms)
+        line.mark(both)
+        terms = [both, send(both, (2, 0))]
+    line.step()
+    grad_query, grad_key = attend_back(
+        queries, keys, mixed, probs, line.after(grad_heads), cos, sin, pairs // 2, pairs - pairs // 2, grads
+    )
+    line.mark(grad_query)
+
+    def column_grads(name, grad):
+        for number, part in enumerate(weight_grads(line.after(turned_attn), [grad] * 2, wide, (0, 1))):
+            line.push(part, *put_columns(name, number, wide))
+        line.mark(part)
+
     column_grads("query", grad_query)
     column_grads("key", grad_key)
     line.step()
-    part_result = products([((acts[0], line.after(rest_acts[0])), w_down)], False)
-    result_other = exchange(part_result, "tensor")
-    line.mark(part_result)
-    line.step()
-    if relay:
-        both = relayed(section, line.after(half_mixed), from_left, from_right)
-        arrived = [send(both, (s, 0)) for s in (1, 2)]
-        line.mark(both)
-    line.step()
-    result = block_result(line.after(part_result), result_other, middle)
-    line.mark(result)
-    line.step()
-    grad_value = first_grad(section, line.after(half_mixed), arrived)
+    grad_value = first_grad(section, half_mixed, [line.after(terms[0])] + terms[1:])
+    line.mark(grad_value)
     column_grads("value", grad_value)
+    line.step()
     part = products(
         [((line.after(grad_query),), w_query), ((grad_key,), w_key), ((grad_value,), w_value)], True
     )
     part_other = exchange(part, "tensor")
     line.mark(part)
-    line.step()
-    line.step()
+    for _ in range(GWAIT):
+        line.step()
     grad_input, grad_gain_attn = norm_back(line.after(part), part_other, (x,), gain_attn, grad_middle, False)
     line.mark(grad_input)
     gains = jnp.concatenate([grad_gain_attn, grad_gain_ffn], axis=0)
     gains = jnp.pad(gains, ((0, 14), (0, 0))).astype(BF16)
     line.push(gains, "gains", (16, width), lambda i, j: (0, 0))
+    line.step()
+    part_result = products([((acts[0], line.after(rest_acts[0])), w_down)], False)
+    line.mark(part_result)
+    line.finish(LAST)
+    part_result = line.after(part_result)
+    result_other = exchange(part_result, "tensor")
     line.finish()
+    result = block_result(part_result, line.after(result_other), middle)
 
     outs = line.outs
     return (

time: 470 us -> 446 us (0.949)
  starting transfers between devices: 161 us -> 133 us
    ppermute x21, starting transfers between devices: 98.8 us -> 73.8 us  [start(): self.inward[i] = lax.ppermute(self.parts[i], self.axis, [(0, 1), (3, 2)])]
    ppermute x21, waiting for transfers between devices: 57 us -> 81.6 us  [step(): lax.ppermute(self.total[i - 1], self.axis, [(1, 0), (2, 3)])]
    ppermute x21, waiting for transfers between devices: 33.6 us -> 10.1 us  [start(): self.inward[i] = lax.ppermute(self.parts[i], self.axis, [(0, 1), (3, 2)])]
    ppermute x8 -> x6, starting transfers between devices: 19.5 us -> 15.9 us  [send(): return lax.ppermute(block, 'section', list(pairs))]
    unnamed x120 -> x94, local copies, waits for them, and re-layouts: 10.8 us -> 7.32 us
    pallas_call x93 -> x92, Pallas kernels: 188 us -> 191 us  [the longest x29 126 us: call(): pl.pallas_call(body, grid=grid, name=name or kernel.__name__.removesuffix...]
  transfers between devices with their start and end apart: 75 -> 73, of which waited for: 23 -> 17; matrix products, arithmetic and copies ran while one was open for 1% -> 1% of each run, Pallas kernels for 31% -> 38%
where the time goes in v3:
time: 446 us; the launch traced here: 439 us
  Pallas kernels  191 us (43%)
  starting transfers between devices  133 us (30%)
  waiting for transfers between devices  97.9 us (22%)
  local copies, waits for them, and re-layouts  7.93 us (2%)
  other arithmetic  5.31 us (1%)
    pallas_call x29, Pallas kernels, call(): pl.pallas_call(body, grid=grid, name=name or kernel.__name__.removesuffix...  126 us
    ppermute x21, waiting for transfers between devices, step(): lax.ppermute(self.total[i - 1], self.axis, [(1, 0), (2, 3)])  81.6 us
    ppermute x21, starting transfers between devices, start(): self.inward[i] = lax.ppermute(self.parts[i], self.axis, [(0, 1), (3, 2)])  73.8 us
    pallas_call x63, Pallas kernels, chosen_call(): pl.pallas_call(body, name=kernel.__name__.removesuffix('_kernel'), grid_s...  65.6 us
    ppermute x21, starting transfers between devices, step(): lax.ppermute(self.total[i - 1], self.axis, [(1, 0), (2, 3)])  28.5 us
    ppermute x6, starting transfers between devices, send(): return lax.ppermute(block, 'section', list(pairs))  15.9 us
    ppermute x21, starting transfers between devices, step(): self.across[i] = lax.ppermute(self.half[i], self.axis, [(1, 2), (2, 1)])  14.9 us
    ppermute x21, waiting for transfers between devices, start(): self.inward[i] = lax.ppermute(self.parts[i], self.axis, [(0, 1), (3, 2)])  10.1 us
  transfers between devices with their start and end apart: 73, of which 17 were waited for; matrix products, arithmetic and copies ran while one was open for 1% of the time, Pallas kernels for 38%

profile of v3, /device:TPU:0, one launch (start us, length us, event | category | flops | bytes accessed | tf_op | source)
XLA Modules:
  0.0 438.6 jit_solution(10716056196466879719)
XLA Ops:
  0.7 5.0 %value.1 = (bf16[1024,1024]{1,0:T(8,128)(2,1)}, bf16[1024,256]{1,0:T(8,128)(2,1)}, bf16[1024,256]{1,0:T(8,128)(2,1)}) custom-call(bf16[1024,1024]{1,0:T(8,128)(2,1)} %bitcast.47, f32[1,1024]{1,0:T(1,128)} %refs_2_.3, bf16[1024,512]{1,0:T(8,128)(2,1)} %bitcast.56), custom_call_target="tpu_custom_call" | custom-call | flops 1 | bytes 1 | tf_op jit(solution)/shard_map/value/pallas_call | solution.py:44
  5.7 5.9 %collective-permute-start = (bf16[1024,256]{1,0:T(8,128)(2,1)}, bf16[1024,256]{1,0:T(8,128)(2,1)}, u32[]{:S(2)}, u32[]{:S(2)}) collective-permute-start(bf16[1024,256]{1,0:T(8,128)(2,1)} %get-tuple-element.240.refs_2_), channel_id=1, source_target_pairs={{0,8},{1,9},{2,10},{3,11},{4,12},{5,13},{6,14},{7,15}} | collective-permute-start | bytes 1572872 | tf_op jit(solution)/shard_map/ppermute | solution.py:807
  31.9 10.5 %probs.1.refs_1_.probs_ref.refs_3_ = bf16[8,1024,768]{2,1,0:T(8,128)(2,1)} custom-call(s32[1,4]{1,0:T(1,128)S(1)} %copy-done.43, bf16[1024,512]{1,0:T(8,128)(2,1)S(1)} %get-tuple-element.244.q_ref.refs_0_, bf16[1024,512]{1,0:T(8,128)(2,1)S(1)} %get-tuple-element.245.k_ref.refs_1_), custom_call_target="tpu_custom_call" | custom-call | flops 1 | bytes 1 | tf_op jit(solution)/shard_map/probs/pallas_call | solution.py:44
  42.5 8.1 %heads.1 = (bf16[1024,512]{1,0:T(8,128)(2,1)S(1)}, bf16[1024,512]{1,0:T(8,128)(2,1)S(1)}, bf16[1024,1024]{1,0:T(8,128)(2,1)S(1)}) custom-call(s32[1]{0:T(128)} %bitcast.1.refs_0_.section_ref, bf16[8,1024,768]{2,1,0:T(8,128)(2,1)} %probs.1.refs_1_.probs_ref.refs_3_, bf16[1024,256]{1,0:T(8,128)(2,1)S(1)} %copy-done.34, bf16[1024,256]{1,0:T(8,128)(2,1)S(1)} %copy-done.35, ...), custom_call_target="tpu_custom_call" | custom-call | flops 1 | bytes 1 | tf_op jit(solution)/shard_map/heads/pallas_call | solution.py:44
  58.1 8.3 %entry.1 = (bf16[1024,1024]{1,0:T(8,128)(2,1)}, bf16[1024,256]{1,0:T(8,128)(2,1)}, bf16[1024,256]{1,0:T(8,128)(2,1)}, bf16[1024,256]{1,0:T(8,128)(2,1)}, bf16[256,1024]{1,0:T(8,128)(2,1)}) custom-call(bf16[1024,1024]{1,0:T(8,128)(2,1)} %bitcast.48, bf16[1024,1024]{1,0:T(8,128)(2,1)} %copy-done.9, bf16[1024,1024]{1,0:T(8,128)(2,1)} %copy-done.12, ...), custom_call_target="tpu_custom_call" | custom-call | flops 1 | bytes 1 | tf_op jit(solution)/shard_map/entry/pallas_call | solution.py:44
  76.9 6.3 %ffn.3 = (bf16[1024,1152]{1,0:T(8,128)(2,1)S(1)}, bf16[1024,1152]{1,0:T(8,128)(2,1)S(1)}, bf16[1024,1152]{1,0:T(8,128)(2,1)S(1)}, bf16[384,1024]{1,0:T(8,128)(2,1)S(1)}) custom-call(bf16[1024,1024]{1,0:T(8,128)(2,1)S(1)} %copy-done.6, bf16[1024,1024]{1,0:T(8,128)(2,1)S(1)} %bitcast.43, bf16[1024,1408]{1,0:T(8,128)(2,1)} %bitcast.26, ...), custom_call_target="tpu_custom_call" | custom-call | flops 1 | bytes 1 | tf_op jit(solution)/shard_map/ffn/pallas_call | solution.py:44
  85.4 6.7 %collective-permute-start.12 = (bf16[384,1024]{1,0:T(8,128)(2,1)S(1)}, bf16[384,1024]{1,0:T(8,128)(2,1)S(1)}, u32[]{:S(2)}, u32[]{:S(2)}) collective-permute-start(bf16[384,1024]{1,0:T(8,128)(2,1)S(1)} %get-tuple-element.297.refs_0_), channel_id=1, source_target_pairs={{0,2},{6,4},{1,3},{7,5},{8,10},{14,12},{9,11},{15,13},{16,18},{22,... | collective-permute-start | bytes 2359304 | tf_op jit(solution)/shard_map/ppermute | solution.py:706
  93.4 6.3 %ffn.4 = (bf16[1024,1152]{1,0:T(8,128)(2,1)S(1)}, bf16[1024,1152]{1,0:T(8,128)(2,1)S(1)}, bf16[1024,1152]{1,0:T(8,128)(2,1)S(1)}, bf16[384,1024]{1,0:T(8,128)(2,1)S(1)}) custom-call(bf16[1024,1024]{1,0:T(8,128)(2,1)S(1)} %copy-done.6, bf16[1024,1024]{1,0:T(8,128)(2,1)S(1)} %bitcast.44, ...), custom_call_target="tpu_custom_call", output_to_operand_aliasing={{0}: (5, {}), {1}: (6, {}), {2}: (7, {})} | custom-call | flops 1 | bytes 1 | tf_op jit(solution)/shard_map/ffn/pallas_call | solution.py:44
  107.6 6.3 %ffn.5 = (bf16[1024,1152]{1,0:T(8,128)(2,1)S(1)}, bf16[1024,1152]{1,0:T(8,128)(2,1)S(1)}, bf16[1024,1152]{1,0:T(8,128)(2,1)S(1)}, bf16[384,1024]{1,0:T(8,128)(2,1)S(1)}) custom-call(bf16[1024,1024]{1,0:T(8,128)(2,1)S(1)} %copy-done.6, bf16[1024,1024]{1,0:T(8,128)(2,1)S(1)} %bitcast.45, ...), custom_call_target="tpu_custom_call", output_to_operand_aliasing={{0}: (5, {}), {1}: (6, {}), {2}: (7, {})} | custom-call | flops 1 | bytes 1 | tf_op jit(solution)/shard_map/ffn/pallas_call | solution.py:44
  113.9 7.8 %collective-permute-done.9.refs_1_ = bf16[1024,256]{1,0:T(8,128)(2,1)S(1)} collective-permute-done((bf16[1024,256]{1,0:T(8,128)(2,1)S(1)}, bf16[1024,256]{1,0:T(8,128)(2,1)S(1)}, u32[]{:S(2)}, u32[]{:S(2)}) %collective-permute-start.9) | collective-permute-done | bytes 524320 | tf_op jit(solution)/shard_map/ppermute | solution.py:706
  130.7 9.3 %collective-permute-start.14 = (bf16[384,1024]{1,0:T(8,128)(2,1)S(1)}, bf16[384,1024]{1,0:T(8,128)(2,1)S(1)}, u32[]{:S(2)}, u32[]{:S(2)}) collective-permute-start(bf16[384,1024]{1,0:T(8,128)(2,1)S(1)} %get-tuple-element.315.refs_0_), channel_id=1, source_target_pairs={{0,2},{6,4},{1,3},{7,5},{8,10},{14,12},{9,11},{15,13},{16,18},{22,... | collective-permute-start | bytes 2359304 | tf_op jit(solution)/shard_map/ppermute | solution.py:706
  143.7 7.4 %products.3.refs_0_ = bf16[1024,1024]{1,0:T(8,128)(2,1)S(1)} custom-call(bf16[1024,1152]{1,0:T(8,128)(2,1)S(1)} %get-tuple-element.283.refs_0_, bf16[1024,256]{1,0:T(8,128)(2,1)S(1)} %copy-done.37, bf16[1024,1152]{1,0:T(8,128)(2,1)S(1)} %get-tuple-element.294.refs_1_.refs_2_, bf16[1024,256]{1,0:T(8,128)(2,1)S(1)} %copy-done.38, ...), custom_call_target="tpu_custom_call" | custom-call | flops 1 | bytes 1 | tf_op jit(solution)/shard_map/products/pallas_call | solution.py:44
  155.8 14.7 %collective-permute-done.15.refs_1_ = bf16[1024,256]{1,0:T(8,128)(2,1)S(1)} collective-permute-done((bf16[1024,256]{1,0:T(8,128)(2,1)S(1)}, bf16[1024,256]{1,0:T(8,128)(2,1)S(1)}, u32[]{:S(2)}, u32[]{:S(2)}) %collective-permute-start.15) | collective-permute-done | bytes 524320 | tf_op jit(solution)/shard_map/ppermute | solution.py:731
  181.0 6.4 %collective-permute-done.20.refs_1_ = bf16[384,1024]{1,0:T(8,128)(2,1)S(1)} collective-permute-done((bf16[384,1024]{1,0:T(8,128)(2,1)S(1)}, bf16[384,1024]{1,0:T(8,128)(2,1)S(1)}, u32[]{:S(2)}, u32[]{:S(2)}) %collective-permute-start.20) | collective-permute-done | bytes 786464 | tf_op jit(solution)/shard_map/ppermute | solution.py:731
  197.2 7.0 %collective-permute-done.25.refs_1_ = bf16[384,1024]{1,0:T(8,128)(2,1)S(1)} collective-permute-done((bf16[384,1024]{1,0:T(8,128)(2,1)S(1)}, bf16[384,1024]{1,0:T(8,128)(2,1)S(1)}, u32[]{:S(2)}, u32[]{:S(2)}) %collective-permute-start.25) | collective-permute-done | bytes 786464 | tf_op jit(solution)/shard_map/ppermute | solution.py:731
  211.5 9.6 %collective-permute-done.22.refs_1_ = bf16[384,1024]{1,0:T(8,128)(2,1)S(1)} collective-permute-done((bf16[384,1024]{1,0:T(8,128)(2,1)S(1)}, bf16[384,1024]{1,0:T(8,128)(2,1)S(1)}, u32[]{:S(2)}, u32[]{:S(2)}) %collective-permute-start.22) | collective-permute-done | bytes 786464 | tf_op jit(solution)/shard_map/ppermute | solution.py:731
  240.8 8.0 %value_back.1 = (bf16[1024,512]{1,0:T(8,128)(2,1)S(1)}, bf16[1024,512]{1,0:T(8,128)(2,1)S(1)}) custom-call(bf16[8,1024,768]{2,1,0:T(8,128)(2,1)S(1)} %bitcast.23, bf16[1024,1024]{1,0:T(8,128)(2,1)S(1)} %get-tuple-element.347.attn_ref.right_ref, bf16[512,1024]{1,0:T(8,128)(2,1)S(1)} %bitcast.59), custom_call_target="tpu_custom_call" | custom-call | flops 1 | bytes 1 | tf_op jit(solution)/shard_map/value_back/pallas_call | solution.py:44
  272.4 8.2 %attend_back.2 = (bf16[1024,512]{1,0:T(8,128)(2,1)S(1)}, bf16[1024,512]{1,0:T(8,128)(2,1)S(1)}) custom-call(bf16[1024,512]{1,0:T(8,128)(2,1)S(1)} %copy-done.16, bf16[1024,512]{1,0:T(8,128)(2,1)S(1)} %copy-done.18, bf16[1024,512]{1,0:T(8,128)(2,1)S(1)} %copy-done.24, bf16[8,1024,768]{2,1,0:T(8,128)(2,1)S(1)} %bitcast.23, ...), custom_call_target="tpu_custom_call" | custom-call | flops 1 | bytes 1 | tf_op jit(solution)/shard_map/attend_back/pallas_call | solution.py:44
  302.0 5.6 %collective-permute-done.38.refs_1_ = bf16[1024,384]{1,0:T(8,128)(2,1)S(1)} collective-permute-done((bf16[1024,384]{1,0:T(8,128)(2,1)S(1)}, bf16[1024,384]{1,0:T(8,128)(2,1)S(1)}, u32[]{:S(2)}, u32[]{:S(2)}) %collective-permute-start.38) | collective-permute-done | bytes 786464 | tf_op jit(solution)/shard_map/ppermute | solution.py:731
  309.4 8.2 %attend_back.3 = (bf16[1024,512]{1,0:T(8,128)(2,1)S(1)}, bf16[1024,512]{1,0:T(8,128)(2,1)S(1)}) custom-call(bf16[1024,512]{1,0:T(8,128)(2,1)S(1)} %copy-done.16, bf16[1024,512]{1,0:T(8,128)(2,1)S(1)} %copy-done.18, bf16[1024,512]{1,0:T(8,128)(2,1)S(1)} %copy-done.24, ...), custom_call_target="tpu_custom_call", output_to_operand_aliasing={{0}: (7, {}), {1}: (8, {})} | custom-call | flops 1 | bytes 1 | tf_op jit(solution)/shard_map/attend_back/pallas_call | solution.py:44
  351.4 7.5 %collective-permute-done.56.refs_1_ = bf16[256,1024]{1,0:T(8,128)(2,1)S(1)} collective-permute-done((bf16[256,1024]{1,0:T(8,128)(2,1)S(1)}, bf16[256,1024]{1,0:T(8,128)(2,1)S(1)}, u32[]{:S(2)}, u32[]{:S(2)}) %collective-permute-start.56) | collective-permute-done | bytes 524320 | tf_op jit(solution)/shard_map/ppermute | solution.py:731
  376.4 4.9 %collective-permute-done.59.refs_1_ = bf16[1024,256]{1,0:T(8,128)(2,1)S(1)} collective-permute-done((bf16[1024,256]{1,0:T(8,128)(2,1)S(1)}, bf16[1024,256]{1,0:T(8,128)(2,1)S(1)}, u32[]{:S(2)}, u32[]{:S(2)}) %collective-permute-start.59) | collective-permute-done | bytes 524320 | tf_op jit(solution)/shard_map/ppermute | solution.py:731
  387.8 5.7 %collective-permute-done.64.refs_1_ = bf16[1024,256]{1,0:T(8,128)(2,1)S(1)} collective-permute-done((bf16[1024,256]{1,0:T(8,128)(2,1)S(1)}, bf16[1024,256]{1,0:T(8,128)(2,1)S(1)}, u32[]{:S(2)}, u32[]{:S(2)}) %collective-permute-start.64) | collective-permute-done | bytes 524320 | tf_op jit(solution)/shard_map/ppermute | solution.py:731
  420.3 12.5 %collective-permute-done.72.refs_1_ = bf16[1024,256]{1,0:T(8,128)(2,1)S(1)} collective-permute-done((bf16[1024,256]{1,0:T(8,128)(2,1)S(1)}, bf16[1024,256]{1,0:T(8,128)(2,1)S(1)}, u32[]{:S(2)}, u32[]{:S(2)}) %collective-permute-start.72) | collective-permute-done | bytes 524320 | tf_op jit(solution)/shard_map/ppermute | solution.py:731
  (322 shorter events, 249.3 us)
Async XLA Ops:
  75.0 24.7 %collective-permute-start.7 = (bf16[1024,256]{1,0:T(8,128)(2,1)S(1)}, bf16[1024,256]{1,0:T(8,128)(2,1)S(1)}, u32[]{:S(2)}, u32[]{:S(2)}) collective-permute-start(bf16[1024,256]{1,0:T(8,128)(2,1)S(1)} %get-tuple-element.271.refs_0_), channel_id=1, source_target_pairs={{0,2},{6,4},{1,3},{7,5},{8,10},{14,12},{9,11},{15,13},{16,18},{22,... | collective-permute-start | bytes 1572872 | tf_op jit(solution)/shard_map/ppermute | solution.py:706
  85.4 44.0 %collective-permute-start.12 = (bf16[384,1024]{1,0:T(8,128)(2,1)S(1)}, bf16[384,1024]{1,0:T(8,128)(2,1)S(1)}, u32[]{:S(2)}, u32[]{:S(2)}) collective-permute-start(bf16[384,1024]{1,0:T(8,128)(2,1)S(1)} %get-tuple-element.297.refs_0_), channel_id=1, source_target_pairs={{0,2},{6,4},{1,3},{7,5},{8,10},{14,12},{9,11},{15,13},{16,18},{22,... | collective-permute-start | bytes 2359304 | tf_op jit(solution)/shard_map/ppermute | solution.py:706
  92.1 29.6 %collective-permute-start.9 = (bf16[1024,256]{1,0:T(8,128)(2,1)S(1)}, bf16[1024,256]{1,0:T(8,128)(2,1)S(1)}, u32[]{:S(2)}, u32[]{:S(2)}) collective-permute-start(bf16[1024,256]{1,0:T(8,128)(2,1)S(1)} %get-tuple-element.286.refs_0_), channel_id=1, source_target_pairs={{0,2},{6,4},{1,3},{7,5},{8,10},{14,12},{9,11},{15,13},{16,18},{22,... | collective-permute-start | bytes 1572872 | tf_op jit(solution)/shard_map/ppermute | solution.py:706
  102.9 48.2 %collective-permute-start.17 = (bf16[384,1024]{1,0:T(8,128)(2,1)S(1)}, bf16[384,1024]{1,0:T(8,128)(2,1)S(1)}, u32[]{:S(2)}, u32[]{:S(2)}) collective-permute-start(bf16[384,1024]{1,0:T(8,128)(2,1)S(1)} %get-tuple-element.306.refs_0_), channel_id=1, source_target_pairs={{0,2},{6,4},{1,3},{7,5},{8,10},{14,12},{9,11},{15,13},{16,18},{22,... | collective-permute-start | bytes 2359304 | tf_op jit(solution)/shard_map/ppermute | solution.py:706
  130.0 23.8 %collective-permute-start.16 = (bf16[384,1024]{1,0:T(8,128)(2,1)S(1)}, bf16[384,1024]{1,0:T(8,128)(2,1)S(1)}, u32[]{:S(2)}, u32[]{:S(2)}) collective-permute-start(bf16[384,1024]{1,0:T(8,128)(2,1)S(1)} %add.51.refs_0_), channel_id=1, source_target_pairs={{2,4},{4,2},{3,5},{5,3},{10,12},{12,10},{11,13},{13,11},{18,20},{2... | collective-permute-start | bytes 2359304 | tf_op jit(solution)/shard_map/ppermute | solution.py:726
  130.7 47.0 %collective-permute-start.14 = (bf16[384,1024]{1,0:T(8,128)(2,1)S(1)}, bf16[384,1024]{1,0:T(8,128)(2,1)S(1)}, u32[]{:S(2)}, u32[]{:S(2)}) collective-permute-start(bf16[384,1024]{1,0:T(8,128)(2,1)S(1)} %get-tuple-element.315.refs_0_), channel_id=1, source_target_pairs={{0,2},{6,4},{1,3},{7,5},{8,10},{14,12},{9,11},{15,13},{16,18},{22,... | collective-permute-start | bytes 2359304 | tf_op jit(solution)/shard_map/ppermute | solution.py:706
  151.8 27.3 %collective-permute-start.21 = (bf16[384,1024]{1,0:T(8,128)(2,1)S(1)}, bf16[384,1024]{1,0:T(8,128)(2,1)S(1)}, u32[]{:S(2)}, u32[]{:S(2)}) collective-permute-start(bf16[384,1024]{1,0:T(8,128)(2,1)S(1)} %add.53.refs_0_), channel_id=1, source_target_pairs={{2,4},{4,2},{3,5},{5,3},{10,12},{12,10},{11,13},{13,11},{18,20},{2... | collective-permute-start | bytes 2359304 | tf_op jit(solution)/shard_map/ppermute | solution.py:726
  154.4 33.0 %collective-permute-start.20 = (bf16[384,1024]{1,0:T(8,128)(2,1)S(1)}, bf16[384,1024]{1,0:T(8,128)(2,1)S(1)}, u32[]{:S(2)}, u32[]{:S(2)}) collective-permute-start(bf16[384,1024]{1,0:T(8,128)(2,1)S(1)} %add.54.refs_0_), channel_id=1, source_target_pairs={{2,0},{4,6},{3,1},{5,7},{10,8},{12,14},{11,9},{13,15},{18,16},{20,... | collective-permute-start | bytes 2359304 | tf_op jit(solution)/shard_map/ppermute | solution.py:731
  155.7 69.9 %collective-permute-start.26 = (bf16[1024,1024]{1,0:T(8,128)(2,1)S(1)}, bf16[1024,1024]{1,0:T(8,128)(2,1)S(1)}, u32[]{:S(2)}, u32[]{:S(2)}) collective-permute-start(bf16[1024,1024]{1,0:T(8,128)(2,1)S(1)} %products.3.refs_0_), channel_id=1, source_target_pairs={{0,1},{1,0},{2,3},{3,2},{4,5},{5,4},{6,7},{7,6},{8,9},{9,8},{10,11... | collective-permute-start | bytes 6291464 | tf_op jit(solution)/shard_map/ppermute | solution.py:779
  170.5 23.5 %collective-permute-start.19 = (bf16[1024,384]{1,0:T(8,128)(2,1)S(1)}, bf16[1024,384]{1,0:T(8,128)(2,1)S(1)}, u32[]{:S(2)}, u32[]{:S(2)}) collective-permute-start(bf16[1024,384]{1,0:T(8,128)(2,1)S(1)} %get-tuple-element.325.refs_0_), channel_id=1, source_target_pairs={{0,2},{6,4},{1,3},{7,5},{8,10},{14,12},{9,11},{15,13},{16,18},{22,... | collective-permute-start | bytes 2359304 | tf_op jit(solution)/shard_map/ppermute | solution.py:706
  179.7 24.6 %collective-permute-start.25 = (bf16[384,1024]{1,0:T(8,128)(2,1)S(1)}, bf16[384,1024]{1,0:T(8,128)(2,1)S(1)}, u32[]{:S(2)}, u32[]{:S(2)}) collective-permute-start(bf16[384,1024]{1,0:T(8,128)(2,1)S(1)} %add.56.refs_0_), channel_id=1, source_target_pairs={{2,0},{4,6},{3,1},{5,7},{10,8},{12,14},{11,9},{13,15},{18,16},{20,... | collective-permute-start | bytes 2359304 | tf_op jit(solution)/shard_map/ppermute | solution.py:731
  195.9 25.1 %collective-permute-start.22 = (bf16[384,1024]{1,0:T(8,128)(2,1)S(1)}, bf16[384,1024]{1,0:T(8,128)(2,1)S(1)}, u32[]{:S(2)}, u32[]{:S(2)}) collective-permute-start(bf16[384,1024]{1,0:T(8,128)(2,1)S(1)} %add.58.refs_0_), channel_id=1, source_target_pairs={{2,0},{4,6},{3,1},{5,7},{10,8},{12,14},{11,9},{13,15},{18,16},{20,... | collective-permute-start | bytes 2359304 | tf_op jit(solution)/shard_map/ppermute | solution.py:731
  204.2 25.3 %collective-permute-start.29 = (bf16[1024,384]{1,0:T(8,128)(2,1)S(1)}, bf16[1024,384]{1,0:T(8,128)(2,1)S(1)}, u32[]{:S(2)}, u32[]{:S(2)}) collective-permute-start(bf16[1024,384]{1,0:T(8,128)(2,1)S(1)} %get-tuple-element.341.refs_0_), channel_id=1, source_target_pairs={{0,2},{6,4},{1,3},{7,5},{8,10},{14,12},{9,11},{15,13},{16,18},{22,... | collective-permute-start | bytes 2359304 | tf_op jit(solution)/shard_map/ppermute | solution.py:706
  209.9 28.1 %collective-permute-start.27 = (bf16[1024,384]{1,0:T(8,128)(2,1)S(1)}, bf16[1024,384]{1,0:T(8,128)(2,1)}, u32[]{:S(2)}, u32[]{:S(2)}) collective-permute-start(bf16[1024,384]{1,0:T(8,128)(2,1)S(1)} %add.60.refs_0_), channel_id=1, source_target_pairs={{2,0},{4,6},{3,1},{5,7},{10,8},{12,14},{11,9},{13,15},{18,16},{20,... | collective-permute-start | bytes 2359304 | tf_op jit(solution)/shard_map/ppermute | solution.py:731
  221.1 27.8 %collective-permute-start.33 = (bf16[1024,384]{1,0:T(8,128)(2,1)}, bf16[1024,384]{1,0:T(8,128)(2,1)}, u32[]{:S(2)}, u32[]{:S(2)}) collective-permute-start(bf16[1024,384]{1,0:T(8,128)(2,1)} %get-tuple-element.352.refs_0_), channel_id=1, source_target_pairs={{0,2},{6,4},{1,3},{7,5},{8,10},{14,12},{9,11},{15,13},{16,18},{22,... | collective-permute-start | bytes 2359304 | tf_op jit(solution)/shard_map/ppermute | solution.py:706
  231.6 26.6 %collective-permute-start.31 = (bf16[1024,384]{1,0:T(8,128)(2,1)S(1)}, bf16[1024,384]{1,0:T(8,128)(2,1)S(1)}, u32[]{:S(2)}, u32[]{:S(2)}) collective-permute-start(bf16[1024,384]{1,0:T(8,128)(2,1)S(1)} %add.62.refs_0_), channel_id=1, source_target_pairs={{2,0},{4,6},{3,1},{5,7},{10,8},{12,14},{11,9},{13,15},{18,16},{20,... | collective-permute-start | bytes 2359304 | tf_op jit(solution)/shard_map/ppermute | solution.py:731
  233.1 29.5 %collective-permute-start.30 = (bf16[1024,384]{1,0:T(8,128)(2,1)}, bf16[1024,384]{1,0:T(8,128)(2,1)S(1)}, u32[]{:S(2)}, u32[]{:S(2)}) collective-permute-start(bf16[1024,384]{1,0:T(8,128)(2,1)} %get-tuple-element.360.refs_0_), channel_id=1, source_target_pairs={{0,2},{6,4},{1,3},{7,5},{8,10},{14,12},{9,11},{15,13},{16,18},{22,... | collective-permute-start | bytes 2359304 | tf_op jit(solution)/shard_map/ppermute | solution.py:706
  253.3 27.4 %collective-permute-start.35 = (bf16[1024,384]{1,0:T(8,128)(2,1)S(1)}, bf16[1024,384]{1,0:T(8,128)(2,1)S(1)}, u32[]{:S(2)}, u32[]{:S(2)}) collective-permute-start(bf16[1024,384]{1,0:T(8,128)(2,1)S(1)} %get-tuple-element.370.refs_0_), channel_id=1, source_target_pairs={{0,2},{6,4},{1,3},{7,5},{8,10},{14,12},{9,11},{15,13},{16,18},{22,... | collective-permute-start | bytes 2359304 | tf_op jit(solution)/shard_map/ppermute | solution.py:706
  264.9 25.5 %collective-permute-start.41 = (bf16[1024,512]{1,0:T(8,128)(2,1)S(1)}, bf16[1024,512]{1,0:T(8,128)(2,1)S(1)}, u32[]{:S(2)}, u32[]{:S(2)}) collective-permute-start(bf16[1024,512]{1,0:T(8,128)(2,1)S(1)} %get-tuple-element.375.refs_0_.half_ref), channel_id=1, source_target_pairs={{8,0},{24,16},{9,1},{25,17},{10,2},{26,18},{11,3},{27,19},{12,4},{... | collective-permute-start | bytes 3145736 | tf_op jit(solution)/shard_map/ppermute | solution.py:807
  290.6 41.5 %collective-permute-start.49 = (bf16[1024,512]{1,0:T(8,128)(2,1)S(1)}, bf16[1024,512]{1,0:T(8,128)(2,1)S(1)}, u32[]{:S(2)}, u32[]{:S(2)}) collective-permute-start(bf16[1024,512]{1,0:T(8,128)(2,1)S(1)} %sum.1.refs_0_), channel_id=1, source_target_pairs={{16,0},{17,1},{18,2},{19,3},{20,4},{21,5},{22,6},{23,7}} | collective-permute-start | bytes 3145736 | tf_op jit(solution)/shard_map/ppermute | solution.py:807
  291.9 30.6 %collective-permute-start.44 = (bf16[256,1024]{1,0:T(8,128)(2,1)S(1)}, bf16[256,1024]{1,0:T(8,128)(2,1)S(1)}, u32[]{:S(2)}, u32[]{:S(2)}) collective-permute-start(bf16[256,1024]{1,0:T(8,128)(2,1)S(1)} %row_grads.3.refs_0_), channel_id=1, source_target_pairs={{0,2},{6,4},{1,3},{7,5},{8,10},{14,12},{9,11},{15,13},{16,18},{22,... | collective-permute-start | bytes 1572872 | tf_op jit(solution)/shard_map/ppermute | solution.py:706
  299.4 24.4 %collective-permute-start.43 = (bf16[256,1024]{1,0:T(8,128)(2,1)S(1)}, bf16[256,1024]{1,0:T(8,128)(2,1)S(1)}, u32[]{:S(2)}, u32[]{:S(2)}) collective-permute-start(bf16[256,1024]{1,0:T(8,128)(2,1)S(1)} %add.69.refs_0_), channel_id=1, source_target_pairs={{2,4},{4,2},{3,5},{5,3},{10,12},{12,10},{11,13},{13,11},{18,20},{2... | collective-permute-start | bytes 1572872 | tf_op jit(solution)/shard_map/ppermute | solution.py:726
  300.7 25.0 %collective-permute-start.48 = (bf16[1024,384]{1,0:T(8,128)(2,1)S(1)}, bf16[1024,384]{1,0:T(8,128)(2,1)S(1)}, u32[]{:S(2)}, u32[]{:S(2)}) collective-permute-start(bf16[1024,384]{1,0:T(8,128)(2,1)S(1)} %add.70.refs_0_), channel_id=1, source_target_pairs={{2,0},{4,6},{3,1},{5,7},{10,8},{12,14},{11,9},{13,15},{18,16},{20,... | collective-permute-start | bytes 2359304 | tf_op jit(solution)/shard_map/ppermute | solution.py:731
  342.2 52.9 %collective-permute-start.65 = (bf16[1024,1024]{1,0:T(8,128)(2,1)S(1)}, bf16[1024,1024]{1,0:T(8,128)(2,1)S(1)}, u32[]{:S(2)}, u32[]{:S(2)}) collective-permute-start(bf16[1024,1024]{1,0:T(8,128)(2,1)S(1)} %products.4.refs_0_), channel_id=1, source_target_pairs={{0,1},{1,0},{2,3},{3,2},{4,5},{5,4},{6,7},{7,6},{8,9},{9,8},{10,11... | collective-permute-start | bytes 6291464 | tf_op jit(solution)/shard_map/ppermute | solution.py:779
  (96 other events, 1191.6 us)

commit v4 on v3

--- a/solution.py
+++ b/solution.py
@@ -15,7 +15,7 @@
 UNITS = 384
 GWAIT = 4
 LAST = 2
-DEPTH = 3
+DEPTH = 2
 
 
 def dot(left, right):
@@ -849,6 +849,7 @@
 
     unit_grads(0)
     line.step()
+    line.depth = 3
     part = products([((acts[1], line.after(rest_acts[1])), w_gate), ((acts[2], rest_acts[2]), w_up)], True)
     part_other = exchange(part, "tensor")
     line.mark(part)
@@ -870,25 +871,32 @@
         arrived = [send(half_mixed, (s, 0)) for s in range(1, n_sections)]
     line.step()
     wide = heads.shape[1] // 2
+    pairs = queries.shape[1] // (2 * HD)
+    grads = [None] * 2
+
+    def some_pairs(first, count):
+        out = attend_back(queries, keys, mixed, probs, line.after(grad_heads), cos, sin, first, count, grads)
+        line.mark(*out)
+        return out
+
     for number in range(2):
         part = row_grads(line.after(heads), grad_attn, number, wide)
         line.mark(part)
         line.push(part, *put_rows("out", number * wide // 128, 128))
-    line.step()
-    pairs = queries.shape[1] // (2 * HD)
-    grads = attend_back(queries, keys, mixed, probs, line.after(grad_heads), cos, sin, 0, pairs // 2, [None] * 2)
-    line.mark(*grads)
+    cuts = [pairs * j // 4 for j in range(5)]
+    grads = some_pairs(cuts[0], cuts[1] - cuts[0])
+    line.step()
+    grads = some_pairs(cuts[1], cuts[2] - cuts[1])
     line.step()
     terms = [half_mixed, line.after(arrived[0])] + arrived[1:]
     if relay:
         both = total_of(*terms)
         line.mark(both)
         terms = [both, send(both, (2, 0))]
-    line.step()
-    grad_query, grad_key = attend_back(
-        queries, keys, mixed, probs, line.after(grad_heads), cos, sin, pairs // 2, pairs - pairs // 2, grads
-    )
-    line.mark(grad_query)
+    grads = some_pairs(cuts[2], cuts[3] - cuts[2])
+    line.step()
+    grads = some_pairs(cuts[3], cuts[4] - cuts[3])
+    grad_query, grad_key = grads
 
     def column_grads(name, grad):
         for number, part in enumerate(weight_grads(line.after(turned_attn), [grad] * 2, wide, (0, 1))):

time: 446 us -> 432 us (0.969)
  waiting for transfers between devices: 97.9 us -> 77.9 us
  starting transfers between devices: 133 us -> 141 us
    ppermute x21, waiting for transfers between devices: 81.6 us -> 64.5 us  [step(): lax.ppermute(self.total[i - 1], self.axis, [(1, 0), (2, 3)])]
    ppermute x21, starting transfers between devices: 73.8 us -> 81.7 us  [start(): self.inward[i] = lax.ppermute(self.parts[i], self.axis, [(0, 1), (3, 2)])]
    pallas_call x29 -> x31, Pallas kernels: 126 us -> 125 us  [call(): pl.pallas_call(body, grid=grid, name=name or kernel.__name__.removesuffix...]
  transfers between devices with their start and end apart: 73 -> 73, of which waited for: 17 -> 22; matrix products, arithmetic and copies ran while one was open for 1% -> 1% of each run, Pallas kernels for 38% -> 39%
where the time goes in v4:
time: 432 us; the launch traced here: 426 us
  Pallas kernels  191 us (44%)
  starting transfers between devices  141 us (33%)
  waiting for transfers between devices  77.9 us (18%)
  local copies, waits for them, and re-layouts  8.5 us (2%)
  other arithmetic  5.31 us (1%)
    pallas_call x31, Pallas kernels, call(): pl.pallas_call(body, grid=grid, name=name or kernel.__name__.removesuffix...  125 us
    ppermute x21, starting transfers between devices, start(): self.inward[i] = lax.ppermute(self.parts[i], self.axis, [(0, 1), (3, 2)])  81.7 us
    pallas_call x63, Pallas kernels, chosen_call(): pl.pallas_call(body, name=kernel.__name__.removesuffix('_kernel'), grid_s...  65.6 us
    ppermute x21, waiting for transfers between devices, step(): lax.ppermute(self.total[i - 1], self.axis, [(1, 0), (2, 3)])  64.5 us
    ppermute x21, starting transfers between devices, step(): lax.ppermute(self.total[i - 1], self.axis, [(1, 0), (2, 3)])  28.2 us
    ppermute x6, starting transfers between devices, send(): return lax.ppermute(block, 'section', list(pairs))  16 us
    ppermute x21, starting transfers between devices, step(): self.across[i] = lax.ppermute(self.half[i], self.axis, [(1, 2), (2, 1)])  15.1 us
  transfers between devices with their start and end apart: 73, of which 22 were waited for; matrix products, arithmetic and copies ran while one was open for 1% of the time, Pallas kernels for 39%

profile of v4, /device:TPU:0, one launch (start us, length us, event | category | flops | bytes accessed | tf_op | source)
XLA Modules:
  0.0 426.5 jit_solution(8338158057332492730)
XLA Ops:
  0.7 5.0 %value.1 = (bf16[1024,1024]{1,0:T(8,128)(2,1)}, bf16[1024,256]{1,0:T(8,128)(2,1)}, bf16[1024,256]{1,0:T(8,128)(2,1)}) custom-call(bf16[1024,1024]{1,0:T(8,128)(2,1)} %bitcast.47, f32[1,1024]{1,0:T(1,128)} %refs_2_.3, bf16[1024,512]{1,0:T(8,128)(2,1)} %bitcast.56), custom_call_target="tpu_custom_call" | custom-call | flops 1 | bytes 1 | tf_op jit(solution)/shard_map/value/pallas_call | solution.py:44
  5.7 5.9 %collective-permute-start = (bf16[1024,256]{1,0:T(8,128)(2,1)}, bf16[1024,256]{1,0:T(8,128)(2,1)}, u32[]{:S(2)}, u32[]{:S(2)}) collective-permute-start(bf16[1024,256]{1,0:T(8,128)(2,1)} %get-tuple-element.246.refs_2_), channel_id=1, source_target_pairs={{0,8},{1,9},{2,10},{3,11},{4,12},{5,13},{6,14},{7,15}} | collective-permute-start | bytes 1572872 | tf_op jit(solution)/shard_map/ppermute | solution.py:807
  32.0 10.5 %probs.1.refs_1_.probs_ref.refs_3_ = bf16[8,1024,768]{2,1,0:T(8,128)(2,1)} custom-call(s32[1,4]{1,0:T(1,128)S(1)} %copy-done.41, bf16[1024,512]{1,0:T(8,128)(2,1)S(1)} %get-tuple-element.250.q_ref.refs_0_, bf16[1024,512]{1,0:T(8,128)(2,1)S(1)} %get-tuple-element.251.k_ref.refs_1_), custom_call_target="tpu_custom_call" | custom-call | flops 1 | bytes 1 | tf_op jit(solution)/shard_map/probs/pallas_call | solution.py:44
  42.6 8.1 %heads.1 = (bf16[1024,512]{1,0:T(8,128)(2,1)S(1)}, bf16[1024,512]{1,0:T(8,128)(2,1)S(1)}, bf16[1024,1024]{1,0:T(8,128)(2,1)S(1)}) custom-call(s32[1]{0:T(128)} %bitcast.1.refs_0_.section_ref, bf16[8,1024,768]{2,1,0:T(8,128)(2,1)} %probs.1.refs_1_.probs_ref.refs_3_, bf16[1024,256]{1,0:T(8,128)(2,1)S(1)} %copy-done.32, bf16[1024,256]{1,0:T(8,128)(2,1)S(1)} %copy-done.33, ...), custom_call_target="tpu_custom_call" | custom-call | flops 1 | bytes 1 | tf_op jit(solution)/shard_map/heads/pallas_call | solution.py:44
  59.4 8.3 %entry.1 = (bf16[1024,1024]{1,0:T(8,128)(2,1)}, bf16[1024,256]{1,0:T(8,128)(2,1)}, bf16[1024,256]{1,0:T(8,128)(2,1)}, bf16[1024,256]{1,0:T(8,128)(2,1)}, bf16[256,1024]{1,0:T(8,128)(2,1)}) custom-call(bf16[1024,1024]{1,0:T(8,128)(2,1)} %bitcast.48, bf16[1024,1024]{1,0:T(8,128)(2,1)} %copy-done.13, bf16[1024,1024]{1,0:T(8,128)(2,1)} %copy-done.16, ...), custom_call_target="tpu_custom_call" | custom-call | flops 1 | bytes 1 | tf_op jit(solution)/shard_map/entry/pallas_call | solution.py:44
  78.3 6.3 %ffn.3 = (bf16[1024,1152]{1,0:T(8,128)(2,1)S(1)}, bf16[1024,1152]{1,0:T(8,128)(2,1)S(1)}, bf16[1024,1152]{1,0:T(8,128)(2,1)S(1)}, bf16[384,1024]{1,0:T(8,128)(2,1)S(1)}) custom-call(bf16[1024,1024]{1,0:T(8,128)(2,1)S(1)} %copy-done.6, bf16[1024,1024]{1,0:T(8,128)(2,1)S(1)} %bitcast.43, bf16[1024,1408]{1,0:T(8,128)(2,1)} %bitcast.26, ...), custom_call_target="tpu_custom_call" | custom-call | flops 1 | bytes 1 | tf_op jit(solution)/shard_map/ffn/pallas_call | solution.py:44
  86.9 6.3 %ffn.4 = (bf16[1024,1152]{1,0:T(8,128)(2,1)S(1)}, bf16[1024,1152]{1,0:T(8,128)(2,1)S(1)}, bf16[1024,1152]{1,0:T(8,128)(2,1)S(1)}, bf16[384,1024]{1,0:T(8,128)(2,1)S(1)}) custom-call(bf16[1024,1024]{1,0:T(8,128)(2,1)S(1)} %copy-done.6, bf16[1024,1024]{1,0:T(8,128)(2,1)S(1)} %bitcast.44, ...), custom_call_target="tpu_custom_call", output_to_operand_aliasing={{0}: (5, {}), {1}: (6, {}), {2}: (7, {})} | custom-call | flops 1 | bytes 1 | tf_op jit(solution)/shard_map/ffn/pallas_call | solution.py:44
  94.1 5.6 %collective-permute-start.9 = (bf16[1024,256]{1,0:T(8,128)(2,1)S(1)}, bf16[1024,256]{1,0:T(8,128)(2,1)S(1)}, u32[]{:S(2)}, u32[]{:S(2)}) collective-permute-start(bf16[1024,256]{1,0:T(8,128)(2,1)S(1)} %get-tuple-element.292.refs_0_), channel_id=1, source_target_pairs={{0,2},{6,4},{1,3},{7,5},{8,10},{14,12},{9,11},{15,13},{16,18},{22,... | collective-permute-start | bytes 1572872 | tf_op jit(solution)/shard_map/ppermute | solution.py:706
  106.9 6.3 %ffn.5 = (bf16[1024,1152]{1,0:T(8,128)(2,1)S(1)}, bf16[1024,1152]{1,0:T(8,128)(2,1)S(1)}, bf16[1024,1152]{1,0:T(8,128)(2,1)S(1)}, bf16[384,1024]{1,0:T(8,128)(2,1)S(1)}) custom-call(bf16[1024,1024]{1,0:T(8,128)(2,1)S(1)} %copy-done.6, bf16[1024,1024]{1,0:T(8,128)(2,1)S(1)} %bitcast.45, ...), custom_call_target="tpu_custom_call", output_to_operand_aliasing={{0}: (5, {}), {1}: (6, {}), {2}: (7, {})} | custom-call | flops 1 | bytes 1 | tf_op jit(solution)/shard_map/ffn/pallas_call | solution.py:44
  141.2 7.5 %products.3.refs_0_ = bf16[1024,1024]{1,0:T(8,128)(2,1)S(1)} custom-call(bf16[1024,1152]{1,0:T(8,128)(2,1)S(1)} %get-tuple-element.289.refs_0_, bf16[1024,256]{1,0:T(8,128)(2,1)S(1)} %copy-done.35, bf16[1024,1152]{1,0:T(8,128)(2,1)S(1)} %get-tuple-element.300.refs_1_.refs_2_, bf16[1024,256]{1,0:T(8,128)(2,1)S(1)} %copy-done.36, ...), custom_call_target="tpu_custom_call" | custom-call | flops 1 | bytes 1 | tf_op jit(solution)/shard_map/products/pallas_call | solution.py:44
  154.3 7.7 %collective-permute-start.19 = (bf16[1024,384]{1,0:T(8,128)(2,1)S(1)}, bf16[1024,384]{1,0:T(8,128)(2,1)S(1)}, u32[]{:S(2)}, u32[]{:S(2)}) collective-permute-start(bf16[1024,384]{1,0:T(8,128)(2,1)S(1)} %get-tuple-element.331.refs_0_), channel_id=1, source_target_pairs={{0,2},{6,4},{1,3},{7,5},{8,10},{14,12},{9,11},{15,13},{16,18},{22,... | collective-permute-start | bytes 2359304 | tf_op jit(solution)/shard_map/ppermute | solution.py:706
  183.1 5.9 %collective-permute-done.25.refs_1_ = bf16[384,1024]{1,0:T(8,128)(2,1)S(1)} collective-permute-done((bf16[384,1024]{1,0:T(8,128)(2,1)S(1)}, bf16[384,1024]{1,0:T(8,128)(2,1)S(1)}, u32[]{:S(2)}, u32[]{:S(2)}) %collective-permute-start.25) | collective-permute-done | bytes 786464 | tf_op jit(solution)/shard_map/ppermute | solution.py:731
  200.2 7.1 %collective-permute-done.22.refs_1_ = bf16[384,1024]{1,0:T(8,128)(2,1)S(1)} collective-permute-done((bf16[384,1024]{1,0:T(8,128)(2,1)S(1)}, bf16[384,1024]{1,0:T(8,128)(2,1)S(1)}, u32[]{:S(2)}, u32[]{:S(2)}) %collective-permute-start.22) | collective-permute-done | bytes 786464 | tf_op jit(solution)/shard_map/ppermute | solution.py:731
  220.6 5.5 %collective-permute-start.30 = (bf16[1024,384]{1,0:T(8,128)(2,1)}, bf16[1024,384]{1,0:T(8,128)(2,1)S(1)}, u32[]{:S(2)}, u32[]{:S(2)}) collective-permute-start(bf16[1024,384]{1,0:T(8,128)(2,1)} %get-tuple-element.369.refs_0_), channel_id=1, source_target_pairs={{0,2},{6,4},{1,3},{7,5},{8,10},{14,12},{9,11},{15,13},{16,18},{22,... | collective-permute-start | bytes 2359304 | tf_op jit(solution)/shard_map/ppermute | solution.py:706
  228.9 8.0 %value_back.1 = (bf16[1024,512]{1,0:T(8,128)(2,1)S(1)}, bf16[1024,512]{1,0:T(8,128)(2,1)S(1)}) custom-call(bf16[8,1024,768]{2,1,0:T(8,128)(2,1)S(1)} %bitcast.23, bf16[1024,1024]{1,0:T(8,128)(2,1)S(1)} %get-tuple-element.353.attn_ref.right_ref, bf16[512,1024]{1,0:T(8,128)(2,1)S(1)} %bitcast.59), custom_call_target="tpu_custom_call" | custom-call | flops 1 | bytes 1 | tf_op jit(solution)/shard_map/value_back/pallas_call | solution.py:44
  241.4 4.9 %collective-permute-start.35 = (bf16[1024,384]{1,0:T(8,128)(2,1)S(1)}, bf16[1024,384]{1,0:T(8,128)(2,1)S(1)}, u32[]{:S(2)}, u32[]{:S(2)}) collective-permute-start(bf16[1024,384]{1,0:T(8,128)(2,1)S(1)} %get-tuple-element.379.refs_0_), channel_id=1, source_target_pairs={{0,2},{6,4},{1,3},{7,5},{8,10},{14,12},{9,11},{15,13},{16,18},{22,... | collective-permute-start | bytes 2359304 | tf_op jit(solution)/shard_map/ppermute | solution.py:706
  267.4 6.6 %collective-permute-start.40 = (bf16[256,1024]{1,0:T(8,128)(2,1)S(1)}, bf16[256,1024]{1,0:T(8,128)(2,1)S(1)}, u32[]{:S(2)}, u32[]{:S(2)}) collective-permute-start(bf16[256,1024]{1,0:T(8,128)(2,1)S(1)} %row_grads.2.refs_0_), channel_id=1, source_target_pairs={{0,2},{6,4},{1,3},{7,5},{8,10},{14,12},{9,11},{15,13},{16,18},{22,... | collective-permute-start | bytes 1572872 | tf_op jit(solution)/shard_map/ppermute | solution.py:706
  330.2 5.8 %collective-permute-start.55 = (bf16[1024,256]{1,0:T(8,128)(2,1)S(1)}, bf16[1024,256]{1,0:T(8,128)(2,1)S(1)}, u32[]{:S(2)}, u32[]{:S(2)}) collective-permute-start(bf16[1024,256]{1,0:T(8,128)(2,1)S(1)} %get-tuple-element.433.refs_0_), channel_id=1, source_target_pairs={{0,2},{6,4},{1,3},{7,5},{8,10},{14,12},{9,11},{15,13},{16,18},{22,... | collective-permute-start | bytes 1572872 | tf_op jit(solution)/shard_map/ppermute | solution.py:706
  339.3 7.5 %collective-permute-done.56.refs_1_ = bf16[256,1024]{1,0:T(8,128)(2,1)S(1)} collective-permute-done((bf16[256,1024]{1,0:T(8,128)(2,1)S(1)}, bf16[256,1024]{1,0:T(8,128)(2,1)S(1)}, u32[]{:S(2)}, u32[]{:S(2)}) %collective-permute-start.56) | collective-permute-done | bytes 524320 | tf_op jit(solution)/shard_map/ppermute | solution.py:731
  353.3 4.8 %collective-permute-done.53.refs_1_ = bf16[1024,256]{1,0:T(8,128)(2,1)S(1)} collective-permute-done((bf16[1024,256]{1,0:T(8,128)(2,1)S(1)}, bf16[1024,256]{1,0:T(8,128)(2,1)S(1)}, u32[]{:S(2)}, u32[]{:S(2)}) %collective-permute-start.53) | collective-permute-done | bytes 524320 | tf_op jit(solution)/shard_map/ppermute | solution.py:731
  364.3 4.9 %collective-permute-done.59.refs_1_ = bf16[1024,256]{1,0:T(8,128)(2,1)S(1)} collective-permute-done((bf16[1024,256]{1,0:T(8,128)(2,1)S(1)}, bf16[1024,256]{1,0:T(8,128)(2,1)S(1)}, u32[]{:S(2)}, u32[]{:S(2)}) %collective-permute-start.59) | collective-permute-done | bytes 524320 | tf_op jit(solution)/shard_map/ppermute | solution.py:731
  375.8 5.9 %collective-permute-done.64.refs_1_ = bf16[1024,256]{1,0:T(8,128)(2,1)S(1)} collective-permute-done((bf16[1024,256]{1,0:T(8,128)(2,1)S(1)}, bf16[1024,256]{1,0:T(8,128)(2,1)S(1)}, u32[]{:S(2)}, u32[]{:S(2)}) %collective-permute-start.64) | collective-permute-done | bytes 524320 | tf_op jit(solution)/shard_map/ppermute | solution.py:731
  390.4 4.8 %collective-permute-start.68 = (bf16[16,1024]{1,0:T(8,128)(2,1)S(1)}, bf16[16,1024]{1,0:T(8,128)(2,1)S(1)}, u32[]{:S(2)}, u32[]{:S(2)}) collective-permute-start(bf16[16,1024]{1,0:T(8,128)(2,1)S(1)} %fusion.3.refs_0_), channel_id=1, source_target_pairs={{0,2},{6,4},{1,3},{7,5},{8,10},{14,12},{9,11},{15,13},{16,18},{22,... | collective-permute-start | bytes 98312 | tf_op jit(solution)/shard_map/ppermute | solution.py:706
  408.5 12.5 %collective-permute-done.72.refs_1_ = bf16[1024,256]{1,0:T(8,128)(2,1)S(1)} collective-permute-done((bf16[1024,256]{1,0:T(8,128)(2,1)S(1)}, bf16[1024,256]{1,0:T(8,128)(2,1)S(1)}, u32[]{:S(2)}, u32[]{:S(2)}) %collective-permute-start.72) | collective-permute-done | bytes 524320 | tf_op jit(solution)/shard_map/ppermute | solution.py:731
  (320 shorter events, 262.1 us)
Async XLA Ops:
  101.0 28.0 %collective-permute-start.12 = (bf16[384,1024]{1,0:T(8,128)(2,1)S(1)}, bf16[384,1024]{1,0:T(8,128)(2,1)S(1)}, u32[]{:S(2)}, u32[]{:S(2)}) collective-permute-start(bf16[384,1024]{1,0:T(8,128)(2,1)S(1)} %get-tuple-element.303.refs_0_), channel_id=1, source_target_pairs={{0,2},{6,4},{1,3},{7,5},{8,10},{14,12},{9,11},{15,13},{16,18},{22,... | collective-permute-start | bytes 2359304 | tf_op jit(solution)/shard_map/ppermute | solution.py:706
  120.2 28.6 %collective-permute-start.17 = (bf16[384,1024]{1,0:T(8,128)(2,1)S(1)}, bf16[384,1024]{1,0:T(8,128)(2,1)S(1)}, u32[]{:S(2)}, u32[]{:S(2)}) collective-permute-start(bf16[384,1024]{1,0:T(8,128)(2,1)S(1)} %get-tuple-element.312.refs_0_), channel_id=1, source_target_pairs={{0,2},{6,4},{1,3},{7,5},{8,10},{14,12},{9,11},{15,13},{16,18},{22,... | collective-permute-start | bytes 2359304 | tf_op jit(solution)/shard_map/ppermute | solution.py:706
  136.8 28.7 %collective-permute-start.14 = (bf16[384,1024]{1,0:T(8,128)(2,1)S(1)}, bf16[384,1024]{1,0:T(8,128)(2,1)S(1)}, u32[]{:S(2)}, u32[]{:S(2)}) collective-permute-start(bf16[384,1024]{1,0:T(8,128)(2,1)S(1)} %get-tuple-element.321.refs_0_), channel_id=1, source_target_pairs={{0,2},{6,4},{1,3},{7,5},{8,10},{14,12},{9,11},{15,13},{16,18},{22,... | collective-permute-start | bytes 2359304 | tf_op jit(solution)/shard_map/ppermute | solution.py:706
  152.0 61.2 %collective-permute-start.26 = (bf16[1024,1024]{1,0:T(8,128)(2,1)S(1)}, bf16[1024,1024]{1,0:T(8,128)(2,1)S(1)}, u32[]{:S(2)}, u32[]{:S(2)}) collective-permute-start(bf16[1024,1024]{1,0:T(8,128)(2,1)S(1)} %products.3.refs_0_), channel_id=1, source_target_pairs={{0,1},{1,0},{2,3},{3,2},{4,5},{5,4},{6,7},{7,6},{8,9},{9,8},{10,11... | collective-permute-start | bytes 6291464 | tf_op jit(solution)/shard_map/ppermute | solution.py:779
  154.3 25.5 %collective-permute-start.19 = (bf16[1024,384]{1,0:T(8,128)(2,1)S(1)}, bf16[1024,384]{1,0:T(8,128)(2,1)S(1)}, u32[]{:S(2)}, u32[]{:S(2)}) collective-permute-start(bf16[1024,384]{1,0:T(8,128)(2,1)S(1)} %get-tuple-element.331.refs_0_), channel_id=1, source_target_pairs={{0,2},{6,4},{1,3},{7,5},{8,10},{14,12},{9,11},{15,13},{16,18},{22,... | collective-permute-start | bytes 2359304 | tf_op jit(solution)/shard_map/ppermute | solution.py:706
  167.4 21.5 %collective-permute-start.25 = (bf16[384,1024]{1,0:T(8,128)(2,1)S(1)}, bf16[384,1024]{1,0:T(8,128)(2,1)S(1)}, u32[]{:S(2)}, u32[]{:S(2)}) collective-permute-start(bf16[384,1024]{1,0:T(8,128)(2,1)S(1)} %add.56.refs_0_), channel_id=1, source_target_pairs={{2,0},{4,6},{3,1},{5,7},{10,8},{12,14},{11,9},{13,15},{18,16},{20,... | collective-permute-start | bytes 2359304 | tf_op jit(solution)/shard_map/ppermute | solution.py:731
  169.3 27.4 %collective-permute-start.24 = (bf16[1024,384]{1,0:T(8,128)(2,1)S(1)}, bf16[1024,384]{1,0:T(8,128)(2,1)S(1)}, u32[]{:S(2)}, u32[]{:S(2)}) collective-permute-start(bf16[1024,384]{1,0:T(8,128)(2,1)S(1)} %get-tuple-element.338.refs_0_), channel_id=1, source_target_pairs={{0,2},{6,4},{1,3},{7,5},{8,10},{14,12},{9,11},{15,13},{16,18},{22,... | collective-permute-start | bytes 2359304 | tf_op jit(solution)/shard_map/ppermute | solution.py:706
  181.8 25.6 %collective-permute-start.22 = (bf16[384,1024]{1,0:T(8,128)(2,1)S(1)}, bf16[384,1024]{1,0:T(8,128)(2,1)S(1)}, u32[]{:S(2)}, u32[]{:S(2)}) collective-permute-start(bf16[384,1024]{1,0:T(8,128)(2,1)S(1)} %add.58.refs_0_), channel_id=1, source_target_pairs={{2,0},{4,6},{3,1},{5,7},{10,8},{12,14},{11,9},{13,15},{18,16},{20,... | collective-permute-start | bytes 2359304 | tf_op jit(solution)/shard_map/ppermute | solution.py:731
  189.0 28.1 %collective-permute-start.29 = (bf16[1024,384]{1,0:T(8,128)(2,1)S(1)}, bf16[1024,384]{1,0:T(8,128)(2,1)S(1)}, u32[]{:S(2)}, u32[]{:S(2)}) collective-permute-start(bf16[1024,384]{1,0:T(8,128)(2,1)S(1)} %get-tuple-element.347.refs_0_), channel_id=1, source_target_pairs={{0,2},{6,4},{1,3},{7,5},{8,10},{14,12},{9,11},{15,13},{16,18},{22,... | collective-permute-start | bytes 2359304 | tf_op jit(solution)/shard_map/ppermute | solution.py:706
  197.3 21.1 %collective-permute-start.28 = (bf16[1024,384]{1,0:T(8,128)(2,1)S(1)}, bf16[1024,384]{1,0:T(8,128)(2,1)S(1)}, u32[]{:S(2)}, u32[]{:S(2)}) collective-permute-start(bf16[1024,384]{1,0:T(8,128)(2,1)S(1)} %add.59.refs_0_), channel_id=1, source_target_pairs={{2,4},{4,2},{3,5},{5,3},{10,12},{12,10},{11,13},{13,11},{18,20},{2... | collective-permute-start | bytes 2359304 | tf_op jit(solution)/shard_map/ppermute | solution.py:726
  198.7 27.4 %collective-permute-start.27 = (bf16[1024,384]{1,0:T(8,128)(2,1)S(1)}, bf16[1024,384]{1,0:T(8,128)(2,1)}, u32[]{:S(2)}, u32[]{:S(2)}) collective-permute-start(bf16[1024,384]{1,0:T(8,128)(2,1)S(1)} %add.60.refs_0_), channel_id=1, source_target_pairs={{2,0},{4,6},{3,1},{5,7},{10,8},{12,14},{11,9},{13,15},{18,16},{20,... | collective-permute-start | bytes 2359304 | tf_op jit(solution)/shard_map/ppermute | solution.py:731
  207.3 29.6 %collective-permute-start.33 = (bf16[1024,384]{1,0:T(8,128)(2,1)}, bf16[1024,384]{1,0:T(8,128)(2,1)}, u32[]{:S(2)}, u32[]{:S(2)}) collective-permute-start(bf16[1024,384]{1,0:T(8,128)(2,1)} %get-tuple-element.358.refs_0_), channel_id=1, source_target_pairs={{0,2},{6,4},{1,3},{7,5},{8,10},{14,12},{9,11},{15,13},{16,18},{22,... | collective-permute-start | bytes 2359304 | tf_op jit(solution)/shard_map/ppermute | solution.py:706
  217.7 21.6 %collective-permute-start.32 = (bf16[1024,384]{1,0:T(8,128)(2,1)S(1)}, bf16[1024,384]{1,0:T(8,128)(2,1)S(1)}, u32[]{:S(2)}, u32[]{:S(2)}) collective-permute-start(bf16[1024,384]{1,0:T(8,128)(2,1)S(1)} %add.61.refs_0_), channel_id=1, source_target_pairs={{2,4},{4,2},{3,5},{5,3},{10,12},{12,10},{11,13},{13,11},{18,20},{2... | collective-permute-start | bytes 2359304 | tf_op jit(solution)/shard_map/ppermute | solution.py:726
  219.1 27.2 %collective-permute-start.31 = (bf16[1024,384]{1,0:T(8,128)(2,1)S(1)}, bf16[1024,384]{1,0:T(8,128)(2,1)S(1)}, u32[]{:S(2)}, u32[]{:S(2)}) collective-permute-start(bf16[1024,384]{1,0:T(8,128)(2,1)S(1)} %add.62.refs_0_), channel_id=1, source_target_pairs={{2,0},{4,6},{3,1},{5,7},{10,8},{12,14},{11,9},{13,15},{18,16},{20,... | collective-permute-start | bytes 2359304 | tf_op jit(solution)/shard_map/ppermute | solution.py:731
  220.6 34.1 %collective-permute-start.30 = (bf16[1024,384]{1,0:T(8,128)(2,1)}, bf16[1024,384]{1,0:T(8,128)(2,1)S(1)}, u32[]{:S(2)}, u32[]{:S(2)}) collective-permute-start(bf16[1024,384]{1,0:T(8,128)(2,1)} %get-tuple-element.369.refs_0_), channel_id=1, source_target_pairs={{0,2},{6,4},{1,3},{7,5},{8,10},{14,12},{9,11},{15,13},{16,18},{22,... | collective-permute-start | bytes 2359304 | tf_op jit(solution)/shard_map/ppermute | solution.py:706
  241.4 24.7 %collective-permute-start.35 = (bf16[1024,384]{1,0:T(8,128)(2,1)S(1)}, bf16[1024,384]{1,0:T(8,128)(2,1)S(1)}, u32[]{:S(2)}, u32[]{:S(2)}) collective-permute-start(bf16[1024,384]{1,0:T(8,128)(2,1)S(1)} %get-tuple-element.379.refs_0_), channel_id=1, source_target_pairs={{0,2},{6,4},{1,3},{7,5},{8,10},{14,12},{9,11},{15,13},{16,18},{22,... | collective-permute-start | bytes 2359304 | tf_op jit(solution)/shard_map/ppermute | solution.py:706
  257.0 24.7 %collective-permute-start.41 = (bf16[1024,512]{1,0:T(8,128)(2,1)S(1)}, bf16[1024,512]{1,0:T(8,128)(2,1)S(1)}, u32[]{:S(2)}, u32[]{:S(2)}) collective-permute-start(bf16[1024,512]{1,0:T(8,128)(2,1)S(1)} %get-tuple-element.384.refs_0_.half_ref), channel_id=1, source_target_pairs={{8,0},{24,16},{9,1},{25,17},{10,2},{26,18},{11,3},{27,19},{12,4},{... | collective-permute-start | bytes 3145736 | tf_op jit(solution)/shard_map/ppermute | solution.py:807
  258.9 20.8 %collective-permute-start.42 = (bf16[1024,384]{1,0:T(8,128)(2,1)S(1)}, bf16[1024,384]{1,0:T(8,128)(2,1)S(1)}, u32[]{:S(2)}, u32[]{:S(2)}) collective-permute-start(bf16[1024,384]{1,0:T(8,128)(2,1)S(1)} %add.66.refs_0_), channel_id=1, source_target_pairs={{2,0},{4,6},{3,1},{5,7},{10,8},{12,14},{11,9},{13,15},{18,16},{20,... | collective-permute-start | bytes 2359304 | tf_op jit(solution)/shard_map/ppermute | solution.py:731
  266.7 25.9 %collective-permute-start.39 = (bf16[1024,384]{1,0:T(8,128)(2,1)S(1)}, bf16[1024,384]{1,0:T(8,128)(2,1)S(1)}, u32[]{:S(2)}, u32[]{:S(2)}) collective-permute-start(bf16[1024,384]{1,0:T(8,128)(2,1)S(1)} %add.67.refs_0_), channel_id=1, source_target_pairs={{2,4},{4,2},{3,5},{5,3},{10,12},{12,10},{11,13},{13,11},{18,20},{2... | collective-permute-start | bytes 2359304 | tf_op jit(solution)/shard_map/ppermute | solution.py:726
  267.4 23.8 %collective-permute-start.40 = (bf16[256,1024]{1,0:T(8,128)(2,1)S(1)}, bf16[256,1024]{1,0:T(8,128)(2,1)S(1)}, u32[]{:S(2)}, u32[]{:S(2)}) collective-permute-start(bf16[256,1024]{1,0:T(8,128)(2,1)S(1)} %row_grads.2.refs_0_), channel_id=1, source_target_pairs={{0,2},{6,4},{1,3},{7,5},{8,10},{14,12},{9,11},{15,13},{16,18},{22,... | collective-permute-start | bytes 1572872 | tf_op jit(solution)/shard_map/ppermute | solution.py:706
  281.9 35.7 %collective-permute-start.49 = (bf16[1024,512]{1,0:T(8,128)(2,1)S(1)}, bf16[1024,512]{1,0:T(8,128)(2,1)S(1)}, u32[]{:S(2)}, u32[]{:S(2)}) collective-permute-start(bf16[1024,512]{1,0:T(8,128)(2,1)S(1)} %sum.1.refs_0_), channel_id=1, source_target_pairs={{16,0},{17,1},{18,2},{19,3},{20,4},{21,5},{22,6},{23,7}} | collective-permute-start | bytes 3145736 | tf_op jit(solution)/shard_map/ppermute | solution.py:807
  283.2 24.7 %collective-permute-start.44 = (bf16[256,1024]{1,0:T(8,128)(2,1)S(1)}, bf16[256,1024]{1,0:T(8,128)(2,1)S(1)}, u32[]{:S(2)}, u32[]{:S(2)}) collective-permute-start(bf16[256,1024]{1,0:T(8,128)(2,1)S(1)} %row_grads.3.refs_0_), channel_id=1, source_target_pairs={{0,2},{6,4},{1,3},{7,5},{8,10},{14,12},{9,11},{15,13},{16,18},{22,... | collective-permute-start | bytes 1572872 | tf_op jit(solution)/shard_map/ppermute | solution.py:706
  312.7 23.3 %collective-permute-start.52 = (bf16[1024,256]{1,0:T(8,128)(2,1)S(1)}, bf16[1024,256]{1,0:T(8,128)(2,1)S(1)}, u32[]{:S(2)}, u32[]{:S(2)}) collective-permute-start(bf16[1024,256]{1,0:T(8,128)(2,1)S(1)} %get-tuple-element.425.refs_0_), channel_id=1, source_target_pairs={{0,2},{6,4},{1,3},{7,5},{8,10},{14,12},{9,11},{15,13},{16,18},{22,... | collective-permute-start | bytes 1572872 | tf_op jit(solution)/shard_map/ppermute | solution.py:706
  328.8 54.4 %collective-permute-start.65 = (bf16[1024,1024]{1,0:T(8,128)(2,1)S(1)}, bf16[1024,1024]{1,0:T(8,128)(2,1)S(1)}, u32[]{:S(2)}, u32[]{:S(2)}) collective-permute-start(bf16[1024,1024]{1,0:T(8,128)(2,1)S(1)} %products.4.refs_0_), channel_id=1, source_target_pairs={{0,1},{1,0},{2,3},{3,2},{4,5},{5,4},{6,7},{7,6},{8,9},{9,8},{10,11... | collective-permute-start | bytes 6291464 | tf_op jit(solution)/shard_map/ppermute | solution.py:779
  (94 other events, 1111.3 us)
